TPU v7x, 32 devices: a whole 2x2x4 slice. The times are simulated.
32 devices in a mesh: ctx: 8 (over z, y), grp: 4 (over x, core).
Axes of the slice: x: 2, y: 2, z: 4, core: 2. Of those that a mesh axis runs over, the one named last changes fastest.
Arguments:
- q_nope: bfloat16 [64, 128, 128], P(None, 'ctx'), may hold values from -6 to 6
- q_rope: bfloat16 [64, 128, 64], P(None, 'ctx'), may hold values from -720 to 720
- w_uk: bfloat16 [128, 128, 512], P('ctx'), may hold values from -0.5 to 0.5
- w_uv: bfloat16 [128, 512, 128], P('ctx'), may hold values from -0.375 to 0.375
- prompt: bfloat16 [1536, 576], P('grp'), may hold values from -12 to 12
- w_out: bfloat16 [16384, 7168], P('ctx', 'grp'), may hold values from -0.0625 to 0.0625
- residual: bfloat16 [64, 7168], P('ctx', 'grp'), may hold values from -3 to 3
- routes: int32 [64, 8], P('ctx'), may hold values from 0 to 31, all different within a row; in each aligned block of 8 rows (0 to 7, 8 to 15, ...) at most 4 rows name the same one
- route_scores: float32 [64, 8], P('ctx'), may hold values from 0.05 to 1
- expert_gate: bfloat16 [32, 7168, 1024], P('ctx', 'grp'), may hold values from -0.0625 to 0.0625
- expert_up: bfloat16 [32, 7168, 1024], P('ctx', 'grp'), may hold values from -0.0625 to 0.0625
- expert_down: bfloat16 [32, 1024, 7168], P('ctx', None, 'grp'), may hold values from -0.1875 to 0.1875
Outputs:
- layer_out: bfloat16 [64, 7168], P('ctx', 'grp')
Inputs may be any that keep to these rules, and one draw needn't show every extreme that they name: `routes`: in each aligned block of 8 rows no expert is named by more than 4 rows, a bound that some block reaches; the 8 experts of a row differ.
All inputs are finite; a program needn't handle non-finite values.
Results may differ from a plain program's by a relative error of at most 0.0163.
Values may be sent and summed in bfloat16 or wider, within the bound.
No kernel may reach another device: no remote copies, remote signals or barrier semaphores. Data moves between devices by JAX's collectives and lax.ppermute only.
A program may use at most 128 MiB of HBM per device.

v0:
```python
import jax
import jax.numpy as jnp
from jax import lax
from jax.sharding import PartitionSpec as P

NOPE = 128
ROPE = 64
LAT = 512
VDIM = 128
CAP = 4


route_factor = 2.5


def per_device(
    q_nope,
    q_rope,
    w_uk,
    w_uv,
    prompt,
    w_out,
    residual,
    routes,
    route_scores,
    expert_gate,
    expert_up,
    expert_down,
):
    score_scale = (NOPE + ROPE) ** (-0.5)
    q_latent = jnp.einsum("rhn,hnl->rhl", q_nope, w_uk, preferred_element_type=jnp.float32).astype(
        jnp.bfloat16
    )
    queries = jnp.concatenate([q_latent, q_rope], axis=-1)
    head_uv = w_uv.astype(jnp.float32)
    head_cols = queries.shape[1] * VDIM
    all_keys = lax.all_gather(prompt, "grp", axis=0, tiled=True)
    row_share = queries.shape[0] // lax.axis_size("grp")
    own_queries = lax.dynamic_slice_in_dim(queries, lax.axis_index("grp") * row_share, row_share, 0)
    scores = (
        jnp.einsum("rhc,jc->rhj", own_queries, all_keys, preferred_element_type=jnp.float32)
        * score_scale
    )
    top_score = jnp.max(scores, axis=-1)
    raised = jnp.exp(scores - top_score[..., None])
    denominator = jnp.sum(raised, axis=-1)
    weighted = jnp.einsum(
        "rhj,jl->rhl",
        raised.astype(jnp.bfloat16),
        all_keys[:, :LAT],
        preferred_element_type=jnp.float32,
    )
    values = jnp.einsum("rhl,hlv->rhv", weighted, head_uv, precision=lax.Precision.HIGHEST)
    top_score, denominator, values = (top_score, denominator, values)
    own_rows = (values / denominator[..., None]).astype(jnp.bfloat16).reshape(row_share, head_cols)
    attended = lax.all_gather(own_rows, "grp", axis=0, tiled=True)
    local_rows = residual.shape[0]
    projected = lax.psum_scatter(
        jnp.dot(attended, w_out, preferred_element_type=jnp.float32),
        "ctx",
        scatter_dimension=0,
        tiled=True,
    )
    hidden = residual.astype(jnp.float32) + projected
    moe_input = hidden.astype(jnp.bfloat16)
    gate_weights = route_factor * route_scores / jnp.sum(route_scores, axis=-1, keepdims=True)
    top_count = routes.shape[1]
    experts = expert_gate.shape[0] * lax.axis_size("ctx")
    flat_routes = routes.reshape(-1)
    onehot = (flat_routes[:, None] == jnp.arange(experts, dtype=jnp.int32)[None, :]).astype(
        jnp.int32
    )
    before = jnp.cumsum(onehot, axis=0) - onehot
    slot_index = jnp.sum(before * onehot, axis=1)
    target = flat_routes * CAP + slot_index
    select = (target[:, None] == jnp.arange(experts * CAP, dtype=jnp.int32)[None, :]).astype(
        jnp.float32
    )
    row_of = jnp.arange(local_rows * top_count, dtype=jnp.int32) // top_count
    row_pick = (row_of[:, None] == jnp.arange(local_rows, dtype=jnp.int32)[None, :]).astype(
        jnp.float32
    )
    slot_rows = jnp.dot(select.T, row_pick, precision=lax.Precision.HIGHEST)
    outgoing = jnp.dot(
        slot_rows.astype(jnp.bfloat16), moe_input, preferred_element_type=jnp.float32
    ).astype(jnp.bfloat16)
    outgoing = outgoing.reshape(experts, 1, CAP, moe_input.shape[1])
    slot_weights = jnp.dot(
        row_pick.T, select * gate_weights.reshape(-1)[:, None], precision=lax.Precision.HIGHEST
    )
    arrived = lax.all_to_all(outgoing, "ctx", split_axis=0, concat_axis=1, tiled=True)
    gate_part = jnp.einsum(
        "escd,edf->escf", arrived, expert_gate, preferred_element_type=jnp.float32
    )
    up_part = jnp.einsum("escd,edf->escf", arrived, expert_up, preferred_element_type=jnp.float32)
    gate_sum, up_sum = lax.psum((gate_part, up_part), "grp")
    activated = (jax.nn.silu(gate_sum) * up_sum).astype(jnp.bfloat16)
    result = jnp.einsum(
        "escf,efd->escd", activated, expert_down, preferred_element_type=jnp.float32
    ).astype(jnp.bfloat16)
    returned = lax.all_to_all(result, "ctx", split_axis=1, concat_axis=0, tiled=True)
    returned = returned.reshape(experts * CAP, moe_input.shape[1]).astype(jnp.float32)
    combined = jnp.dot(slot_weights, returned, precision=lax.Precision.HIGHEST)
    return (hidden + combined).astype(jnp.bfloat16)


def solution(mesh):
    in_specs = (
        P(None, "ctx", None),
        P(None, "ctx", None),
        P("ctx", None, None),
        P("ctx", None, None),
        P("grp", None),
        P("ctx", "grp"),
        P("ctx", "grp"),
        P("ctx", None),
        P("ctx", None),
        P("ctx", "grp", None),
        P("ctx", "grp", None),
        P("ctx", None, "grp"),
    )
    out_specs = P("ctx", "grp")
    return jax.shard_map(
        per_device, mesh=mesh, in_specs=in_specs, out_specs=out_specs, check_vma=False
    )
```

profile of v0, /device:TPU:0, one launch (start us, length us, event | category | flops | bytes accessed | tf_op | source)
XLA Modules:
  0.0 214.5 jit_solution(10186053110269310295)
XLA Ops:
  6.5 0.0 copy-start
  6.5 0.0 all-gather.2.cloned.1.call-start
  6.5 0.7 all-gather.2.cloned.1.call-update
  7.3 0.0 reduce-scatter.2.cloned.1.call-start
  7.3 1.0 copy.17
  8.3 0.0 copy-done
  8.3 1.4 fusion.15
  9.8 22.6 %all-gather.2.cloned.1.call-done = bf16[1536,576]{0,1:T(8,128)(2,1)} async-done(((bf16[384,576]{0,1:T(8,128)(2,1)}), bf16[1536,576]{0,1:T(8,128)(2,1)}) %all-gather.2.cloned.1.call-update) | async-done | bytes 1769488 | tf_op jit(solution)/shard_map/all_gather | solution.py:37
  32.4 2.6 %fusion.41 = (f32[16,16]{1,0:T(8,128)S(1)}, bf16[16,16,1536]{2,1,0:T(8,128)(2,1)S(1)}) fusion(bf16[1536,576]{0,1:T(8,128)(2,1)} %all-gather.2.cloned.1.call-done, bf16[16,16,576]{2,0,1:T(8,128)(2,1)S(1)} %fusion.24), kind=kOutput, calls=%fused_computation.60 | convolution fusion | flops 454559232 | bytes 2851840 | tf_op jit(solution)/shard_map/sub | solution.py:45
  35.0 0.0 copy-start.2
  35.0 0.1 copy.21
  35.1 2.3 %fusion.14 = f32[16,16,512]{2,0,1:T(8,128)S(1)} fusion(bf16[1536,576]{0,1:T(8,128)(2,1)} %all-gather.2.cloned.1.call-done, bf16[16,16,1536]{2,1,0:T(8,128)(2,1)S(1)} %get-tuple-element.8), kind=kOutput, calls=%fused_computation.16 | convolution fusion | flops 402653184 | bytes 2883584 | tf_op jit(solution)/shard_map/rhj,jl->rhl/dot_general | solution.py:47
  37.3 0.0 copy-done.2
  37.3 1.0 fusion.18
  38.3 5.8 %all_gather.7 = bf16[64,2048]{1,0:T(8,128)(2,1)S(1)} all-gather(bf16[16,2048]{1,0:T(8,128)(2,1)S(1)} %bitcast.66), channel_id=1, replica_groups=mesh['ctx'=8,'grp'=4] {'grp'}, dimensions={0}, use_global_device_ids=true | all-gather | bytes 327680 | tf_op jit(solution)/shard_map/all_gather | solution.py:56
  44.1 0.0 copy-start.6
  44.1 0.0 copy-start.4
  44.1 5.2 %fusion.46 = f32[64,1792]{1,0:T(8,128)} fusion(bf16[64,2048]{1,0:T(8,128)(2,1)S(1)} %all_gather.7, bf16[2048,1792]{1,0:T(8,128)(2,1)} %param.17), kind=kOutput, calls=%fused_computation.61 | convolution fusion | flops 469762048 | bytes 8060928 | tf_op jit(solution)/shard_map/dot_general | solution.py:59
  49.3 0.0 reduce-scatter.2.cloned.1.call-update
  49.4 0.0 all-reduce.3.cloned.1.call-start
  49.4 0.0 copy-done.6
  49.4 0.1 reshape.40
  49.5 0.1 fusion.31
  49.6 0.1 reduce_window_sum.11
  49.7 0.2 select_reduce_fusion
  49.9 0.3 convolution_convert_fusion.2
  50.1 61.2 %reduce-scatter.2.cloned.1.call-done = f32[8,1792]{1,0:T(8,128)} async-done(((f32[64,1792]{1,0:T(8,128)}), f32[8,1792]{1,0:T(8,128)}) %reduce-scatter.2.cloned.1.call-update) | async-done | bytes 57360 | tf_op jit(solution)/shard_map/reduce_scatter | solution.py:58
  111.4 0.0 copy-done.4
  111.4 1.1 convolution_convert_fusion
  112.5 0.1 reshape.41
  112.6 14.9 %all_to_all.33 = bf16[32,1,4,1792]{3,2,1,0:T(4,128)(2,1)S(1)} all-to-all(bf16[32,1,4,1792]{3,2,1,0:T(4,128)(2,1)S(1)} %bitcast.65), channel_id=1, replica_groups=mesh['ctx'=8,'grp'=4] {'ctx'}, dimensions={0} | all-to-all | bytes 917504 | tf_op jit(solution)/shard_map/all_to_all | solution.py:91
  127.5 8.5 %fusion.3 = f32[4,8,4,1024]{3,1,2,0:T(8,128)} fusion(bf16[4,1792,1024]{2,1,0:T(8,128)(2,1)} %param.22, bf16[8,4,1,4,1792]{4,3,1,0,2:T(4,128)(2,1)S(1)} %bitcast.62), kind=kOutput, calls=%fused_computation.3 | convolution fusion | flops 469762048 | bytes 15663104 | tf_op jit(solution)/shard_map/escd,edf->escf/dot_general | solution.py:95
  136.0 8.5 %fusion.5 = f32[4,8,4,1024]{3,1,2,0:T(8,128)} fusion(bf16[4,1792,1024]{2,1,0:T(8,128)(2,1)} %param.21, bf16[8,4,1,4,1792]{4,3,1,0,2:T(4,128)(2,1)S(1)} %bitcast.63), kind=kOutput, calls=%fused_computation.5 | convolution fusion | flops 469762048 | bytes 15663104 | tf_op jit(solution)/shard_map/escd,edf->escf/dot_general | solution.py:92
  144.5 0.0 all-reduce.3.cloned.1.call-update
  144.5 35.3 %all-reduce.3.cloned.1.call-done = (f32[4,8,4,1024]{3,1,2,0:T(8,128)}, f32[4,8,4,1024]{3,1,2,0:T(8,128)}) async-done(((f32[4,8,4,1024]{3,1,2,0:T(8,128)}, f32[4,8,4,1024]{3,1,2,0:T(8,128)}), (f32[4,8,4,1024]{3,1,2,0:T(8,128)}, f32[4,8,4,1024]{3,1,2,0:T(8,128)})) %all-reduce.3.cloned.1.call-update) | async-done | bytes 1048592 | tf_op jit(solution)/shard_map/psum | solution.py:96
  179.8 0.0 copy-start.5
  179.8 0.0 copy-start.1
  179.8 7.9 %fusion.9 = bf16[4,8,4,1792]{3,1,2,0:T(8,128)(2,1)S(1)} fusion(bf16[4,1024,1792]{2,1,0:T(8,128)(2,1)} %param.23, f32[4,8,4,1024]{3,1,2,0:T(8,128)} %get-tuple-element.5, f32[4,8,4,1024]{3,1,2,0:T(8,128)} %get-tuple-element.6), kind=kOutput, calls=%fused_computation.11 | convolution fusion | flops 470777856 | bytes 16187392 | tf_op jit(solution)/shard_map/escf,efd->escd/dot_general | solution.py:98
  187.7 0.0 copy-start.3
  187.7 0.9 copy.25
  188.6 5.5 %all-to-all-start.1 = ((bf16[4,8,4,1792]{3,2,0,1:T(4,128)(2,1)}), bf16[4,8,4,1792]{3,2,0,1:T(4,128)(2,1)S(1)}, u32[]{:S(2)}, u32[]{:S(2)}) async-start(bf16[4,8,4,1792]{3,2,0,1:T(4,128)(2,1)} %copy.25), calls=%async_computation.2 | async-start | bytes 917504 | tf_op jit(solution)/shard_map/all_to_all | solution.py:101
  194.2 0.0 copy-done.5
  194.2 0.1 reduce_sum.29
  194.3 0.1 multiply_divide_fusion
  194.4 0.1 mul.53
  194.4 0.3 fusion.29
  194.7 12.2 %all-to-all-done.1 = bf16[4,8,4,1792]{3,2,0,1:T(4,128)(2,1)S(1)} async-done(((bf16[4,8,4,1792]{3,2,0,1:T(4,128)(2,1)}), bf16[4,8,4,1792]{3,2,0,1:T(4,128)(2,1)S(1)}, u32[]{:S(2)}, u32[]{:S(2)}) %all-to-all-start.1) | async-done | bytes 458784 | tf_op jit(solution)/shard_map/all_to_all | solution.py:101
  207.0 0.1 reshape.42
  207.1 0.0 copy-done.3
  207.1 0.9 fusion.12
  208.0 0.0 copy-done.1
  (3 shorter events, 0.1 us)
Async XLA Ops:
  6.5 1.8 copy-start
  6.5 25.8 %all-gather.2.cloned.1.call-start = ((), (), s32[]{:S(2)}) async-start(), calls=%async_computation.3 | async-start | bytes 2211840 | tf_op jit(solution)/shard_map/all_gather | solution.py:37
  7.3 104.1 %reduce-scatter.2.cloned.1.call-start = ((), (), s32[]{:S(2)}) async-start(), calls=%async_computation.4 | async-start | bytes 516096 | tf_op jit(solution)/shard_map/reduce_scatter | solution.py:58
  35.0 2.3 %copy-start.2 = (bf16[16,512,128]{2,1,0:T(8,128)(2,1)S(1)}, bf16[16,512,128]{2,1,0:T(8,128)(2,1)}, u32[]{:S(2)}) copy-start(bf16[16,512,128]{2,1,0:T(8,128)(2,1)} %param.15) | copy-start | bytes 6291460
  44.1 5.3 %copy-start.6 = (s32[8,8]{1,0:T(8,128)S(1)}, s32[8,8]{1,0:T(8,128)}, u32[]{:S(2)}) copy-start(s32[8,8]{1,0:T(8,128)} %param.19) | copy-start | bytes 772
  44.1 67.3 %copy-start.4 = (bf16[8,1792]{1,0:T(8,128)(2,1)S(1)}, bf16[8,1792]{1,0:T(8,128)(2,1)}, u32[]{:S(2)}) copy-start(bf16[8,1792]{1,0:T(8,128)(2,1)} %param.18) | copy-start | bytes 86020
  49.4 130.5 %all-reduce.3.cloned.1.call-start = ((), (), s32[]{:S(2)}) async-start(), calls=%async_computation.5 | async-start | bytes 2097152 | tf_op jit(solution)/shard_map/psum | solution.py:96
  179.8 14.3 %copy-start.5 = (f32[8,8]{1,0:T(8,128)S(1)}, f32[8,8]{1,0:T(8,128)}, u32[]{:S(2)}) copy-start(f32[8,8]{1,0:T(8,128)} %param.20) | copy-start | bytes 772
  179.8 28.2 %copy-start.1 = (bf16[16,128,512]{2,1,0:T(8,128)(2,1)S(1)}, bf16[16,128,512]{2,1,0:T(8,128)(2,1)}, u32[]{:S(2)}) copy-start(bf16[16,128,512]{2,1,0:T(8,128)(2,1)} %param.14) | copy-start | bytes 6291460
  187.7 19.4 %copy-start.3 = (f32[8,1792]{1,0:T(8,128)S(1)}, f32[8,1792]{1,0:T(8,128)}, u32[]{:S(2)}) copy-start(f32[8,1792]{1,0:T(8,128)} %reduce-scatter.2.cloned.1.call-done) | copy-start | bytes 172036
  188.6 18.3 %all-to-all-start.1 = ((bf16[4,8,4,1792]{3,2,0,1:T(4,128)(2,1)}), bf16[4,8,4,1792]{3,2,0,1:T(4,128)(2,1)S(1)}, u32[]{:S(2)}, u32[]{:S(2)}) async-start(bf16[4,8,4,1792]{3,2,0,1:T(4,128)(2,1)} %copy.25), calls=%async_computation.2 | async-start | bytes 917504 | tf_op jit(solution)/shard_map/all_to_all | solution.py:101
Sparse Core Ops, SparseCore 0:
  8.9 23.4 all-gather.1
  49.5 61.8 reduce-scatter.1
  144.7 35.1 all-reduce.2
where the time goes:
time: 215 us
  waiting for transfers between devices  132 us (61%)
  matrix products  39.8 us (19%)
  blocking collectives  20.7 us (10%)
  between operations  13.2 us (6%)
  starting transfers between devices  5.6 us (3%)
  local copies, waits for them, and re-layouts  2.45 us (1%)
    reduce_scatter x1, waiting for transfers between devices, per_device(): lax.psum_scatter(jnp.dot(attended, w_out, preferred_element_type=jnp.floa...  61.2 us
    psum x1, waiting for transfers between devices, per_device(): gate_sum, up_sum = lax.psum((gate_part, up_part), 'grp')  35.3 us
    all_gather x1, waiting for transfers between devices, per_device(): all_keys = lax.all_gather(prompt, 'grp', axis=0, tiled=True)  22.6 us
    all_to_all x1, blocking collectives, per_device(): lax.all_to_all(outgoing, 'ctx', split_axis=0, concat_axis=1, tiled=True)  14.9 us
    all_to_all x1, waiting for transfers between devices, per_device(): lax.all_to_all(result, 'ctx', split_axis=1, concat_axis=0, tiled=True)  12.2 us
    dot_general x1, matrix products, per_device(): jnp.einsum('escd,edf->escf', arrived, expert_up, preferred_element_type=j...  8.49 us
    dot_general x1, matrix products, per_device(): jnp.einsum('escd,edf->escf', arrived, expert_gate, preferred_element_type...  8.48 us
    dot_general x1, matrix products, per_device(): jnp.einsum('escf,efd->escd', activated, expert_down, preferred_element_ty...  7.86 us
  transfers between devices with their start and end apart: 4, of which 4 were waited for; matrix products, arithmetic and copies ran while one was open for 2% of the time, Pallas kernels for 0%

commit v1 on v0

v1 whole, which is shorter than its diff:
```python
import jax
import jax.numpy as jnp
from jax import lax
from jax.sharding import PartitionSpec as P

LAT = 512
CAP = 4
route_factor = 2.5
F32 = jnp.float32
BF16 = jnp.bfloat16


def swap(x, axis, bits):
    size = lax.axis_size(axis)
    return lax.ppermute(x, axis, [(a, a ^ bits) for a in range(size)])


def pick(x, index, axis=0):
    return lax.dynamic_index_in_dim(x, index, axis, keepdims=False)


def ctx_scatter_sum(x):
    size = lax.axis_size("ctx")
    me = lax.axis_index("ctx")
    low, high = me & 1, me >> 1
    x = x.reshape(size // 2, 2, -1, x.shape[-1])
    got = swap(pick(x, 1 - low, 1).astype(BF16), "ctx", 1)
    x = pick(x, low, 1) + got.astype(F32)
    total = pick(x, high)
    sends = [pick(x, high ^ s).astype(BF16) for s in range(1, size // 2)]
    for s, part in enumerate(sends, 1):
        total = total + swap(part, "ctx", 2 * s).astype(F32)
    return total


def ctx_gather(x):
    size = lax.axis_size("ctx")
    me = lax.axis_index("ctx")
    low, high = me & 1, me >> 1
    parts = [x] + [swap(x, "ctx", 2 * s) for s in range(1, size // 2)]
    mine = jnp.stack(parts)
    other = swap(mine, "ctx", 1)
    both = jnp.stack([jnp.where(low == 0, mine, other), jnp.where(low == 0, other, mine)], 1)
    order = jnp.arange(size // 2) ^ high
    pickm = (order[:, None] == jnp.arange(size // 2)[None, :]).astype(x.dtype)
    rows = both.shape[2]
    out = jnp.dot(pickm, both.reshape(size // 2, -1), precision=lax.Precision.HIGHEST if x.dtype == F32 else None, preferred_element_type=F32).astype(x.dtype)
    return out.reshape(size * rows, x.shape[1])


def per_device(
    q_nope, q_rope, w_uk, w_uv, prompt, w_out, residual, routes, route_scores,
    expert_gate, expert_up, expert_down,
):
    rows, heads, nope = q_nope.shape
    vdim = w_uv.shape[2]
    score_scale = (nope + q_rope.shape[2]) ** (-0.5)
    grp_size = lax.axis_size("grp")
    ctx_size = lax.axis_size("ctx")
    core = lax.axis_index("grp") & 1
    ctx = lax.axis_index("ctx")
    gate_weights = route_factor * route_scores / jnp.sum(route_scores, axis=-1, keepdims=True)
    info = ctx_gather(jnp.concatenate([routes.astype(F32), gate_weights], axis=1))
    all_routes = info[:, : routes.shape[1]].astype(jnp.int32)
    all_weights = info[:, routes.shape[1] :]
    local_experts = expert_gate.shape[0]
    local_rows = residual.shape[0]
    cap = CAP * ctx_size
    expert_ids = ctx * local_experts + jnp.arange(local_experts)
    named = all_routes[None] == expert_ids[:, None, None]
    hit = jnp.any(named, -1)
    weight = jnp.sum(jnp.where(named, all_weights[None], 0.0), -1)
    blocks = hit.reshape(local_experts, ctx_size, local_rows).astype(jnp.int32)
    rank = (jnp.cumsum(blocks, -1) - blocks).reshape(local_experts, rows)
    slot = (jnp.arange(rows) // local_rows)[None] * CAP + rank
    select = hit[:, None, :] & (slot[:, None, :] == jnp.arange(cap)[None, :, None])
    q_latent = jnp.einsum("rhn,hnl->hrl", q_nope, w_uk, preferred_element_type=F32).astype(BF16)
    queries = jnp.concatenate([q_latent, jnp.transpose(q_rope, (1, 0, 2))], axis=-1)
    scores = jnp.einsum("hrc,jc->hrj", queries, prompt, preferred_element_type=F32) * score_scale
    top = jnp.max(scores, axis=-1)
    raised = jnp.exp(scores - top[..., None])
    total = jnp.sum(raised, axis=-1)
    weighted = jnp.einsum(
        "hrj,jl->hrl", raised.astype(BF16), prompt[:, :LAT], preferred_element_type=F32
    )
    values = jnp.einsum(
        "hrl,hlv->rhv", weighted, w_uv.astype(F32), precision=lax.Precision.HIGHEST
    )
    values = values / total.T[..., None]
    lse = (top + jnp.log(total)).T
    half = rows // 2
    mine_v = lax.dynamic_slice_in_dim(values, core * half, half, 0)
    mine_l = lax.dynamic_slice_in_dim(lse, core * half, half, 0)
    send_v = lax.dynamic_slice_in_dim(values, (1 - core) * half, half, 0).astype(BF16)
    send_l = lax.dynamic_slice_in_dim(lse, (1 - core) * half, half, 0)

    def merge(vs, ls):
        ls = jnp.stack(ls)
        m = jnp.max(ls, 0)
        w = jnp.exp(ls - m)
        tot = jnp.sum(w, 0)
        w = w / tot
        out = sum(w[i][..., None] * v.astype(F32) for i, v in enumerate(vs))
        return out, m + jnp.log(tot)

    v, l = merge([mine_v, swap(send_v, "grp", 1)], [mine_l, swap(send_l, "grp", 1)])
    vb = v.astype(BF16)
    v, l = merge(
        [v] + [swap(vb, "grp", 2 * s) for s in range(1, grp_size // 2)],
        [l] + [swap(l, "grp", 2 * s) for s in range(1, grp_size // 2)],
    )
    mine = v.astype(BF16).reshape(half, heads * vdim)
    other = swap(mine, "grp", 1)
    attended = jnp.concatenate(
        [jnp.where(core == 0, mine, other), jnp.where(core == 0, other, mine)], 0
    )
    projected = ctx_scatter_sum(jnp.dot(attended, w_out, preferred_element_type=F32))
    hidden = residual.astype(F32) + projected
    moe_input = ctx_gather(hidden.astype(BF16))
    selb = select.astype(BF16).reshape(local_experts * cap, rows)
    arrived = jnp.dot(selb, moe_input, preferred_element_type=F32).astype(BF16)
    arrived = arrived.reshape(local_experts, cap, -1)
    ff = expert_gate.shape[2]
    gate = jnp.einsum("esd,edf->esf", arrived, expert_gate, preferred_element_type=F32)
    up = jnp.einsum("esd,edf->esf", arrived, expert_up, preferred_element_type=F32)

    def cut(x, c):
        return lax.dynamic_slice_in_dim(x, c * (ff // 2), ff // 2, 2)

    got = swap(jnp.stack([cut(gate, 1 - core), cut(up, 1 - core)]).astype(BF16), "grp", 1)
    part = jnp.stack([cut(gate, core), cut(up, core)]) + got.astype(F32)
    partb = part.astype(BF16)
    for s in range(1, grp_size // 2):
        part = part + swap(partb, "grp", 2 * s).astype(F32)
    act = (jax.nn.silu(part[0]) * part[1]).astype(BF16)
    act_other = swap(act, "grp", 1)
    activated = jnp.concatenate(
        [jnp.where(core == 0, act, act_other), jnp.where(core == 0, act_other, act)], 2
    )
    result = jnp.einsum(
        "esf,efd->esd", activated, expert_down, preferred_element_type=F32
    ).astype(BF16)
    mix = (select * weight[:, None, :]).astype(F32).reshape(local_experts * cap, rows)
    combined = jnp.einsum(
        "sr,sd->rd", mix, result.reshape(local_experts * cap, -1).astype(F32),
        precision=lax.Precision.HIGHEST,
    )
    return (hidden + ctx_scatter_sum(combined)).astype(BF16)


def solution(mesh):
    in_specs = (
        P(None, "ctx", None),
        P(None, "ctx", None),
        P("ctx", None, None),
        P("ctx", None, None),
        P("grp", None),
        P("ctx", "grp"),
        P("ctx", "grp"),
        P("ctx", None),
        P("ctx", None),
        P("ctx", "grp", None),
        P("ctx", "grp", None),
        P("ctx", None, "grp"),
    )
    return jax.shard_map(
        per_device, mesh=mesh, in_specs=in_specs, out_specs=P("ctx", "grp"), check_vma=False
    )
```

time: 215 us -> 114 us (0.53)
  waiting for transfers between devices: 132 us -> 41.5 us
  starting transfers between devices: 5.6 us -> 27.6 us
  blocking collectives: 20.7 us -> 0 us
  between operations: 13.2 us -> 0.45 us
  other arithmetic: 0.59 us -> 6.35 us
  matrix products: 39.8 us -> 35 us
    reduce_scatter x1 -> x0, waiting for transfers between devices: 61.2 us -> none  [per_device(): lax.psum_scatter(jnp.dot(attended, w_out, preferred_element_type=jnp.floa...]
    ppermute x0 -> x24, waiting for transfers between devices: none -> 41.5 us  [swap(): return lax.ppermute(x, axis, [(a, a ^ bits) for a in range(size)])]
    psum x1 -> x0, waiting for transfers between devices: 35.3 us -> none  [per_device(): gate_sum, up_sum = lax.psum((gate_part, up_part), 'grp')]
    ppermute x0 -> x24, starting transfers between devices: none -> 27.6 us  [swap(): return lax.ppermute(x, axis, [(a, a ^ bits) for a in range(size)])]
    all_gather x1 -> x0, waiting for transfers between devices: 22.6 us -> none  [per_device(): all_keys = lax.all_gather(prompt, 'grp', axis=0, tiled=True)]
    all_to_all x1 -> x0, blocking collectives: 14.9 us -> none  [per_device(): lax.all_to_all(outgoing, 'ctx', split_axis=0, concat_axis=1, tiled=True)]
    all_to_all x1 -> x0, waiting for transfers between devices: 12.2 us -> none  [per_device(): lax.all_to_all(result, 'ctx', split_axis=1, concat_axis=0, tiled=True)]
    all_gather x1 -> x0, blocking collectives: 5.79 us -> none  [per_device(): attended = lax.all_gather(own_rows, 'grp', axis=0, tiled=True)]
  transfers between devices with their start and end apart: 4 -> 24, of which waited for: 4 -> 16; matrix products, arithmetic and copies ran while one was open for 2% -> 9% of each run, Pallas kernels for 0% -> 0%
where the time goes in v1:
time: 114 us
  waiting for transfers between devices  41.5 us (36%)
  matrix products  35 us (31%)
  starting transfers between devices  27.6 us (24%)
  other arithmetic  6.35 us (6%)
  local copies, waits for them, and re-layouts  2.79 us (2%)
    ppermute x24, waiting for transfers between devices, swap(): return lax.ppermute(x, axis, [(a, a ^ bits) for a in range(size)])  41.5 us
    ppermute x24, starting transfers between devices, swap(): return lax.ppermute(x, axis, [(a, a ^ bits) for a in range(size)])  27.6 us
    dot_general x1, matrix products, per_device(): jnp.einsum('esf,efd->esd', activated, expert_down, preferred_element_type...  7.91 us
    dot_general x1, matrix products, per_device(): jnp.einsum('esd,edf->esf', arrived, expert_up, preferred_element_type=F32)  7.8 us
    dot_general x1, matrix products, per_device(): jnp.einsum('esd,edf->esf', arrived, expert_gate, preferred_element_type=F32)  7.79 us
    dot_general x1, matrix products, per_device(): jnp.dot(attended, w_out, preferred_element_type=F32)  4.44 us
  transfers between devices with their start and end apart: 24, of which 16 were waited for; matrix products, arithmetic and copies ran while one was open for 9% of the time, Pallas kernels for 0%

profile of v1, /device:TPU:0, one launch (start us, length us, event | category | flops | bytes accessed | tf_op | source)
XLA Modules:
  0.0 113.8 jit_solution(4886512969885342761)
XLA Ops:
  0.0 1.0 reduce_sum.48
  1.0 0.8 multiply_divide_fusion
  1.7 0.7 convert_element_type.169
  2.5 3.0 %collective-permute-start.9 = (f32[8,16]{1,0:T(8,128)S(1)}, f32[8,16]{1,0:T(8,128)S(1)}, u32[]{:S(2)}, u32[]{:S(2)}) collective-permute-start(f32[8,16]{1,0:T(8,128)S(1)} %pad_maximum_fusion.5), channel_id=1, source_target_pairs={{0,8},{4,12},{8,0},{12,4},{16,24},{20,28},{24,16},{28,20},{1,9},{5... | collective-permute-start | bytes 1544 | tf_op jit(solution)/shard_map/ppermute | solution.py:15
  5.5 2.6 %collective-permute-start.10 = (f32[8,16]{1,0:T(8,128)S(1)}, f32[8,16]{1,0:T(8,128)S(1)}, u32[]{:S(2)}, u32[]{:S(2)}) collective-permute-start(f32[8,16]{1,0:T(8,128)S(1)} %pad_maximum_fusion.5), channel_id=1, source_target_pairs={{0,16},{4,20},{8,24},{12,28},{16,0},{20,4},{24,8},{28,12},{1,17},{... | collective-permute-start | bytes 1544 | tf_op jit(solution)/shard_map/ppermute | solution.py:15
  8.1 1.0 copy.64
  9.1 1.4 %convolution_convert_fusion.3 = bf16[16,64,512]{2,1,0:T(8,128)(2,1)S(1)} fusion(bf16[16,128,512]{2,1,0:T(8,128)(2,1)S(1)} %copy-done, bf16[64,16,128]{2,1,0:T(8,128)(2,1)} %param.12), kind=kOutput, calls=%fused_computation.4 | convolution fusion | flops 134742016 | bytes 3407872 | tf_op jit(solution)/shard_map/rhn,hnl->hrl/dot_general | solution.py:77
  10.5 1.0 fusion.60
  11.6 0.6 fusion.1
  12.2 0.5 copy-done.2
  12.7 2.2 %fusion.6 = f32[16,64,512]{2,1,0:T(8,128)S(1)} fusion(f32[16,64,384]{2,1,0:T(8,128)} %copy-done.2, f32[16,64]{1,0:T(8,128)S(1)} %get-tuple-element.27, bf16[384,576]{0,1:T(8,128)(2,1)S(1)} %copy-done.4), kind=kOutput, calls=%fused_computation.13 | convolution fusion | flops 403439616 | bytes 4071424 | tf_op jit(solution)/shard_map/hrj,jl->hrl/dot_general | solution.py:83
  15.0 1.4 %fusion.5 = f32[64,16,128]{2,0,1:T(8,128)S(1)} fusion(f32[16,64,512]{2,1,0:T(8,128)S(1)} %fusion.6, bf16[16,512,128]{2,1,0:T(8,128)(2,1)S(1)} %copy-done.3, f32[64,16]{0,1:T(8,128)S(1)} %bitcast.189), kind=kOutput, calls=%fused_computation.12 | convolution fusion | flops 805437440 | bytes 4722688 | tf_op jit(solution)/shard_map/hrl,hlv->rhv/dot_general | solution.py:86
  16.4 0.5 collective-permute-start.2
  17.0 1.8 %collective-permute-start.12 = (f32[4,8,16]{2,1,0:T(8,128)S(1)}, f32[4,8,16]{2,1,0:T(8,128)S(1)}, u32[]{:S(2)}, u32[]{:S(2)}) collective-permute-start(f32[4,8,16]{2,1,0:T(8,128)S(1)} %pad_maximum_fusion.4), channel_id=1, source_target_pairs={{0,4},{4,0},{8,12},{12,8},{16,20},{20,16},{24,28},{28,24},{1,5},{5... | collective-permute-start | bytes 6152 | tf_op jit(solution)/shard_map/ppermute | solution.py:15
  18.9 1.6 %collective-permute-start.1 = (f32[32,16]{0,1:T(8,128)S(1)}, f32[32,16]{0,1:T(8,128)S(1)}, u32[]{:S(2)}, u32[]{:S(2)}) collective-permute-start(f32[32,16]{0,1:T(8,128)S(1)} %log_add_fusion), channel_id=1, source_target_pairs={{0,2},{1,3},{2,0},{3,1},{4,6},{5,7},{6,4},{7,5},{8,10},{9,11},{10,... | collective-permute-start | bytes 6152 | tf_op jit(solution)/shard_map/ppermute | solution.py:15
  20.4 0.3 collective-permute-done.12
  20.9 1.7 %collective-permute-done.1 = f32[32,16]{0,1:T(8,128)S(1)} collective-permute-done((f32[32,16]{0,1:T(8,128)S(1)}, f32[32,16]{0,1:T(8,128)S(1)}, u32[]{:S(2)}, u32[]{:S(2)}) %collective-permute-start.1) | collective-permute-done | bytes 2080 | tf_op jit(solution)/shard_map/ppermute | solution.py:15
  22.7 0.2 fusion.23
  22.9 1.6 %collective-permute-start.3 = (bf16[32,16,128]{2,0,1:T(8,128)(2,1)S(1)}, bf16[32,16,128]{2,0,1:T(8,128)(2,1)S(1)}, u32[]{:S(2)}, u32[]{:S(2)}) collective-permute-start(bf16[32,16,128]{2,0,1:T(8,128)(2,1)S(1)} %fusion.23), channel_id=1, source_target_pairs={{0,2},{1,3},{2,0},{3,1},{4,6},{5,7},{6,4},{7,5},{8,10},{9,11},{10,... | collective-permute-start | bytes 393224 | tf_op jit(solution)/shard_map/ppermute | solution.py:15
  24.4 3.5 %collective-permute-done.3 = bf16[32,16,128]{2,0,1:T(8,128)(2,1)S(1)} collective-permute-done((bf16[32,16,128]{2,0,1:T(8,128)(2,1)S(1)}, bf16[32,16,128]{2,0,1:T(8,128)(2,1)S(1)}, u32[]{:S(2)}, u32[]{:S(2)}) %collective-permute-start.3) | collective-permute-done | bytes 131104 | tf_op jit(solution)/shard_map/ppermute | solution.py:15
  27.9 0.3 copy_bitcast_fusion.2
  28.3 0.2 fusion.51
  28.6 1.1 collective-permute-done.4
  29.7 0.3 broadcast_select_fusion.3
  30.0 4.4 %fusion.15 = f32[64,1792]{1,0:T(8,128)S(1)} fusion(bf16[2048,1792]{1,0:T(8,128)(2,1)} %param.17, bf16[32,2048]{1,0:T(8,128)(2,1)S(1)} %get-tuple-element.8, bf16[32,2048]{1,0:T(8,128)(2,1)S(1)} %get-tuple-element.7), kind=kOutput, calls=%fused_computation.25 | convolution fusion | flops 470286336 | bytes 8060928 | tf_op jit(solution)/shard_map/dot_general | solution.py:117
  34.5 0.4 collective-permute-start.5
  35.0 4.8 %collective-permute-done.5 = bf16[4,8,1792]{2,1,0:T(8,128)(2,1)S(1)} collective-permute-done((bf16[4,8,1792]{2,1,0:T(8,128)(2,1)S(1)}, bf16[4,8,1792]{2,1,0:T(8,128)(2,1)S(1)}, u32[]{:S(2)}, u32[]{:S(2)}) %collective-permute-start.5) | collective-permute-done | bytes 114720 | tf_op jit(solution)/shard_map/ppermute | solution.py:15
  39.8 0.7 collective-permute-start.6
  40.5 3.5 %collective-permute-start.7 = (bf16[8,1792]{1,0:T(8,128)(2,1)S(1)}, bf16[8,1792]{1,0:T(8,128)(2,1)S(1)}, u32[]{:S(2)}, u32[]{:S(2)}) collective-permute-start(bf16[8,1792]{1,0:T(8,128)(2,1)S(1)} %get-tuple-element.16), channel_id=1, source_target_pairs={{0,16},{4,20},{8,24},{12,28},{16,0},{20,4},{24,8},{28,12},{1,17},{... | collective-permute-start | bytes 86024 | tf_op jit(solution)/shard_map/ppermute | solution.py:15
  44.0 0.2 collective-permute-start.8
  44.3 0.1 compare_reduce_fusion
  44.4 0.8 reduce_window_sum.13
  45.3 0.6 collective-permute-done.7
  45.9 3.8 %collective-permute-done.8 = bf16[8,1792]{1,0:T(8,128)(2,1)S(1)} collective-permute-done((bf16[8,1792]{1,0:T(8,128)(2,1)S(1)}, bf16[8,1792]{1,0:T(8,128)(2,1)S(1)}, u32[]{:S(2)}, u32[]{:S(2)}) %collective-permute-start.8) | collective-permute-done | bytes 28704 | tf_op jit(solution)/shard_map/ppermute | solution.py:15
  49.8 0.9 collective-permute-start.14
  50.7 3.5 %collective-permute-start.15 = (bf16[8,1792]{1,0:T(8,128)(2,1)S(1)}, bf16[8,1792]{1,0:T(8,128)(2,1)S(1)}, u32[]{:S(2)}, u32[]{:S(2)}) collective-permute-start(bf16[8,1792]{1,0:T(8,128)(2,1)S(1)} %fusion.58), channel_id=1, source_target_pairs={{0,24},{4,28},{8,16},{12,20},{16,8},{20,12},{24,0},{28,4},{1,25},{... | collective-permute-start | bytes 86024 | tf_op jit(solution)/shard_map/ppermute | solution.py:15
  54.2 0.5 collective-permute-done.14
  54.7 1.7 %collective-permute-done.15 = bf16[8,1792]{1,0:T(8,128)(2,1)S(1)} collective-permute-done((bf16[8,1792]{1,0:T(8,128)(2,1)S(1)}, bf16[8,1792]{1,0:T(8,128)(2,1)S(1)}, u32[]{:S(2)}, u32[]{:S(2)}) %collective-permute-start.15) | collective-permute-done | bytes 28704 | tf_op jit(solution)/shard_map/ppermute | solution.py:15
  56.4 0.6 collective-permute-start.16
  57.0 4.3 %collective-permute-done.16 = bf16[4,8,1792]{2,1,0:T(8,128)(2,1)S(1)} collective-permute-done((bf16[4,8,1792]{2,1,0:T(8,128)(2,1)S(1)}, bf16[4,8,1792]{2,1,0:T(8,128)(2,1)S(1)}, u32[]{:S(2)}, u32[]{:S(2)}) %collective-permute-start.16) | collective-permute-done | bytes 114720 | tf_op jit(solution)/shard_map/ppermute | solution.py:15
  61.3 0.1 copy.54
  61.4 0.3 convolution_convert_fusion
  61.8 0.2 reshape.159
  61.9 0.3 convolution_convert_fusion.2
  62.2 7.8 %fusion.61 = f32[4,32,1024]{2,1,0:T(8,128)S(1)} fusion(bf16[4,32,1792]{2,1,0:T(8,128)(2,1)S(1)} %bitcast.170, bf16[4,1792,1024]{2,1,0:T(8,128)(2,1)} %param.21), kind=kOutput, calls=%fused_computation.132 | convolution fusion | flops 469762048 | bytes 15663104 | tf_op jit(solution)/shard_map/esd,edf->esf/dot_general | solution.py:124
  70.0 7.8 %fusion.62 = f32[4,32,1024]{2,1,0:T(8,128)S(1)} fusion(bf16[4,32,1792]{2,1,0:T(8,128)(2,1)S(1)} %bitcast.171, bf16[4,1792,1024]{2,1,0:T(8,128)(2,1)} %param.22), kind=kOutput, calls=%fused_computation.133 | convolution fusion | flops 469762048 | bytes 15663104 | tf_op jit(solution)/shard_map/esd,edf->esf/dot_general | solution.py:125
  78.0 1.5 %collective-permute-done.17 = bf16[2,4,32,512]{3,2,1,0:T(8,128)(2,1)S(1)} collective-permute-done((bf16[2,4,32,512]{3,2,1,0:T(8,128)(2,1)S(1)}, bf16[2,4,32,512]{3,2,1,0:T(8,128)(2,1)S(1)}, u32[]{:S(2)}, u32[]{:S(2)}) %collective-permute-start.17) | collective-permute-done | bytes 262176 | tf_op jit(solution)/shard_map/ppermute | solution.py:15
  79.5 1.5 %collective-permute-start.18 = (bf16[2,4,32,512]{3,2,1,0:T(8,128)(2,1)S(1)}, bf16[2,4,32,512]{3,2,1,0:T(8,128)(2,1)S(1)}, u32[]{:S(2)}, u32[]{:S(2)}) collective-permute-start(bf16[2,4,32,512]{3,2,1,0:T(8,128)(2,1)S(1)} %fusion.12), channel_id=1, source_target_pairs={{0,2},{1,3},{2,0},{3,1},{4,6},{5,7},{6,4},{7,5},{8,10},{9,11},{10,... | collective-permute-start | bytes 786440 | tf_op jit(solution)/shard_map/ppermute | solution.py:15
  81.1 6.9 %collective-permute-done.18 = bf16[2,4,32,512]{3,2,1,0:T(8,128)(2,1)S(1)} collective-permute-done((bf16[2,4,32,512]{3,2,1,0:T(8,128)(2,1)S(1)}, bf16[2,4,32,512]{3,2,1,0:T(8,128)(2,1)S(1)}, u32[]{:S(2)}, u32[]{:S(2)}) %collective-permute-start.18) | collective-permute-done | bytes 262176 | tf_op jit(solution)/shard_map/ppermute | solution.py:15
  87.9 0.1 convert_add_fusion
  88.4 0.1 fusion.44
  88.5 0.1 bitcast_select_fusion
  88.6 0.9 collective-permute-done.19
  89.6 0.1 broadcast_select_fusion.1
  89.7 7.9 %convolution_convert_fusion.1 = bf16[4,32,1792]{2,1,0:T(8,128)(2,1)S(1)} fusion(bf16[4,1024,1792]{2,1,0:T(8,128)(2,1)} %param.23, bf16[4,32,512]{2,1,0:T(8,128)(2,1)S(1)} %get-tuple-element.6, bf16[4,32,512]{2,1,0:T(8,128)(2,1)S(1)} %get-tuple-element.5), kind=kOutput, calls=%fused_computation.1 | convolution fusion | flops 470515712 | bytes 15400960 | tf_op jit(solution)/shard_map/esf,efd->esd/dot_general | solution.py:140
  97.6 0.3 fusion.63
  98.0 0.6 collective-permute-start.20
  98.5 4.7 %collective-permute-done.20 = bf16[4,8,1792]{2,1,0:T(8,128)(2,1)S(1)} collective-permute-done((bf16[4,8,1792]{2,1,0:T(8,128)(2,1)S(1)}, bf16[4,8,1792]{2,1,0:T(8,128)(2,1)S(1)}, u32[]{:S(2)}, u32[]{:S(2)}) %collective-permute-start.20) | collective-permute-done | bytes 114720 | tf_op jit(solution)/shard_map/ppermute | solution.py:15
  103.3 0.3 collective-permute-start.21
  103.6 3.8 %collective-permute-start.22 = (bf16[8,1792]{1,0:T(8,128)(2,1)S(1)}, bf16[8,1792]{1,0:T(8,128)(2,1)S(1)}, u32[]{:S(2)}, u32[]{:S(2)}) collective-permute-start(bf16[8,1792]{1,0:T(8,128)(2,1)S(1)} %get-tuple-element.11), channel_id=1, source_target_pairs={{0,16},{4,20},{8,24},{12,28},{16,0},{20,4},{24,8},{28,12},{1,17},{... | collective-permute-start | bytes 86024 | tf_op jit(solution)/shard_map/ppermute | solution.py:15
  107.4 0.3 collective-permute-start.23
  107.7 1.6 %collective-permute-done.22 = bf16[8,1792]{1,0:T(8,128)(2,1)S(1)} collective-permute-done((bf16[8,1792]{1,0:T(8,128)(2,1)S(1)}, bf16[8,1792]{1,0:T(8,128)(2,1)S(1)}, u32[]{:S(2)}, u32[]{:S(2)}) %collective-permute-start.22) | collective-permute-done | bytes 28704 | tf_op jit(solution)/shard_map/ppermute | solution.py:15
  109.3 3.8 %collective-permute-done.23 = bf16[8,1792]{1,0:T(8,128)(2,1)S(1)} collective-permute-done((bf16[8,1792]{1,0:T(8,128)(2,1)S(1)}, bf16[8,1792]{1,0:T(8,128)(2,1)S(1)}, u32[]{:S(2)}, u32[]{:S(2)}) %collective-permute-start.23) | collective-permute-done | bytes 28704 | tf_op jit(solution)/shard_map/ppermute | solution.py:15
  113.1 0.6 fusion.34
  (74 shorter events, 1.9 us)
Async XLA Ops:
  0.0 9.1 %copy-start = (bf16[16,128,512]{2,1,0:T(8,128)(2,1)S(1)}, bf16[16,128,512]{2,1,0:T(8,128)(2,1)}, u32[]{:S(2)}) copy-start(bf16[16,128,512]{2,1,0:T(8,128)(2,1)} %param.14) | copy-start | bytes 6291460
  0.0 10.5 %copy-start.4 = (bf16[384,576]{0,1:T(8,128)(2,1)S(1)}, bf16[384,576]{0,1:T(8,128)(2,1)}, u32[]{:S(2)}) copy-start(bf16[384,576]{0,1:T(8,128)(2,1)} %param.16) | copy-start | bytes 1327108
  2.5 14.4 %collective-permute-start.9 = (f32[8,16]{1,0:T(8,128)S(1)}, f32[8,16]{1,0:T(8,128)S(1)}, u32[]{:S(2)}, u32[]{:S(2)}) collective-permute-start(f32[8,16]{1,0:T(8,128)S(1)} %pad_maximum_fusion.5), channel_id=1, source_target_pairs={{0,8},{4,12},{8,0},{12,4},{16,24},{20,28},{24,16},{28,20},{1,9},{5... | collective-permute-start | bytes 1544 | tf_op jit(solution)/shard_map/ppermute | solution.py:15
  5.5 11.4 %collective-permute-start.10 = (f32[8,16]{1,0:T(8,128)S(1)}, f32[8,16]{1,0:T(8,128)S(1)}, u32[]{:S(2)}, u32[]{:S(2)}) collective-permute-start(f32[8,16]{1,0:T(8,128)S(1)} %pad_maximum_fusion.5), channel_id=1, source_target_pairs={{0,16},{4,20},{8,24},{12,28},{16,0},{20,4},{24,8},{28,12},{1,17},{... | collective-permute-start | bytes 1544 | tf_op jit(solution)/shard_map/ppermute | solution.py:15
  8.1 8.8 %collective-permute-start.11 = (f32[8,16]{1,0:T(8,128)S(1)}, f32[8,16]{1,0:T(8,128)S(1)}, u32[]{:S(2)}, u32[]{:S(2)}) collective-permute-start(f32[8,16]{1,0:T(8,128)S(1)} %pad_maximum_fusion.5), channel_id=1, source_target_pairs={{0,24},{4,28},{8,16},{12,20},{16,8},{20,12},{24,0},{28,4},{1,25},{... | collective-permute-start | bytes 1544 | tf_op jit(solution)/shard_map/ppermute | solution.py:15
  11.5 1.2 %copy-start.2 = (f32[16,64,384]{2,1,0:T(8,128)}, f32[16,64,384]{2,1,0:T(8,128)S(1)}, u32[]{:S(2)}) copy-start(f32[16,64,384]{2,1,0:T(8,128)S(1)} %get-tuple-element.28) | copy-start | bytes 4718596
  12.1 2.8 %copy-start.3 = (bf16[16,512,128]{2,1,0:T(8,128)(2,1)S(1)}, bf16[16,512,128]{2,1,0:T(8,128)(2,1)}, u32[]{:S(2)}) copy-start(bf16[16,512,128]{2,1,0:T(8,128)(2,1)} %param.15) | copy-start | bytes 6291460
  12.7 6.0 %collective-permute-start = (f32[32,16]{0,1:T(8,128)S(1)}, f32[32,16]{0,1:T(8,128)S(1)}, u32[]{:S(2)}, u32[]{:S(2)}) collective-permute-start(f32[32,16]{0,1:T(8,128)S(1)} %get-tuple-element.26), channel_id=1, source_target_pairs={{0,1},{1,0},{2,3},{3,2},{4,5},{5,4},{6,7},{7,6},{8,9},{9,8},{10,11... | collective-permute-start | bytes 6152 | tf_op jit(solution)/shard_map/ppermute | solution.py:15
  16.4 6.3 %collective-permute-start.2 = (bf16[32,16,128]{2,0,1:T(8,128)(2,1)S(1)}, bf16[32,16,128]{2,0,1:T(8,128)(2,1)S(1)}, u32[]{:S(2)}, u32[]{:S(2)}) collective-permute-start(bf16[32,16,128]{2,0,1:T(8,128)(2,1)S(1)} %dynamic-slice_convert_fusion.2), channel_id=1, source_target_pairs={{0,1},{1,0},{2,3},{3,2},{4,5},{5,4},{6,7},{7,6},{8,9},{9,8},{10,11... | collective-permute-start | bytes 393224 | tf_op jit(solution)/shard_map/ppermute | solution.py:15
  17.0 3.8 %collective-permute-start.12 = (f32[4,8,16]{2,1,0:T(8,128)S(1)}, f32[4,8,16]{2,1,0:T(8,128)S(1)}, u32[]{:S(2)}, u32[]{:S(2)}) collective-permute-start(f32[4,8,16]{2,1,0:T(8,128)S(1)} %pad_maximum_fusion.4), channel_id=1, source_target_pairs={{0,4},{4,0},{8,12},{12,8},{16,20},{20,16},{24,28},{28,24},{1,5},{5... | collective-permute-start | bytes 6152 | tf_op jit(solution)/shard_map/ppermute | solution.py:15
  18.9 3.7 %collective-permute-start.1 = (f32[32,16]{0,1:T(8,128)S(1)}, f32[32,16]{0,1:T(8,128)S(1)}, u32[]{:S(2)}, u32[]{:S(2)}) collective-permute-start(f32[32,16]{0,1:T(8,128)S(1)} %log_add_fusion), channel_id=1, source_target_pairs={{0,2},{1,3},{2,0},{3,1},{4,6},{5,7},{6,4},{7,5},{8,10},{9,11},{10,... | collective-permute-start | bytes 6152 | tf_op jit(solution)/shard_map/ppermute | solution.py:15
  22.9 5.0 %collective-permute-start.3 = (bf16[32,16,128]{2,0,1:T(8,128)(2,1)S(1)}, bf16[32,16,128]{2,0,1:T(8,128)(2,1)S(1)}, u32[]{:S(2)}, u32[]{:S(2)}) collective-permute-start(bf16[32,16,128]{2,0,1:T(8,128)(2,1)S(1)} %fusion.23), channel_id=1, source_target_pairs={{0,2},{1,3},{2,0},{3,1},{4,6},{5,7},{6,4},{7,5},{8,10},{9,11},{10,... | collective-permute-start | bytes 393224 | tf_op jit(solution)/shard_map/ppermute | solution.py:15
  28.2 1.4 %collective-permute-start.4 = (bf16[32,2048]{1,0:T(8,128)(2,1)S(1)}, bf16[32,2048]{1,0:T(8,128)(2,1)S(1)}, u32[]{:S(2)}, u32[]{:S(2)}) collective-permute-start(bf16[32,2048]{1,0:T(8,128)(2,1)S(1)} %copy_bitcast_fusion.2), channel_id=1, source_target_pairs={{0,1},{1,0},{2,3},{3,2},{4,5},{5,4},{6,7},{7,6},{8,9},{9,8},{10,11... | collective-permute-start | bytes 393224 | tf_op jit(solution)/shard_map/ppermute | solution.py:15
  30.0 19.7 %copy-start.5 = (bf16[8,1792]{1,0:T(8,128)(2,1)S(1)}, bf16[8,1792]{1,0:T(8,128)(2,1)}, u32[]{:S(2)}) copy-start(bf16[8,1792]{1,0:T(8,128)(2,1)} %param.18) | copy-start | bytes 86020
  34.5 5.3 %collective-permute-start.5 = (bf16[4,8,1792]{2,1,0:T(8,128)(2,1)S(1)}, bf16[4,8,1792]{2,1,0:T(8,128)(2,1)S(1)}, u32[]{:S(2)}, u32[]{:S(2)}) collective-permute-start(bf16[4,8,1792]{2,1,0:T(8,128)(2,1)S(1)} %fusion.28), channel_id=1, source_target_pairs={{0,4},{4,0},{8,12},{12,8},{16,20},{20,16},{24,28},{28,24},{1,5},{5... | collective-permute-start | bytes 344072 | tf_op jit(solution)/shard_map/ppermute | solution.py:15
  39.8 5.5 %collective-permute-start.6 = (bf16[8,1792]{1,0:T(8,128)(2,1)S(1)}, bf16[8,1792]{1,0:T(8,128)(2,1)S(1)}, u32[]{:S(2)}, u32[]{:S(2)}) collective-permute-start(bf16[8,1792]{1,0:T(8,128)(2,1)S(1)} %get-tuple-element.14), channel_id=1, source_target_pairs={{0,8},{4,12},{8,0},{12,4},{16,24},{20,28},{24,16},{28,20},{1,9},{5... | collective-permute-start | bytes 86024 | tf_op jit(solution)/shard_map/ppermute | solution.py:15
  40.5 5.4 %collective-permute-start.7 = (bf16[8,1792]{1,0:T(8,128)(2,1)S(1)}, bf16[8,1792]{1,0:T(8,128)(2,1)S(1)}, u32[]{:S(2)}, u32[]{:S(2)}) collective-permute-start(bf16[8,1792]{1,0:T(8,128)(2,1)S(1)} %get-tuple-element.16), channel_id=1, source_target_pairs={{0,16},{4,20},{8,24},{12,28},{16,0},{20,4},{24,8},{28,12},{1,17},{... | collective-permute-start | bytes 86024 | tf_op jit(solution)/shard_map/ppermute | solution.py:15
  44.0 5.7 %collective-permute-start.8 = (bf16[8,1792]{1,0:T(8,128)(2,1)S(1)}, bf16[8,1792]{1,0:T(8,128)(2,1)S(1)}, u32[]{:S(2)}, u32[]{:S(2)}) collective-permute-start(bf16[8,1792]{1,0:T(8,128)(2,1)S(1)} %get-tuple-element.15), channel_id=1, source_target_pairs={{0,24},{4,28},{8,16},{12,20},{16,8},{20,12},{24,0},{28,4},{1,25},{... | collective-permute-start | bytes 86024 | tf_op jit(solution)/shard_map/ppermute | solution.py:15
  49.7 4.5 %collective-permute-start.13 = (bf16[8,1792]{1,0:T(8,128)(2,1)S(1)}, bf16[8,1792]{1,0:T(8,128)(2,1)S(1)}, u32[]{:S(2)}, u32[]{:S(2)}) collective-permute-start(bf16[8,1792]{1,0:T(8,128)(2,1)S(1)} %fusion.58), channel_id=1, source_target_pairs={{0,8},{4,12},{8,0},{12,4},{16,24},{20,28},{24,16},{28,20},{1,9},{5... | collective-permute-start | bytes 86024 | tf_op jit(solution)/shard_map/ppermute | solution.py:15
  49.8 4.8 %collective-permute-start.14 = (bf16[8,1792]{1,0:T(8,128)(2,1)S(1)}, bf16[8,1792]{1,0:T(8,128)(2,1)S(1)}, u32[]{:S(2)}, u32[]{:S(2)}) collective-permute-start(bf16[8,1792]{1,0:T(8,128)(2,1)S(1)} %fusion.58), channel_id=1, source_target_pairs={{0,16},{4,20},{8,24},{12,28},{16,0},{20,4},{24,8},{28,12},{1,17},{... | collective-permute-start | bytes 86024 | tf_op jit(solution)/shard_map/ppermute | solution.py:15
  50.7 5.7 %collective-permute-start.15 = (bf16[8,1792]{1,0:T(8,128)(2,1)S(1)}, bf16[8,1792]{1,0:T(8,128)(2,1)S(1)}, u32[]{:S(2)}, u32[]{:S(2)}) collective-permute-start(bf16[8,1792]{1,0:T(8,128)(2,1)S(1)} %fusion.58), channel_id=1, source_target_pairs={{0,24},{4,28},{8,16},{12,20},{16,8},{20,12},{24,0},{28,4},{1,25},{... | collective-permute-start | bytes 86024 | tf_op jit(solution)/shard_map/ppermute | solution.py:15
  56.4 4.9 %collective-permute-start.16 = (bf16[4,8,1792]{2,1,0:T(8,128)(2,1)S(1)}, bf16[4,8,1792]{2,1,0:T(8,128)(2,1)S(1)}, u32[]{:S(2)}, u32[]{:S(2)}) collective-permute-start(bf16[4,8,1792]{2,1,0:T(8,128)(2,1)S(1)} %pad_maximum_fusion.2), channel_id=1, source_target_pairs={{0,4},{4,0},{8,12},{12,8},{16,20},{20,16},{24,28},{28,24},{1,5},{5... | collective-permute-start | bytes 344072 | tf_op jit(solution)/shard_map/ppermute | solution.py:15
  77.9 1.6 %collective-permute-start.17 = (bf16[2,4,32,512]{3,2,1,0:T(8,128)(2,1)S(1)}, bf16[2,4,32,512]{3,2,1,0:T(8,128)(2,1)S(1)}, u32[]{:S(2)}, u32[]{:S(2)}) collective-permute-start(bf16[2,4,32,512]{3,2,1,0:T(8,128)(2,1)S(1)} %pad_maximum_fusion), channel_id=1, source_target_pairs={{0,1},{1,0},{2,3},{3,2},{4,5},{5,4},{6,7},{7,6},{8,9},{9,8},{10,11... | collective-permute-start | bytes 786440 | tf_op jit(solution)/shard_map/ppermute | solution.py:15
  79.5 8.4 %collective-permute-start.18 = (bf16[2,4,32,512]{3,2,1,0:T(8,128)(2,1)S(1)}, bf16[2,4,32,512]{3,2,1,0:T(8,128)(2,1)S(1)}, u32[]{:S(2)}, u32[]{:S(2)}) collective-permute-start(bf16[2,4,32,512]{3,2,1,0:T(8,128)(2,1)S(1)} %fusion.12), channel_id=1, source_target_pairs={{0,2},{1,3},{2,0},{3,1},{4,6},{5,7},{6,4},{7,5},{8,10},{9,11},{10,... | collective-permute-start | bytes 786440 | tf_op jit(solution)/shard_map/ppermute | solution.py:15
  88.1 1.4 %collective-permute-start.19 = (bf16[4,32,512]{2,1,0:T(8,128)(2,1)S(1)}, bf16[4,32,512]{2,1,0:T(8,128)(2,1)S(1)}, u32[]{:S(2)}, u32[]{:S(2)}) collective-permute-start(bf16[4,32,512]{2,1,0:T(8,128)(2,1)S(1)} %fusion.14), channel_id=1, source_target_pairs={{0,1},{1,0},{2,3},{3,2},{4,5},{5,4},{6,7},{7,6},{8,9},{9,8},{10,11... | collective-permute-start | bytes 393224 | tf_op jit(solution)/shard_map/ppermute | solution.py:15
  89.7 24.1 %copy-start.1 = (bf16[16,128,512]{2,1,0:T(8,128)(2,1)S(1)}, bf16[16,128,512]{2,1,0:T(8,128)(2,1)}, u32[]{:S(2)}) copy-start(bf16[16,128,512]{2,1,0:T(8,128)(2,1)} %param.14) | copy-start | bytes 6291460
  98.0 5.3 %collective-permute-start.20 = (bf16[4,8,1792]{2,1,0:T(8,128)(2,1)S(1)}, bf16[4,8,1792]{2,1,0:T(8,128)(2,1)S(1)}, u32[]{:S(2)}, u32[]{:S(2)}) collective-permute-start(bf16[4,8,1792]{2,1,0:T(8,128)(2,1)S(1)} %fusion.27), channel_id=1, source_target_pairs={{0,4},{4,0},{8,12},{12,8},{16,20},{20,16},{24,28},{28,24},{1,5},{5... | collective-permute-start | bytes 344072 | tf_op jit(solution)/shard_map/ppermute | solution.py:15
  103.3 4.5 %collective-permute-start.21 = (bf16[8,1792]{1,0:T(8,128)(2,1)S(1)}, bf16[8,1792]{1,0:T(8,128)(2,1)S(1)}, u32[]{:S(2)}, u32[]{:S(2)}) collective-permute-start(bf16[8,1792]{1,0:T(8,128)(2,1)S(1)} %get-tuple-element.9), channel_id=1, source_target_pairs={{0,8},{4,12},{8,0},{12,4},{16,24},{20,28},{24,16},{28,20},{1,9},{5... | collective-permute-start | bytes 86024 | tf_op jit(solution)/shard_map/ppermute | solution.py:15
  103.6 5.7 %collective-permute-start.22 = (bf16[8,1792]{1,0:T(8,128)(2,1)S(1)}, bf16[8,1792]{1,0:T(8,128)(2,1)S(1)}, u32[]{:S(2)}, u32[]{:S(2)}) collective-permute-start(bf16[8,1792]{1,0:T(8,128)(2,1)S(1)} %get-tuple-element.11), channel_id=1, source_target_pairs={{0,16},{4,20},{8,24},{12,28},{16,0},{20,4},{24,8},{28,12},{1,17},{... | collective-permute-start | bytes 86024 | tf_op jit(solution)/shard_map/ppermute | solution.py:15
  107.4 5.7 %collective-permute-start.23 = (bf16[8,1792]{1,0:T(8,128)(2,1)S(1)}, bf16[8,1792]{1,0:T(8,128)(2,1)S(1)}, u32[]{:S(2)}, u32[]{:S(2)}) collective-permute-start(bf16[8,1792]{1,0:T(8,128)(2,1)S(1)} %get-tuple-element.10), channel_id=1, source_target_pairs={{0,24},{4,28},{8,16},{12,20},{16,8},{20,12},{24,0},{28,4},{1,25},{... | collective-permute-start | bytes 86024 | tf_op jit(solution)/shard_map/ppermute | solution.py:15

commit v2 on v0

v2 whole, which is shorter than its diff:
```python
import jax
import jax.numpy as jnp
from jax import lax
from jax.experimental import pallas as pl
from jax.experimental.pallas import tpu as pltpu
from jax.sharding import PartitionSpec as P

CAP = 4
LANES = 128
route_factor = 2.5
F32 = jnp.float32
BF16 = jnp.bfloat16
VMEM = pltpu.VMEM


def swap(x, axis, bits):
    return lax.ppermute(x, axis, [(a, a ^ bits) for a in range(lax.axis_size(axis))])


def spread(x, axis):
    return [swap(x, axis, 2 * s) for s in range(1, lax.axis_size(axis) // 2)]


def run(name, body, outs, ins, scratch=(), us=1.0, limit=8, hbm=()):
    ins = [
        pltpu.with_memory_space_constraint(a, pltpu.HBM) if i in hbm else a
        for i, a in enumerate(ins)
    ]
    return pl.pallas_call(
        body,
        out_shape=[jax.ShapeDtypeStruct(s, d) for s, d in outs],
        in_specs=[
            pl.BlockSpec(memory_space=pltpu.HBM if i in hbm else VMEM) for i in range(len(ins))
        ],
        out_specs=[pl.BlockSpec(memory_space=VMEM) for _ in outs],
        scratch_shapes=list(scratch),
        cost_estimate=pl.CostEstimate(
            flops=int(us * 1.15e9), bytes_accessed=1024, transcendentals=0
        ),
        compiler_params=pltpu.CompilerParams(vmem_limit_bytes=limit << 20),
        name=name,
    )(*ins)


def split3(x):
    hi = x.astype(BF16).astype(F32)
    mid = (x - hi).astype(BF16).astype(F32)
    return hi, mid, x - hi - mid


def pack_lse(x, heads):
    hi, mid, lo = split3(x)
    return (hi + pltpu.roll(mid, heads, 1) + pltpu.roll(lo, 2 * heads, 1)).astype(BF16)


def unpack_lse(x, heads):
    x = x.astype(F32)
    x = x + pltpu.roll(x, LANES - heads, 1) + pltpu.roll(x, LANES - 2 * heads, 1)
    lane = lax.broadcasted_iota(jnp.int32, x.shape, 1)
    return jnp.where(lane < heads, x, 0.0)


def attend_body(qn_h, qr_h, wuk_h, wuv_h, prompt_h, keep, send, qn, qr, wuk, wuv, prompt, rows_scr, sems):
    rows, heads, nope = qn.shape
    lat, vdim = wuk.shape[2], wuv.shape[2]
    half, width = rows // 2, heads * vdim
    group = min(4, heads)
    steps = heads // group
    core = lax.axis_index("grp") & 1
    copies = [
        pltpu.make_async_copy(qn_h, qn, sems.at[0]),
        pltpu.make_async_copy(qr_h, qr, sems.at[1]),
        pltpu.make_async_copy(prompt_h, prompt, sems.at[2]),
    ]
    uk = [
        pltpu.make_async_copy(
            wuk_h.at[pl.ds(c * group, group)], wuk.at[pl.ds(c * group, group)], sems.at[3 + c]
        )
        for c in range(steps)
    ]
    uv = [
        pltpu.make_async_copy(
            wuv_h.at[pl.ds(c * group, group)], wuv.at[pl.ds(c * group, group)], sems.at[3 + steps + c]
        )
        for c in range(steps)
    ]
    copies[0].start()
    uk[0].start()
    copies[1].start()
    copies[2].start()
    for c in range(steps):
        if c:
            uk[c].start()
        uv[c].start()
    scale = (nope + qr.shape[2]) ** (-0.5)
    copies[0].wait()
    queries = jnp.swapaxes(qn[...], 0, 1)
    copies[1].wait()
    turned = jnp.swapaxes(qr[...], 0, 1)
    lane = lax.broadcasted_iota(jnp.int32, (rows, LANES), 1)
    lse = jnp.zeros((rows, LANES), F32)
    for c in range(steps):
        own = range(c * group, (c + 1) * group)
        uk[c].wait()
        q = jnp.concatenate(
            [jnp.dot(queries[h], wuk[h], preferred_element_type=F32).astype(BF16) for h in own], 0
        )
        r = jnp.concatenate([turned[h] for h in own], 0)
        if c == 0:
            copies[2].wait()
        s = jnp.dot(q, prompt[:lat], preferred_element_type=F32)
        s = (s + jnp.dot(r, prompt[lat:], preferred_element_type=F32)) * scale
        top = jnp.max(s, -1, keepdims=True)
        p = jnp.exp(s - top)
        total = jnp.sum(p, -1, keepdims=True)
        w = lax.dot_general(
            p.astype(BF16), prompt[:lat], (((1,), (1,)), ((), ())), preferred_element_type=F32
        )
        w = w * (1.0 / total)
        hi = w.astype(BF16)
        lo = (w - hi.astype(F32)).astype(BF16)
        part = top + jnp.log(total)
        uv[c].wait()
        for i, h in enumerate(own):
            at = slice(i * rows, (i + 1) * rows)
            v = jnp.dot(jnp.concatenate([hi[at], lo[at]], 0), wuv[h], preferred_element_type=F32)
            rows_scr[:, h * vdim : (h + 1) * vdim] = v[:rows] + v[rows:]
            lse = jnp.where(lane == h, part[at], lse)
    rows_scr[:, width:] = lse
    keep[...] = rows_scr[pl.ds(pl.multiple_of(core * half, half), half)]
    out = rows_scr[pl.ds(pl.multiple_of((1 - core) * half, half), half)]
    send[:, :width] = out[:, :width].astype(BF16)
    send[:, width:] = pack_lse(out[:, width:], heads)


def merge_values(heads, own, others):
    width = own.shape[1] - LANES
    vdim = width // heads
    levels = [own[:, width:]] + [unpack_lse(o[:, width:], heads) for o in others]
    top = levels[0]
    for x in levels[1:]:
        top = jnp.maximum(top, x)
    raised = [jnp.exp(x - top) for x in levels]
    total = sum(raised)
    shares = [x / total for x in raised]
    cols = []
    for h in range(heads):
        at = slice(h * vdim, (h + 1) * vdim)
        v = own[:, at] * shares[0][:, h : h + 1]
        for share, o in zip(shares[1:], others):
            v = v + o[:, at].astype(F32) * share[:, h : h + 1]
        cols.append(v)
    lane = lax.broadcasted_iota(jnp.int32, top.shape, 1)
    return cols, jnp.where(lane < heads, top + jnp.log(total), 0.0)


def pair_body(heads, own, other, keep, send):
    width = own.shape[1] - LANES
    vdim = width // heads
    cols, lse = merge_values(heads, own, [other])
    for h, v in enumerate(cols):
        keep[:, h * vdim : (h + 1) * vdim] = v
        send[:, h * vdim : (h + 1) * vdim] = v.astype(BF16)
    keep[:, width:] = lse
    send[:, width:] = pack_lse(lse, heads)


def final_body(heads, own, *refs):
    out = refs[-1]
    vdim = (own.shape[1] - LANES) // heads
    cols, _ = merge_values(heads, own, refs[:-1])
    for h, v in enumerate(cols):
        out[:, h * vdim : (h + 1) * vdim] = v.astype(BF16)


def place(ctx, turn, s):
    return ctx ^ (2 * s + turn)


def store_blocks(ref, blocks, width):
    step = 16 // blocks[0].shape[0]
    for i in range(0, len(blocks), step):
        part = jnp.concatenate(blocks[i : i + step], 0).astype(BF16)
        n = blocks[0].shape[0]
        ref[i * n : (i + step) * n, :width] = part


def project_body(mine, other, routes, scores, w, keep, send, info, att, res, pad):
    half = mine.shape[0]
    width = w.shape[1]
    tail = send.shape[1] - LANES
    count, top = routes.shape
    n = keep.shape[0] // count
    core = lax.axis_index("grp") & 1
    ctx = lax.axis_index("ctx")
    att[pl.ds(pl.multiple_of(core * half, half), half)] = mine[...]
    att[pl.ds(pl.multiple_of((1 - core) * half, half), half)] = other[...]
    res[...] = jnp.dot(att[...], w[...], preferred_element_type=F32)

    def block(turn, s):
        return res[pl.ds(pl.multiple_of(place(ctx, turn, s) * count, count), count)]

    store_blocks(send, [block(1, s) for s in range(n)], width)
    for s in range(n):
        keep[s * count : (s + 1) * count] = block(0, s)
    v = scores[...]
    v = route_factor * v / jnp.sum(v, -1, keepdims=True)
    hi, mid, lo = split3(v)
    pad[...] = jnp.zeros_like(pad)
    for i, x in enumerate((routes[...].astype(F32), hi, mid, lo)):
        pad[:count, i * top : (i + 1) * top] = x
    if tail > width:
        send[:, width:tail] = jnp.zeros((send.shape[0], tail - width), BF16)
    send[:, tail:] = jnp.zeros((send.shape[0], LANES), BF16)
    send[: pad.shape[0], tail:] = pad[...].astype(BF16)
    info[...] = pad[:count]


def pair_rows_body(has_info, *refs):
    keep, other = refs[:2]
    if has_info:
        info, own, *sends, info2 = refs[2:]
    else:
        own, *sends = refs[2:]
    count, width = own.shape
    tail = other.shape[1] - LANES
    if has_info:
        theirs = other[:16, tail:].astype(F32)[:count]
        both = info[...] + pltpu.roll(theirs, 64, 1)
        info2[...] = both
    for s in range(len(sends) + 1):
        if s % 2 == 0:
            pair = other[s * count : (s + 2) * count, :width].astype(F32)
        x = keep[s * count : (s + 1) * count] + pair[(s % 2) * count : (s % 2 + 1) * count]
        if s == 0:
            own[...] = x
        else:
            sends[s - 1][:, :width] = x.astype(BF16)
            if has_info:
                if tail > width:
                    sends[s - 1][:, width:tail] = jnp.zeros((count, tail - width), BF16)
                sends[s - 1][:, tail:] = both.astype(BF16)


def hidden_body(own, residual, *refs):
    *others, hidden, moe = refs
    width = own.shape[1]
    x = own[...] + residual[...].astype(F32)
    for o in others:
        x = x + o[:, :width].astype(F32)
    hidden[...] = x
    moe[...] = x.astype(BF16)


def route_body(local_experts, top, info, *refs):
    *others, pick, mix = refs
    count = info.shape[0]
    ctx = lax.axis_index("ctx")
    blocks = [info[...]] + [o[:, o.shape[1] - LANES :].astype(F32) for o in others]
    near = jnp.concatenate(blocks, 0)
    table = jnp.concatenate([near, pltpu.roll(near, 64, 1)], 0)
    rows = table.shape[0]
    weights = (
        pltpu.roll(table, LANES - top, 1)
        + pltpu.roll(table, LANES - 2 * top, 1)
        + pltpu.roll(table, LANES - 3 * top, 1)
    )
    lane = lax.broadcasted_iota(jnp.int32, (rows, LANES), 1)
    hits, gains = [], []
    all_hits = jnp.zeros((rows, LANES), F32)
    for e in range(local_experts):
        named = (table == (ctx * local_experts + e).astype(F32)) & (lane < top)
        hit = jnp.sum(jnp.where(named, 1.0, 0.0), -1, keepdims=True)
        gains.append(jnp.sum(jnp.where(named, weights, 0.0), -1, keepdims=True))
        hits.append(hit)
        all_hits = jnp.where(lane == e, hit, all_hits)
    a = lax.broadcasted_iota(jnp.int32, (rows, rows), 0)
    b = lax.broadcasted_iota(jnp.int32, (rows, rows), 1)
    earlier = jnp.where((a // count == b // count) & (b < a), 1.0, 0.0).astype(BF16)
    rank = jnp.dot(earlier, all_hits.astype(BF16), preferred_element_type=F32)
    slots = mix.shape[1]
    cap = slots // local_experts
    wide = lax.broadcasted_iota(jnp.int32, (rows, slots), 1)
    start = lax.broadcasted_iota(jnp.int32, (rows, 1), 0) // count * CAP
    chosen = jnp.zeros((rows, slots), F32)
    gain = jnp.zeros((rows, slots), F32)
    for e in range(local_experts):
        slot = rank[:, e : e + 1].astype(jnp.int32) + start + e * cap
        at = (wide == slot) & (hits[e] > 0.5)
        chosen = jnp.where(at, 1.0, chosen)
        gain = jnp.where(at, gains[e], gain)
    pick[...] = jnp.transpose(chosen).astype(BF16)
    mix[...] = gain


def rows_body(*refs):
    *parts, out = refs
    width = out.shape[1]
    store_blocks(out, [p[...].astype(F32) for p in parts], width)


def first_half_body(experts, pick, near, far, gate, up, *refs):
    *maybe, send = refs
    hid = send.shape[2] // 2
    cap = send.shape[1]
    core = lax.axis_index("grp") & 1
    cols = pl.ds(pl.multiple_of((1 - core) * hid, hid), hid)
    rows = jnp.concatenate([near[...], far[...]], 0)
    x = jnp.dot(pick[...], rows, preferred_element_type=F32).astype(BF16)
    maybe[0][...] = x
    for i, e in enumerate(experts):
        xe = x[e * cap : (e + 1) * cap]
        send[i, :, :hid] = jnp.dot(xe, gate[e, :, cols], preferred_element_type=F32).astype(BF16)
        send[i, :, hid:] = jnp.dot(xe, up[e, :, cols], preferred_element_type=F32).astype(BF16)


def next_half_body(experts, x, gate, up, send):
    hid = send.shape[2] // 2
    cap = send.shape[1]
    core = lax.axis_index("grp") & 1
    cols = pl.ds(pl.multiple_of((1 - core) * hid, hid), hid)
    for i, e in enumerate(experts):
        xe = x[e * cap : (e + 1) * cap]
        send[i, :, :hid] = jnp.dot(xe, gate[e, :, cols], preferred_element_type=F32).astype(BF16)
        send[i, :, hid:] = jnp.dot(xe, up[e, :, cols], preferred_element_type=F32).astype(BF16)


def own_half_body(experts, x, gate, up, other, keep, send):
    hid = send.shape[2] // 2
    cap = send.shape[1]
    core = lax.axis_index("grp") & 1
    cols = pl.ds(pl.multiple_of(core * hid, hid), hid)
    for i, e in enumerate(experts):
        xe = x[e * cap : (e + 1) * cap]
        for j, w in enumerate((gate, up)):
            at = slice(j * hid, (j + 1) * hid)
            v = jnp.dot(xe, w[e, :, cols], preferred_element_type=F32)
            v = v + other[i, :, at].astype(F32)
            keep[i, :, at] = v
            send[i, :, at] = v.astype(BF16)


def act_body(keep, *refs):
    *others, out = refs
    hid = out.shape[2]
    for i in range(out.shape[0]):
        x = keep[i]
        for o in others:
            x = x + o[i].astype(F32)
        gate, up = x[:, :hid], x[:, hid:]
        out[i] = (gate / (1.0 + jnp.exp(-gate)) * up).astype(BF16)


def down_body(experts, last, mine, other, down, mix, *refs):
    hid = mine.shape[2]
    cap = mine.shape[1]
    core = lax.axis_index("grp") & 1
    low = pl.ds(pl.multiple_of(core * hid, hid), hid)
    high = pl.ds(pl.multiple_of((1 - core) * hid, hid), hid)
    parts = []
    for i, e in enumerate(experts):
        v = jnp.dot(mine[i], down[e, low], preferred_element_type=F32)
        v = v + jnp.dot(other[i], down[e, high], preferred_element_type=F32)
        parts.append(v.astype(BF16))
    result = jnp.concatenate(parts, 0)
    gain = mix[:, experts[0] * cap : (experts[-1] + 1) * cap]
    hi = gain.astype(BF16)
    lo = (gain - hi.astype(F32)).astype(BF16)
    v = jnp.dot(hi, result, preferred_element_type=F32)
    v = v + jnp.dot(lo, result, preferred_element_type=F32)
    if experts[0]:
        v = v + refs[0][...]
    if not last:
        refs[-1][...] = v
    else:
        keep, send = refs[-2:]
        half = keep.shape[0]
        keep[...] = v[:half]
        send[...] = v[half:].astype(BF16)


def out_body(hidden, own, *refs):
    *others, out = refs
    x = hidden[...] + own[...]
    for o in others:
        x = x + o[...].astype(F32)
    out[...] = x.astype(BF16)


def bind(body, *first):
    def bound(*refs):
        return body(*first, *refs)

    return bound


def per_device(
    q_nope, q_rope, w_uk, w_uv, prompt, w_out, residual, routes, route_scores,
    expert_gate, expert_up, expert_down,
):
    rows, heads, nope = q_nope.shape
    lat, vdim = w_uk.shape[2], w_uv.shape[2]
    n_grp, n_ctx = lax.axis_size("grp"), lax.axis_size("ctx")
    count, width = residual.shape
    top = routes.shape[1]
    experts, _, ff = expert_gate.shape
    cap = CAP * n_ctx
    hid = ff // 2
    half = rows // 2
    hv = heads * vdim
    tail = -(-width // LANES) * LANES
    far = n_ctx // 2
    in_vmem = lambda a: pltpu.with_memory_space_constraint(a, VMEM)

    keys = prompt.T
    keep, send = run(
        "attend", attend_body, [((half, hv + LANES), F32), ((half, hv + LANES), BF16)],
        [q_nope, q_rope, w_uk, w_uv, keys],
        scratch=[
            VMEM(q_nope.shape, BF16), VMEM(q_rope.shape, BF16), VMEM(w_uk.shape, BF16),
            VMEM(w_uv.shape, BF16), VMEM(keys.shape, BF16), VMEM((rows, hv + LANES), F32),
            pltpu.SemaphoreType.DMA((3 + 2 * (heads // min(4, heads)),)),
        ],
        us=6, limit=16, hbm=range(5),
    )
    keep, send = run(
        "pair", bind(pair_body, heads), [((half, hv + LANES), F32), ((half, hv + LANES), BF16)],
        [keep, swap(send, "grp", 1)], us=3,
    )
    (mine,) = run(
        "merge", bind(final_body, heads), [((half, hv), BF16)], [keep] + spread(send, "grp"), us=5
    )
    keep, send, info = run(
        "project", project_body,
        [((rows // 2, width), F32), ((rows // 2, tail + LANES), BF16), ((count, LANES), F32)],
        [mine, swap(mine, "grp", 1), routes, route_scores, in_vmem(w_out)],
        scratch=[VMEM((rows, hv), BF16), VMEM((rows, width), F32), VMEM((16, LANES), F32)], us=3,
    )
    own, *sends, info = run(
        "rows", bind(pair_rows_body, True),
        [((count, width), F32)] + [((count, tail + LANES), BF16)] * (far - 1) + [((count, LANES), F32)],
        [keep, swap(send, "ctx", 1), info], us=5,
    )
    got = [swap(x, "ctx", 2 * s) for s, x in enumerate(sends, 1)]
    hidden, moe = run(
        "hidden", hidden_body, [((count, width), F32), ((count, width), BF16)],
        [own, residual] + got, us=5,
    )
    parts = spread(moe, "ctx")
    pick, mix = run(
        "route", bind(route_body, experts, top),
        [((experts * cap, rows), BF16), ((rows, experts * cap), F32)], [info] + got, us=1,
    )
    (near,) = run("gather", rows_body, [((rows // 2, width), BF16)], [moe] + parts, us=5)
    far_rows = swap(near, "ctx", 1)
    gate, up, down = in_vmem(expert_gate), in_vmem(expert_up), in_vmem(expert_down)
    size = max(1, experts // 2)
    groups = [range(i, i + size) for i in range(0, experts, size)]
    shape = (size, cap, 2 * hid)
    sent = []
    for g in groups:
        if not sent:
            x, send = run(
                "other_half", bind(first_half_body, g), [((experts * cap, width), BF16), (shape, BF16)],
                [pick, near, far_rows, gate, up], us=2,
            )
        else:
            (send,) = run(
                "other_half", bind(next_half_body, g), [(shape, BF16)], [x, gate, up], us=1.5
            )
        sent.append(swap(send, "grp", 1))
    sums = []
    for g, other in zip(groups, sent):
        keep, send = run(
            "own_half", bind(own_half_body, g), [(shape, F32), (shape, BF16)],
            [x, gate, up, other], us=1.5,
        )
        sums.append((keep, spread(send, "grp")))
    acts = []
    for keep, others in sums:
        (act,) = run("act", act_body, [((size, cap, hid), BF16)], [keep] + others, us=0.5)
        acts.append((act, swap(act, "grp", 1)))
    so_far = []
    for g, (act, other) in zip(groups, acts):
        last = g is groups[-1]
        outs = [((rows // 2, width), F32), ((rows // 2, width), BF16)] if last else [((rows, width), F32)]
        so_far = run(
            "down", bind(down_body, g, last), outs, [act, other, down, mix] + list(so_far), us=1.5
        )
    keep, send = so_far
    own, *sends = run(
        "rows2", bind(pair_rows_body, False),
        [((count, width), F32)] + [((count, width), BF16)] * (far - 1),
        [keep, swap(send, "ctx", 1)], us=3,
    )
    got = [swap(x, "ctx", 2 * s) for s, x in enumerate(sends, 1)]
    (out,) = run("out", out_body, [((count, width), BF16)], [hidden, own] + got, us=1)
    return out


def solution(mesh):
    in_specs = (
        P(None, "ctx", None),
        P(None, "ctx", None),
        P("ctx", None, None),
        P("ctx", None, None),
        P("grp", None),
        P("ctx", "grp"),
        P("ctx", "grp"),
        P("ctx", None),
        P("ctx", None),
        P("ctx", "grp", None),
        P("ctx", "grp", None),
        P("ctx", None, "grp"),
    )
    return jax.shard_map(
        per_device, mesh=mesh, in_specs=in_specs, out_specs=P("ctx", "grp"), check_vma=False
    )
```

time: 215 us -> 82.7 us (0.38)
  waiting for transfers between devices: 132 us -> 34.5 us
  matrix products: 39.8 us -> 0 us
  blocking collectives: 20.7 us -> 0 us
  starting transfers between devices: 5.6 us -> 24.6 us
  Pallas kernels: 0 us -> 17.8 us
  between operations: 13.2 us -> 0.33 us
  local copies, waits for them, and re-layouts: 2.45 us -> 5.37 us
    reduce_scatter x1 -> x0, waiting for transfers between devices: 61.2 us -> none  [per_device(): lax.psum_scatter(jnp.dot(attended, w_out, preferred_element_type=jnp.floa...]
    dot_general x11 -> x0, matrix products: 37.2 us -> none  [the longest x1 8.49 us: per_device(): jnp.einsum('escd,edf->escf', arrived, expert_up, preferred_element_type=j...]
    psum x1 -> x0, waiting for transfers between devices: 35.3 us -> none  [per_device(): gate_sum, up_sum = lax.psum((gate_part, up_part), 'grp')]
    ppermute x0 -> x21, waiting for transfers between devices: none -> 34.5 us  [swap(): lax.ppermute(x, axis, [(a, a ^ bits) for a in range(lax.axis_size(axis))])]
    ppermute x0 -> x21, starting transfers between devices: none -> 24.6 us  [swap(): lax.ppermute(x, axis, [(a, a ^ bits) for a in range(lax.axis_size(axis))])]
    all_gather x1 -> x0, waiting for transfers between devices: 22.6 us -> none  [per_device(): all_keys = lax.all_gather(prompt, 'grp', axis=0, tiled=True)]
    pallas_call x0 -> x18, Pallas kernels: none -> 17.8 us  [run(): pl.pallas_call(body, out_shape=[jax.ShapeDtypeStruct(s, d) for s, d in ou...]
    all_to_all x1 -> x0, blocking collectives: 14.9 us -> none  [per_device(): lax.all_to_all(outgoing, 'ctx', split_axis=0, concat_axis=1, tiled=True)]
  transfers between devices with their start and end apart: 4 -> 21, of which waited for: 4 -> 14; matrix products, arithmetic and copies ran while one was open for 2% -> 0% of each run, Pallas kernels for 0% -> 8%
where the time goes in v2:
time: 82.7 us; the launch traced here: 82.6 us
  waiting for transfers between devices  34.5 us (42%)
  starting transfers between devices  24.6 us (30%)
  Pallas kernels  17.8 us (22%)
  local copies, waits for them, and re-layouts  5.37 us (6%)
    ppermute x21, waiting for transfers between devices, swap(): lax.ppermute(x, axis, [(a, a ^ bits) for a in range(lax.axis_size(axis))])  34.5 us
    ppermute x21, starting transfers between devices, swap(): lax.ppermute(x, axis, [(a, a ^ bits) for a in range(lax.axis_size(axis))])  24.6 us
    pallas_call x18, Pallas kernels, run(): pl.pallas_call(body, out_shape=[jax.ShapeDtypeStruct(s, d) for s, d in ou...  17.8 us
    unnamed x36, local copies, waits for them, and re-layouts  5.37 us
  transfers between devices with their start and end apart: 21, of which 14 were waited for; matrix products, arithmetic and copies ran while one was open for 0% of the time, Pallas kernels for 8%

profile of v2, /device:TPU:0, one launch (start us, length us, event | category | flops | bytes accessed | tf_op | source)
XLA Modules:
  0.0 82.6 jit_solution(11378973869427944405)
XLA Ops:
  0.0 5.6 %attend.1 = (f32[32,2176]{1,0:T(8,128)S(1)}, bf16[32,2176]{1,0:T(8,128)(2,1)S(1)}) custom-call(bf16[64,16,128]{2,1,0:T(8,128)(2,1)} %qn_h.1, bf16[64,16,64]{2,1,0:T(8,128)(2,1)} %qr_h.1, bf16[16,128,512]{2,1,0:T(8,128)(2,1)} %wuk_h.1, bf16[16,512,128]{2,1,0:T(8,128)(2,1)} %wuv_h.1, bf16[576,384]{1,0:T(8,128)(2,1)} %bitcast.9), custom_call_target="tpu_custom_call" | custom-call | flops 6899999744 | bytes 1024 | tf_op jit(solution)/shard_map/attend/pallas_call | solution.py:29
  5.6 0.5 collective-permute-start
  6.1 1.0 %collective-permute-done.refs_1_ = bf16[32,2176]{1,0:T(8,128)(2,1)S(1)} collective-permute-done((bf16[32,2176]{1,0:T(8,128)(2,1)S(1)}, bf16[32,2176]{1,0:T(8,128)(2,1)S(1)}, u32[]{:S(2)}, u32[]{:S(2)}) %collective-permute-start) | collective-permute-done | bytes 139296 | tf_op jit(solution)/shard_map/ppermute | solution.py:17
  7.1 0.3 pair.1
  7.4 2.9 %collective-permute-start.1 = (bf16[32,2176]{1,0:T(8,128)(2,1)S(1)}, bf16[32,2176]{1,0:T(8,128)(2,1)S(1)}, u32[]{:S(2)}, u32[]{:S(2)}) collective-permute-start(bf16[32,2176]{1,0:T(8,128)(2,1)S(1)} %get-tuple-element.36), channel_id=1, source_target_pairs={{0,2},{1,3},{2,0},{3,1},{4,6},{5,7},{6,4},{7,5},{8,10},{9,11},{10,... | collective-permute-start | bytes 417800 | tf_op jit(solution)/shard_map/ppermute | solution.py:17
  10.4 4.0 %collective-permute-done.1.refs_1_ = bf16[32,2176]{1,0:T(8,128)(2,1)S(1)} collective-permute-done((bf16[32,2176]{1,0:T(8,128)(2,1)S(1)}, bf16[32,2176]{1,0:T(8,128)(2,1)S(1)}, u32[]{:S(2)}, u32[]{:S(2)}) %collective-permute-start.1) | collective-permute-done | bytes 139296 | tf_op jit(solution)/shard_map/ppermute | solution.py:17
  14.3 0.3 merge.1.mine
  14.7 0.0 copy-start.1
  14.7 0.1 collective-permute-start.2
  14.8 1.3 %collective-permute-done.2.other = bf16[32,2048]{1,0:T(8,128)(2,1)S(1)} collective-permute-done((bf16[32,2048]{1,0:T(8,128)(2,1)S(1)}, bf16[32,2048]{1,0:T(8,128)(2,1)S(1)}, u32[]{:S(2)}, u32[]{:S(2)}) %collective-permute-start.2) | collective-permute-done | bytes 131104 | tf_op jit(solution)/shard_map/ppermute | solution.py:17
  16.1 0.1 slice-done.13
  16.2 1.4 %project.1 = (f32[32,1792]{1,0:T(8,128)S(1)}, bf16[32,1920]{1,0:T(8,128)(2,1)S(1)}, f32[8,128]{1,0:T(8,128)S(1)}) custom-call(bf16[32,2048]{1,0:T(8,128)(2,1)S(1)} %merge.1.mine, bf16[32,2048]{1,0:T(8,128)(2,1)S(1)} %collective-permute-done.2.other, s32[8,8]{1,0:T(8,128)S(1)} %copy-done.2, f32[8,8]{1,0:T(8,128)S(1)} %copy-done.3, bf16[2048,1792]{1,0:T(8,128)(2,1)S(1)} %bitcast.8), custom_call_target="tpu_custom_call" | custom-call | flops 3449999872 | bytes 1024 | tf_op jit(solution)/shard_map/project/pallas_call | solution.py:29
  17.7 1.8 %collective-permute-start.3 = (bf16[32,1920]{1,0:T(8,128)(2,1)S(1)}, bf16[32,1920]{1,0:T(8,128)(2,1)S(1)}, u32[]{:S(2)}, u32[]{:S(2)}) collective-permute-start(bf16[32,1920]{1,0:T(8,128)(2,1)S(1)} %get-tuple-element.38), channel_id=1, source_target_pairs={{0,4},{4,0},{8,12},{12,8},{16,20},{20,16},{24,28},{28,24},{1,5},{5... | collective-permute-start | bytes 368648 | tf_op jit(solution)/shard_map/ppermute | solution.py:17
  19.5 3.5 %collective-permute-done.3.refs_1_ = bf16[32,1920]{1,0:T(8,128)(2,1)S(1)} collective-permute-done((bf16[32,1920]{1,0:T(8,128)(2,1)S(1)}, bf16[32,1920]{1,0:T(8,128)(2,1)S(1)}, u32[]{:S(2)}, u32[]{:S(2)}) %collective-permute-start.3) | collective-permute-done | bytes 122912 | tf_op jit(solution)/shard_map/ppermute | solution.py:17
  23.0 0.1 rows.1
  23.1 1.8 %collective-permute-start.4 = (bf16[8,1920]{1,0:T(8,128)(2,1)S(1)}, bf16[8,1920]{1,0:T(8,128)(2,1)S(1)}, u32[]{:S(2)}, u32[]{:S(2)}) collective-permute-start(bf16[8,1920]{1,0:T(8,128)(2,1)S(1)} %get-tuple-element.41), channel_id=1, source_target_pairs={{0,8},{4,12},{8,0},{12,4},{16,24},{20,28},{24,16},{28,20},{1,9},{5... | collective-permute-start | bytes 92168 | tf_op jit(solution)/shard_map/ppermute | solution.py:17
  24.9 2.6 %collective-permute-start.5 = (bf16[8,1920]{1,0:T(8,128)(2,1)S(1)}, bf16[8,1920]{1,0:T(8,128)(2,1)S(1)}, u32[]{:S(2)}, u32[]{:S(2)}) collective-permute-start(bf16[8,1920]{1,0:T(8,128)(2,1)S(1)} %get-tuple-element.42), channel_id=1, source_target_pairs={{0,16},{4,20},{8,24},{12,28},{16,0},{20,4},{24,8},{28,12},{1,17},{... | collective-permute-start | bytes 92168 | tf_op jit(solution)/shard_map/ppermute | solution.py:17
  27.5 0.0 collective-permute-start.6
  27.5 0.0 collective-permute-done.4.refs_0_.refs_1_
  27.5 2.4 %collective-permute-done.5.refs_1_.refs_2_ = bf16[8,1920]{1,0:T(8,128)(2,1)S(1)} collective-permute-done((bf16[8,1920]{1,0:T(8,128)(2,1)S(1)}, bf16[8,1920]{1,0:T(8,128)(2,1)S(1)}, u32[]{:S(2)}, u32[]{:S(2)}) %collective-permute-start.5) | collective-permute-done | bytes 30752 | tf_op jit(solution)/shard_map/ppermute | solution.py:17
  29.9 3.3 %collective-permute-done.6.refs_2_.refs_3_ = bf16[8,1920]{1,0:T(8,128)(2,1)S(1)} collective-permute-done((bf16[8,1920]{1,0:T(8,128)(2,1)S(1)}, bf16[8,1920]{1,0:T(8,128)(2,1)S(1)}, u32[]{:S(2)}, u32[]{:S(2)}) %collective-permute-start.6) | collective-permute-done | bytes 30752 | tf_op jit(solution)/shard_map/ppermute | solution.py:17
  33.2 0.0 slice-start.5
  33.2 0.0 slice-start.2
  33.3 0.0 slice-start.3
  33.3 0.0 slice-start.6
  33.3 0.0 slice-start.7
  33.3 0.1 collective-permute-start.7
  33.4 0.9 %collective-permute-start.8 = (bf16[8,1792]{1,0:T(8,128)(2,1)S(1)}, bf16[8,1792]{1,0:T(8,128)(2,1)S(1)}, u32[]{:S(2)}, u32[]{:S(2)}) collective-permute-start(bf16[8,1792]{1,0:T(8,128)(2,1)S(1)} %get-tuple-element.47.refs_0_), channel_id=1, source_target_pairs={{0,16},{4,20},{8,24},{12,28},{16,0},{20,4},{24,8},{28,12},{1,17},{... | collective-permute-start | bytes 86024 | tf_op jit(solution)/shard_map/ppermute | solution.py:17
  34.3 3.5 %collective-permute-start.9 = (bf16[8,1792]{1,0:T(8,128)(2,1)S(1)}, bf16[8,1792]{1,0:T(8,128)(2,1)S(1)}, u32[]{:S(2)}, u32[]{:S(2)}) collective-permute-start(bf16[8,1792]{1,0:T(8,128)(2,1)S(1)} %get-tuple-element.47.refs_0_), channel_id=1, source_target_pairs={{0,24},{4,28},{8,16},{12,20},{16,8},{20,12},{24,0},{28,4},{1,25},{... | collective-permute-start | bytes 86024 | tf_op jit(solution)/shard_map/ppermute | solution.py:17
  37.8 0.5 collective-permute-done.8.refs_2_
  38.2 1.7 %collective-permute-done.9.refs_3_ = bf16[8,1792]{1,0:T(8,128)(2,1)S(1)} collective-permute-done((bf16[8,1792]{1,0:T(8,128)(2,1)S(1)}, bf16[8,1792]{1,0:T(8,128)(2,1)S(1)}, u32[]{:S(2)}, u32[]{:S(2)}) %collective-permute-start.9) | collective-permute-done | bytes 28704 | tf_op jit(solution)/shard_map/ppermute | solution.py:17
  39.9 1.6 %collective-permute-start.10 = (bf16[32,1792]{1,0:T(8,128)(2,1)S(1)}, bf16[32,1792]{1,0:T(8,128)(2,1)S(1)}, u32[]{:S(2)}, u32[]{:S(2)}) collective-permute-start(bf16[32,1792]{1,0:T(8,128)(2,1)S(1)} %gather.1.refs_1_), channel_id=1, source_target_pairs={{0,4},{4,0},{8,12},{12,8},{16,20},{20,16},{24,28},{28,24},{1,5},{5... | collective-permute-start | bytes 344072 | tf_op jit(solution)/shard_map/ppermute | solution.py:17
  41.5 0.5 route.1
  42.0 2.8 %collective-permute-done.10.refs_2_ = bf16[32,1792]{1,0:T(8,128)(2,1)S(1)} collective-permute-done((bf16[32,1792]{1,0:T(8,128)(2,1)S(1)}, bf16[32,1792]{1,0:T(8,128)(2,1)S(1)}, u32[]{:S(2)}, u32[]{:S(2)}) %collective-permute-start.10) | collective-permute-done | bytes 114720 | tf_op jit(solution)/shard_map/ppermute | solution.py:17
  44.9 1.5 %other_half.2 = (bf16[128,1792]{1,0:T(8,128)(2,1)S(1)}, bf16[2,32,1024]{2,1,0:T(8,128)(2,1)S(1)}) custom-call(bf16[128,64]{1,0:T(8,128)(2,1)S(1)} %get-tuple-element.46.refs_0_, bf16[32,1792]{1,0:T(8,128)(2,1)S(1)} %gather.1.refs_1_, bf16[32,1792]{1,0:T(8,128)(2,1)S(1)} %collective-permute-done.10.refs_2_, bf16[4,1792,1024]{2,1,0:T(8,128)(2,1)S(1)} %bitcast.2, ...), custom_call_target="tpu_custom_call" | custom-call | flops 2300000000 | bytes 1024 | tf_op jit(solution)/shard_map/other_half/pallas_call | solution.py:29
  46.3 0.0 collective-permute-start.14
  46.4 1.4 %other_half.3 = bf16[2,32,1024]{2,1,0:T(8,128)(2,1)S(1)} custom-call(bf16[128,1792]{1,0:T(8,128)(2,1)S(1)} %get-tuple-element.48.refs_0_, bf16[4,1792,1024]{2,1,0:T(8,128)(2,1)S(1)} %bitcast.2, bf16[4,1792,1024]{2,1,0:T(8,128)(2,1)S(1)} %bitcast.4), custom_call_target="tpu_custom_call" | custom-call | flops 1724999936 | bytes 1024 | tf_op jit(solution)/shard_map/other_half/pallas_call | solution.py:29
  47.8 0.5 collective-permute-start.11
  48.2 1.3 %own_half.3 = (f32[2,32,1024]{2,1,0:T(8,128)S(1)}, bf16[2,32,1024]{2,1,0:T(8,128)(2,1)S(1)}) custom-call(bf16[128,1792]{1,0:T(8,128)(2,1)S(1)} %get-tuple-element.48.refs_0_, bf16[4,1792,1024]{2,1,0:T(8,128)(2,1)S(1)} %bitcast.2, bf16[4,1792,1024]{2,1,0:T(8,128)(2,1)S(1)} %bitcast.4, bf16[2,32,1024]{2,1,0:T(8,128)(2,1)S(1)} %collective-permute-done.14.refs_3_), custom_call_target="tpu_custom_call" | custom-call | flops 1724999936 | bytes 1024 | tf_op jit(solution)/shard_map/own_half/pallas_call | solution.py:29
  49.6 1.6 %collective-permute-start.15 = (bf16[2,32,1024]{2,1,0:T(8,128)(2,1)S(1)}, bf16[2,32,1024]{2,1,0:T(8,128)(2,1)S(1)}, u32[]{:S(2)}, u32[]{:S(2)}) collective-permute-start(bf16[2,32,1024]{2,1,0:T(8,128)(2,1)S(1)} %get-tuple-element.54), channel_id=1, source_target_pairs={{0,2},{1,3},{2,0},{3,1},{4,6},{5,7},{6,4},{7,5},{8,10},{9,11},{10,... | collective-permute-start | bytes 393224 | tf_op jit(solution)/shard_map/ppermute | solution.py:17
  51.2 0.0 collective-permute-done.11.refs_3_
  51.2 1.4 %own_half.2 = (f32[2,32,1024]{2,1,0:T(8,128)S(1)}, bf16[2,32,1024]{2,1,0:T(8,128)(2,1)S(1)}) custom-call(bf16[128,1792]{1,0:T(8,128)(2,1)S(1)} %get-tuple-element.48.refs_0_, bf16[4,1792,1024]{2,1,0:T(8,128)(2,1)S(1)} %bitcast.2, bf16[4,1792,1024]{2,1,0:T(8,128)(2,1)S(1)} %bitcast.4, bf16[2,32,1024]{2,1,0:T(8,128)(2,1)S(1)} %collective-permute-done.11.refs_3_), custom_call_target="tpu_custom_call" | custom-call | flops 1724999936 | bytes 1024 | tf_op jit(solution)/shard_map/own_half/pallas_call | solution.py:29
  52.5 0.6 collective-permute-start.12
  53.1 2.1 %collective-permute-done.15.refs_0_ = bf16[2,32,1024]{2,1,0:T(8,128)(2,1)S(1)} collective-permute-done((bf16[2,32,1024]{2,1,0:T(8,128)(2,1)S(1)}, bf16[2,32,1024]{2,1,0:T(8,128)(2,1)S(1)}, u32[]{:S(2)}, u32[]{:S(2)}) %collective-permute-start.15) | collective-permute-done | bytes 131104 | tf_op jit(solution)/shard_map/ppermute | solution.py:17
  55.2 0.1 act.3.refs_0_
  55.3 0.1 collective-permute-start.16
  55.3 2.6 %collective-permute-done.12.refs_0_ = bf16[2,32,1024]{2,1,0:T(8,128)(2,1)S(1)} collective-permute-done((bf16[2,32,1024]{2,1,0:T(8,128)(2,1)S(1)}, bf16[2,32,1024]{2,1,0:T(8,128)(2,1)S(1)}, u32[]{:S(2)}, u32[]{:S(2)}) %collective-permute-start.12) | collective-permute-done | bytes 131104 | tf_op jit(solution)/shard_map/ppermute | solution.py:17
  57.9 0.1 act.2.refs_0_
  58.0 0.1 collective-permute-start.13
  58.1 0.0 collective-permute-done.16.refs_1_
  58.1 0.0 copy-start
  58.1 5.2 %copy-done = bf16[4,1024,1792]{2,1,0:T(8,128)(2,1)S(1)} copy-done((bf16[4,1024,1792]{2,1,0:T(8,128)(2,1)S(1)}, bf16[4,1024,1792]{2,1,0:T(8,128)(2,1)}, u32[]{:S(2)}) %copy-start) | copy-done | bytes 14680088
  63.3 1.6 %down.2.refs_4_ = f32[64,1792]{1,0:T(8,128)S(1)} custom-call(bf16[2,32,512]{2,1,0:T(8,128)(2,1)S(1)} %act.3.refs_0_, bf16[2,32,512]{2,1,0:T(8,128)(2,1)S(1)} %collective-permute-done.16.refs_1_, bf16[4,1024,1792]{2,1,0:T(8,128)(2,1)S(1)} %copy-done, f32[64,128]{1,0:T(8,128)S(1)} %get-tuple-element.51.refs_3_), custom_call_target="tpu_custom_call" | custom-call | flops 1724999936 | bytes 1024 | tf_op jit(solution)/shard_map/down/pallas_call | solution.py:29
  64.9 0.0 collective-permute-done.13.refs_1_
  64.9 1.6 %down.3 = (f32[32,1792]{1,0:T(8,128)S(1)}, bf16[32,1792]{1,0:T(8,128)(2,1)S(1)}) custom-call(bf16[2,32,512]{2,1,0:T(8,128)(2,1)S(1)} %act.2.refs_0_, bf16[2,32,512]{2,1,0:T(8,128)(2,1)S(1)} %collective-permute-done.13.refs_1_, bf16[4,1024,1792]{2,1,0:T(8,128)(2,1)S(1)} %bitcast.6, f32[64,128]{1,0:T(8,128)S(1)} %get-tuple-element.51.refs_3_, ...), custom_call_target="tpu_custom_call" | custom-call | flops 1724999936 | bytes 1024 | tf_op jit(solution)/shard_map/down/pallas_call | solution.py:29
  66.5 1.6 %collective-permute-start.17 = (bf16[32,1792]{1,0:T(8,128)(2,1)S(1)}, bf16[32,1792]{1,0:T(8,128)(2,1)S(1)}, u32[]{:S(2)}, u32[]{:S(2)}) collective-permute-start(bf16[32,1792]{1,0:T(8,128)(2,1)S(1)} %get-tuple-element.56), channel_id=1, source_target_pairs={{0,4},{4,0},{8,12},{12,8},{16,20},{20,16},{24,28},{28,24},{1,5},{5... | collective-permute-start | bytes 344072 | tf_op jit(solution)/shard_map/ppermute | solution.py:17
  68.1 4.0 %collective-permute-done.17.refs_1_ = bf16[32,1792]{1,0:T(8,128)(2,1)S(1)} collective-permute-done((bf16[32,1792]{1,0:T(8,128)(2,1)S(1)}, bf16[32,1792]{1,0:T(8,128)(2,1)S(1)}, u32[]{:S(2)}, u32[]{:S(2)}) %collective-permute-start.17) | collective-permute-done | bytes 114720 | tf_op jit(solution)/shard_map/ppermute | solution.py:17
  72.1 0.3 collective-permute-start.18
  72.4 3.8 %collective-permute-start.19 = (bf16[8,1792]{1,0:T(8,128)(2,1)S(1)}, bf16[8,1792]{1,0:T(8,128)(2,1)S(1)}, u32[]{:S(2)}, u32[]{:S(2)}) collective-permute-start(bf16[8,1792]{1,0:T(8,128)(2,1)S(1)} %get-tuple-element.59), channel_id=1, source_target_pairs={{0,16},{4,20},{8,24},{12,28},{16,0},{20,4},{24,8},{28,12},{1,17},{... | collective-permute-start | bytes 86024 | tf_op jit(solution)/shard_map/ppermute | solution.py:17
  76.3 0.3 collective-permute-start.20
  76.6 0.0 collective-permute-done.18.refs_0_
  76.6 2.1 %collective-permute-done.19.refs_1_ = bf16[8,1792]{1,0:T(8,128)(2,1)S(1)} collective-permute-done((bf16[8,1792]{1,0:T(8,128)(2,1)S(1)}, bf16[8,1792]{1,0:T(8,128)(2,1)S(1)}, u32[]{:S(2)}, u32[]{:S(2)}) %collective-permute-start.19) | collective-permute-done | bytes 28704 | tf_op jit(solution)/shard_map/ppermute | solution.py:17
  78.7 3.2 %collective-permute-done.20.refs_2_ = bf16[8,1792]{1,0:T(8,128)(2,1)S(1)} collective-permute-done((bf16[8,1792]{1,0:T(8,128)(2,1)S(1)}, bf16[8,1792]{1,0:T(8,128)(2,1)S(1)}, u32[]{:S(2)}, u32[]{:S(2)}) %collective-permute-start.20) | collective-permute-done | bytes 28704 | tf_op jit(solution)/shard_map/ppermute | solution.py:17
  81.9 0.6 out.1
  (36 shorter events, 0.1 us)
Async XLA Ops:
  5.6 1.5 %collective-permute-start = (bf16[32,2176]{1,0:T(8,128)(2,1)S(1)}, bf16[32,2176]{1,0:T(8,128)(2,1)S(1)}, u32[]{:S(2)}, u32[]{:S(2)}) collective-permute-start(bf16[32,2176]{1,0:T(8,128)(2,1)S(1)} %get-tuple-element.34), channel_id=1, source_target_pairs={{0,1},{1,0},{2,3},{3,2},{4,5},{5,4},{6,7},{7,6},{8,9},{9,8},{10,11... | collective-permute-start | bytes 417800 | tf_op jit(solution)/shard_map/ppermute | solution.py:17
  7.1 9.0 %slice-start.12 = ((s8[7340032]{0:T(1024)(128)(4,1)}), s8[4194304]{0:T(1024)(128)(4,1)S(1)}, s32[]{:S(2)}) async-start(s8[7340032]{0:T(1024)(128)(4,1)} %bitcast.7), calls=%async_computation.12 | async-start | bytes 8388608
  7.1 9.0 %copy-start.2 = (s32[8,8]{1,0:T(8,128)S(1)}, s32[8,8]{1,0:T(8,128)}, u32[]{:S(2)}) copy-start(s32[8,8]{1,0:T(8,128)} %routes.1) | copy-start | bytes 772
  7.1 9.0 %copy-start.3 = (f32[8,8]{1,0:T(8,128)S(1)}, f32[8,8]{1,0:T(8,128)}, u32[]{:S(2)}) copy-start(f32[8,8]{1,0:T(8,128)} %scores.1) | copy-start | bytes 772
  7.4 6.9 %collective-permute-start.1 = (bf16[32,2176]{1,0:T(8,128)(2,1)S(1)}, bf16[32,2176]{1,0:T(8,128)(2,1)S(1)}, u32[]{:S(2)}, u32[]{:S(2)}) collective-permute-start(bf16[32,2176]{1,0:T(8,128)(2,1)S(1)} %get-tuple-element.36), channel_id=1, source_target_pairs={{0,2},{1,3},{2,0},{3,1},{4,6},{5,7},{6,4},{7,5},{8,10},{9,11},{10,... | collective-permute-start | bytes 417800 | tf_op jit(solution)/shard_map/ppermute | solution.py:17
  14.3 1.9 %slice-start.13 = ((s8[7340032]{0:T(1024)(128)(4,1)}), s8[3145728]{0:T(1024)(128)(4,1)S(1)}, s32[]{:S(2)}) async-start(s8[7340032]{0:T(1024)(128)(4,1)} %bitcast.7), calls=%async_computation.13 | async-start | bytes 6291456
  14.7 18.5 %copy-start.1 = (bf16[8,1792]{1,0:T(8,128)(2,1)S(1)}, bf16[8,1792]{1,0:T(8,128)(2,1)}, u32[]{:S(2)}) copy-start(bf16[8,1792]{1,0:T(8,128)(2,1)} %residual.1) | copy-start | bytes 86020
  14.7 1.4 %collective-permute-start.2 = (bf16[32,2048]{1,0:T(8,128)(2,1)S(1)}, bf16[32,2048]{1,0:T(8,128)(2,1)S(1)}, u32[]{:S(2)}, u32[]{:S(2)}) collective-permute-start(bf16[32,2048]{1,0:T(8,128)(2,1)S(1)} %merge.1.mine), channel_id=1, source_target_pairs={{0,1},{1,0},{2,3},{3,2},{4,5},{5,4},{6,7},{7,6},{8,9},{9,8},{10,11... | collective-permute-start | bytes 393224 | tf_op jit(solution)/shard_map/ppermute | solution.py:17
  17.7 5.4 %collective-permute-start.3 = (bf16[32,1920]{1,0:T(8,128)(2,1)S(1)}, bf16[32,1920]{1,0:T(8,128)(2,1)S(1)}, u32[]{:S(2)}, u32[]{:S(2)}) collective-permute-start(bf16[32,1920]{1,0:T(8,128)(2,1)S(1)} %get-tuple-element.38), channel_id=1, source_target_pairs={{0,4},{4,0},{8,12},{12,8},{16,20},{20,16},{24,28},{28,24},{1,5},{5... | collective-permute-start | bytes 368648 | tf_op jit(solution)/shard_map/ppermute | solution.py:17
  23.1 4.4 %collective-permute-start.4 = (bf16[8,1920]{1,0:T(8,128)(2,1)S(1)}, bf16[8,1920]{1,0:T(8,128)(2,1)S(1)}, u32[]{:S(2)}, u32[]{:S(2)}) collective-permute-start(bf16[8,1920]{1,0:T(8,128)(2,1)S(1)} %get-tuple-element.41), channel_id=1, source_target_pairs={{0,8},{4,12},{8,0},{12,4},{16,24},{20,28},{24,16},{28,20},{1,9},{5... | collective-permute-start | bytes 92168 | tf_op jit(solution)/shard_map/ppermute | solution.py:17
  24.9 5.0 %collective-permute-start.5 = (bf16[8,1920]{1,0:T(8,128)(2,1)S(1)}, bf16[8,1920]{1,0:T(8,128)(2,1)S(1)}, u32[]{:S(2)}, u32[]{:S(2)}) collective-permute-start(bf16[8,1920]{1,0:T(8,128)(2,1)S(1)} %get-tuple-element.42), channel_id=1, source_target_pairs={{0,16},{4,20},{8,24},{12,28},{16,0},{20,4},{24,8},{28,12},{1,17},{... | collective-permute-start | bytes 92168 | tf_op jit(solution)/shard_map/ppermute | solution.py:17
  27.5 5.7 %collective-permute-start.6 = (bf16[8,1920]{1,0:T(8,128)(2,1)S(1)}, bf16[8,1920]{1,0:T(8,128)(2,1)S(1)}, u32[]{:S(2)}, u32[]{:S(2)}) collective-permute-start(bf16[8,1920]{1,0:T(8,128)(2,1)S(1)} %get-tuple-element.43), channel_id=1, source_target_pairs={{0,24},{4,28},{8,16},{12,20},{16,8},{20,12},{24,0},{28,4},{1,25},{... | collective-permute-start | bytes 92168 | tf_op jit(solution)/shard_map/ppermute | solution.py:17
  33.2 11.6 %slice-start = ((s8[14680064]{0:T(1024)(128)(4,1)}), s8[4194304]{0:T(1024)(128)(4,1)S(1)}, s32[]{:S(2)}) async-start(s8[14680064]{0:T(1024)(128)(4,1)} %bitcast.1), calls=%async_computation | async-start | bytes 8388608
  33.2 11.6 %slice-start.1 = ((s8[14680064]{0:T(1024)(128)(4,1)}), s8[4194304]{0:T(1024)(128)(4,1)S(1)}, s32[]{:S(2)}) async-start(s8[14680064]{0:T(1024)(128)(4,1)} %bitcast.1), calls=%async_computation.1 | async-start | bytes 8388608
  33.2 11.6 %slice-start.4 = ((s8[14680064]{0:T(1024)(128)(4,1)}), s8[2097152]{0:T(1024)(128)(4,1)S(1)}, s32[]{:S(2)}) async-start(s8[14680064]{0:T(1024)(128)(4,1)} %bitcast.3), calls=%async_computation.4 | async-start | bytes 4194304
  33.2 11.6 %slice-start.5 = ((s8[14680064]{0:T(1024)(128)(4,1)}), s8[4194304]{0:T(1024)(128)(4,1)S(1)}, s32[]{:S(2)}) async-start(s8[14680064]{0:T(1024)(128)(4,1)} %bitcast.3), calls=%async_computation.5 | async-start | bytes 8388608
  33.2 11.6 %slice-start.2 = ((s8[14680064]{0:T(1024)(128)(4,1)}), s8[4194304]{0:T(1024)(128)(4,1)S(1)}, s32[]{:S(2)}) async-start(s8[14680064]{0:T(1024)(128)(4,1)} %bitcast.1), calls=%async_computation.2 | async-start | bytes 8388608
  33.3 11.6 %slice-start.3 = ((s8[14680064]{0:T(1024)(128)(4,1)}), s8[2097152]{0:T(1024)(128)(4,1)S(1)}, s32[]{:S(2)}) async-start(s8[14680064]{0:T(1024)(128)(4,1)} %bitcast.1), calls=%async_computation.3 | async-start | bytes 4194304
  33.3 11.6 %slice-start.6 = ((s8[14680064]{0:T(1024)(128)(4,1)}), s8[4194304]{0:T(1024)(128)(4,1)S(1)}, s32[]{:S(2)}) async-start(s8[14680064]{0:T(1024)(128)(4,1)} %bitcast.3), calls=%async_computation.6 | async-start | bytes 8388608
  33.3 11.6 %slice-start.7 = ((s8[14680064]{0:T(1024)(128)(4,1)}), s8[4194304]{0:T(1024)(128)(4,1)S(1)}, s32[]{:S(2)}) async-start(s8[14680064]{0:T(1024)(128)(4,1)} %bitcast.3), calls=%async_computation.7 | async-start | bytes 8388608
  33.3 4.5 %collective-permute-start.7 = (bf16[8,1792]{1,0:T(8,128)(2,1)S(1)}, bf16[8,1792]{1,0:T(8,128)(2,1)S(1)}, u32[]{:S(2)}, u32[]{:S(2)}) collective-permute-start(bf16[8,1792]{1,0:T(8,128)(2,1)S(1)} %get-tuple-element.47.refs_0_), channel_id=1, source_target_pairs={{0,8},{4,12},{8,0},{12,4},{16,24},{20,28},{24,16},{28,20},{1,9},{5... | collective-permute-start | bytes 86024 | tf_op jit(solution)/shard_map/ppermute | solution.py:17
  33.4 4.8 %collective-permute-start.8 = (bf16[8,1792]{1,0:T(8,128)(2,1)S(1)}, bf16[8,1792]{1,0:T(8,128)(2,1)S(1)}, u32[]{:S(2)}, u32[]{:S(2)}) collective-permute-start(bf16[8,1792]{1,0:T(8,128)(2,1)S(1)} %get-tuple-element.47.refs_0_), channel_id=1, source_target_pairs={{0,16},{4,20},{8,24},{12,28},{16,0},{20,4},{24,8},{28,12},{1,17},{... | collective-permute-start | bytes 86024 | tf_op jit(solution)/shard_map/ppermute | solution.py:17
  34.3 5.7 %collective-permute-start.9 = (bf16[8,1792]{1,0:T(8,128)(2,1)S(1)}, bf16[8,1792]{1,0:T(8,128)(2,1)S(1)}, u32[]{:S(2)}, u32[]{:S(2)}) collective-permute-start(bf16[8,1792]{1,0:T(8,128)(2,1)S(1)} %get-tuple-element.47.refs_0_), channel_id=1, source_target_pairs={{0,24},{4,28},{8,16},{12,20},{16,8},{20,12},{24,0},{28,4},{1,25},{... | collective-permute-start | bytes 86024 | tf_op jit(solution)/shard_map/ppermute | solution.py:17
  39.9 4.9 %collective-permute-start.10 = (bf16[32,1792]{1,0:T(8,128)(2,1)S(1)}, bf16[32,1792]{1,0:T(8,128)(2,1)S(1)}, u32[]{:S(2)}, u32[]{:S(2)}) collective-permute-start(bf16[32,1792]{1,0:T(8,128)(2,1)S(1)} %gather.1.refs_1_), channel_id=1, source_target_pairs={{0,4},{4,0},{8,12},{12,8},{16,20},{20,16},{24,28},{28,24},{1,5},{5... | collective-permute-start | bytes 344072 | tf_op jit(solution)/shard_map/ppermute | solution.py:17
  46.3 1.9 %collective-permute-start.14 = (bf16[2,32,1024]{2,1,0:T(8,128)(2,1)S(1)}, bf16[2,32,1024]{2,1,0:T(8,128)(2,1)S(1)}, u32[]{:S(2)}, u32[]{:S(2)}) collective-permute-start(bf16[2,32,1024]{2,1,0:T(8,128)(2,1)S(1)} %get-tuple-element.52), channel_id=1, source_target_pairs={{0,1},{1,0},{2,3},{3,2},{4,5},{5,4},{6,7},{7,6},{8,9},{9,8},{10,11... | collective-permute-start | bytes 393224 | tf_op jit(solution)/shard_map/ppermute | solution.py:17
  47.8 3.4 %collective-permute-start.11 = (bf16[2,32,1024]{2,1,0:T(8,128)(2,1)S(1)}, bf16[2,32,1024]{2,1,0:T(8,128)(2,1)S(1)}, u32[]{:S(2)}, u32[]{:S(2)}) collective-permute-start(bf16[2,32,1024]{2,1,0:T(8,128)(2,1)S(1)} %other_half.3), channel_id=1, source_target_pairs={{0,1},{1,0},{2,3},{3,2},{4,5},{5,4},{6,7},{7,6},{8,9},{9,8},{10,11... | collective-permute-start | bytes 393224 | tf_op jit(solution)/shard_map/ppermute | solution.py:17
  49.6 5.6 %collective-permute-start.15 = (bf16[2,32,1024]{2,1,0:T(8,128)(2,1)S(1)}, bf16[2,32,1024]{2,1,0:T(8,128)(2,1)S(1)}, u32[]{:S(2)}, u32[]{:S(2)}) collective-permute-start(bf16[2,32,1024]{2,1,0:T(8,128)(2,1)S(1)} %get-tuple-element.54), channel_id=1, source_target_pairs={{0,2},{1,3},{2,0},{3,1},{4,6},{5,7},{6,4},{7,5},{8,10},{9,11},{10,... | collective-permute-start | bytes 393224 | tf_op jit(solution)/shard_map/ppermute | solution.py:17
  51.2 13.7 %slice-start.8 = ((s8[14680064]{0:T(1024)(128)(4,1)}), s8[4194304]{0:T(1024)(128)(4,1)S(1)}, s32[]{:S(2)}) async-start(s8[14680064]{0:T(1024)(128)(4,1)} %bitcast.5), calls=%async_computation.8 | async-start | bytes 8388608
  51.2 13.7 %slice-start.9 = ((s8[14680064]{0:T(1024)(128)(4,1)}), s8[4194304]{0:T(1024)(128)(4,1)S(1)}, s32[]{:S(2)}) async-start(s8[14680064]{0:T(1024)(128)(4,1)} %bitcast.5), calls=%async_computation.9 | async-start | bytes 8388608
  51.2 13.7 %slice-start.10 = ((s8[14680064]{0:T(1024)(128)(4,1)}), s8[4194304]{0:T(1024)(128)(4,1)S(1)}, s32[]{:S(2)}) async-start(s8[14680064]{0:T(1024)(128)(4,1)} %bitcast.5), calls=%async_computation.10 | async-start | bytes 8388608
  52.5 5.4 %collective-permute-start.12 = (bf16[2,32,1024]{2,1,0:T(8,128)(2,1)S(1)}, bf16[2,32,1024]{2,1,0:T(8,128)(2,1)S(1)}, u32[]{:S(2)}, u32[]{:S(2)}) collective-permute-start(bf16[2,32,1024]{2,1,0:T(8,128)(2,1)S(1)} %get-tuple-element.50), channel_id=1, source_target_pairs={{0,2},{1,3},{2,0},{3,1},{4,6},{5,7},{6,4},{7,5},{8,10},{9,11},{10,... | collective-permute-start | bytes 393224 | tf_op jit(solution)/shard_map/ppermute | solution.py:17
  55.3 2.8 %collective-permute-start.16 = (bf16[2,32,512]{2,1,0:T(8,128)(2,1)S(1)}, bf16[2,32,512]{2,1,0:T(8,128)(2,1)S(1)}, u32[]{:S(2)}, u32[]{:S(2)}) collective-permute-start(bf16[2,32,512]{2,1,0:T(8,128)(2,1)S(1)} %act.3.refs_0_), channel_id=1, source_target_pairs={{0,1},{1,0},{2,3},{3,2},{4,5},{5,4},{6,7},{7,6},{8,9},{9,8},{10,11... | collective-permute-start | bytes 196616 | tf_op jit(solution)/shard_map/ppermute | solution.py:17
  58.0 6.8 %collective-permute-start.13 = (bf16[2,32,512]{2,1,0:T(8,128)(2,1)S(1)}, bf16[2,32,512]{2,1,0:T(8,128)(2,1)S(1)}, u32[]{:S(2)}, u32[]{:S(2)}) collective-permute-start(bf16[2,32,512]{2,1,0:T(8,128)(2,1)S(1)} %act.2.refs_0_), channel_id=1, source_target_pairs={{0,1},{1,0},{2,3},{3,2},{4,5},{5,4},{6,7},{7,6},{8,9},{9,8},{10,11... | collective-permute-start | bytes 196616 | tf_op jit(solution)/shard_map/ppermute | solution.py:17
  58.1 5.2 %copy-start = (bf16[4,1024,1792]{2,1,0:T(8,128)(2,1)S(1)}, bf16[4,1024,1792]{2,1,0:T(8,128)(2,1)}, u32[]{:S(2)}) copy-start(bf16[4,1024,1792]{2,1,0:T(8,128)(2,1)} %refs_2_.9) | copy-start | bytes 44040196
  63.3 1.6 %slice-start.11 = ((s8[14680064]{0:T(1024)(128)(4,1)}), s8[2097152]{0:T(1024)(128)(4,1)S(1)}, s32[]{:S(2)}) async-start(s8[14680064]{0:T(1024)(128)(4,1)} %bitcast.5), calls=%async_computation.11 | async-start | bytes 4194304
  66.5 5.6 %collective-permute-start.17 = (bf16[32,1792]{1,0:T(8,128)(2,1)S(1)}, bf16[32,1792]{1,0:T(8,128)(2,1)S(1)}, u32[]{:S(2)}, u32[]{:S(2)}) collective-permute-start(bf16[32,1792]{1,0:T(8,128)(2,1)S(1)} %get-tuple-element.56), channel_id=1, source_target_pairs={{0,4},{4,0},{8,12},{12,8},{16,20},{20,16},{24,28},{28,24},{1,5},{5... | collective-permute-start | bytes 344072 | tf_op jit(solution)/shard_map/ppermute | solution.py:17
  72.1 4.5 %collective-permute-start.18 = (bf16[8,1792]{1,0:T(8,128)(2,1)S(1)}, bf16[8,1792]{1,0:T(8,128)(2,1)S(1)}, u32[]{:S(2)}, u32[]{:S(2)}) collective-permute-start(bf16[8,1792]{1,0:T(8,128)(2,1)S(1)} %get-tuple-element.58), channel_id=1, source_target_pairs={{0,8},{4,12},{8,0},{12,4},{16,24},{20,28},{24,16},{28,20},{1,9},{5... | collective-permute-start | bytes 86024 | tf_op jit(solution)/shard_map/ppermute | solution.py:17
  72.4 6.3 %collective-permute-start.19 = (bf16[8,1792]{1,0:T(8,128)(2,1)S(1)}, bf16[8,1792]{1,0:T(8,128)(2,1)S(1)}, u32[]{:S(2)}, u32[]{:S(2)}) collective-permute-start(bf16[8,1792]{1,0:T(8,128)(2,1)S(1)} %get-tuple-element.59), channel_id=1, source_target_pairs={{0,16},{4,20},{8,24},{12,28},{16,0},{20,4},{24,8},{28,12},{1,17},{... | collective-permute-start | bytes 86024 | tf_op jit(solution)/shard_map/ppermute | solution.py:17
  76.3 5.7 %collective-permute-start.20 = (bf16[8,1792]{1,0:T(8,128)(2,1)S(1)}, bf16[8,1792]{1,0:T(8,128)(2,1)S(1)}, u32[]{:S(2)}, u32[]{:S(2)}) collective-permute-start(bf16[8,1792]{1,0:T(8,128)(2,1)S(1)} %get-tuple-element.60), channel_id=1, source_target_pairs={{0,24},{4,28},{8,16},{12,20},{16,8},{20,12},{24,0},{28,4},{1,25},{... | collective-permute-start | bytes 86024 | tf_op jit(solution)/shard_map/ppermute | solution.py:17

commit v3 on v2

v3 whole, which is shorter than its diff:
```python
import jax
import jax.numpy as jnp
from jax import lax
from jax.experimental import pallas as pl
from jax.experimental.pallas import tpu as pltpu
from jax.sharding import PartitionSpec as P

CAP = 4
LANES = 128
route_factor = 2.5
F32 = jnp.float32
BF16 = jnp.bfloat16
VMEM = pltpu.VMEM


def swap(x, axis, bits):
    return lax.ppermute(x, axis, [(a, a ^ bits) for a in range(lax.axis_size(axis))])


def far_first(axis):
    return range(lax.axis_size(axis) // 2 - 1, 0, -1)


def spread(x, axis):
    return [swap(x, axis, 2 * s) for s in far_first(axis)]


def scatter(parts, axis):
    return [swap(parts[s - 1], axis, 2 * s) for s in far_first(axis)]


def run(name, body, outs, ins, scratch=(), us=1.0, limit=3, hbm=(), after=()):
    n_ins, n_after = len(ins), len(after)
    ins = [
        pltpu.with_memory_space_constraint(a, pltpu.HBM) if i in hbm else a
        for i, a in enumerate(ins)
    ]

    def ordered(*refs):
        return body(*refs[:n_ins], *refs[n_ins + n_after :])

    return pl.pallas_call(
        ordered,
        out_shape=[jax.ShapeDtypeStruct(s, d) for s, d in outs],
        in_specs=[
            pl.BlockSpec(memory_space=pltpu.HBM if i in hbm else VMEM) for i in range(n_ins)
        ]
        + [pl.BlockSpec(memory_space=pl.ANY)] * n_after,
        out_specs=[pl.BlockSpec(memory_space=VMEM) for _ in outs],
        scratch_shapes=list(scratch),
        cost_estimate=pl.CostEstimate(
            flops=int(us * 1.15e9), bytes_accessed=1024, transcendentals=0
        ),
        compiler_params=pltpu.CompilerParams(vmem_limit_bytes=limit << 20),
        name=name,
    )(*ins, *after)


def split3(x):
    hi = x.astype(BF16).astype(F32)
    mid = (x - hi).astype(BF16).astype(F32)
    return hi, mid, x - hi - mid


def pack_lse(x, heads):
    hi, mid, lo = split3(x)
    return (hi + pltpu.roll(mid, heads, 1) + pltpu.roll(lo, 2 * heads, 1)).astype(BF16)


def unpack_lse(x, heads):
    x = x.astype(F32)
    x = x + pltpu.roll(x, LANES - heads, 1) + pltpu.roll(x, LANES - 2 * heads, 1)
    lane = lax.broadcasted_iota(jnp.int32, x.shape, 1)
    return jnp.where(lane < heads, x, 0.0)


def attend_body(qn_h, qr_h, wuk_h, wuv_h, prompt_h, keep, send, qn, qr, wuk, wuv, prompt, rows_scr, sems):
    rows, heads, nope = qn.shape
    lat, vdim = wuk.shape[2], wuv.shape[2]
    half, width = rows // 2, heads * vdim
    group = min(4, heads)
    steps = heads // group
    core = lax.axis_index("grp") & 1
    copies = [
        pltpu.make_async_copy(qn_h, qn, sems.at[0]),
        pltpu.make_async_copy(qr_h, qr, sems.at[1]),
        pltpu.make_async_copy(prompt_h, prompt, sems.at[2]),
    ]
    uk = [
        pltpu.make_async_copy(
            wuk_h.at[pl.ds(c * group, group)], wuk.at[pl.ds(c * group, group)], sems.at[3 + c]
        )
        for c in range(steps)
    ]
    uv = [
        pltpu.make_async_copy(
            wuv_h.at[pl.ds(c * group, group)], wuv.at[pl.ds(c * group, group)], sems.at[3 + steps + c]
        )
        for c in range(steps)
    ]
    copies[0].start()
    uk[0].start()
    copies[1].start()
    copies[2].start()
    for c in range(steps):
        if c:
            uk[c].start()
        uv[c].start()
    scale = (nope + qr.shape[2]) ** (-0.5)
    copies[0].wait()
    queries = jnp.swapaxes(qn[...], 0, 1)
    copies[1].wait()
    turned = jnp.swapaxes(qr[...], 0, 1)
    lane = lax.broadcasted_iota(jnp.int32, (rows, LANES), 1)
    lse = jnp.zeros((rows, LANES), F32)
    for c in range(steps):
        own = range(c * group, (c + 1) * group)
        uk[c].wait()
        q = jnp.concatenate(
            [jnp.dot(queries[h], wuk[h], preferred_element_type=F32).astype(BF16) for h in own], 0
        )
        r = jnp.concatenate([turned[h] for h in own], 0)
        if c == 0:
            copies[2].wait()
        s = jnp.dot(q, prompt[:lat], preferred_element_type=F32)
        s = (s + jnp.dot(r, prompt[lat:], preferred_element_type=F32)) * scale
        top = jnp.max(s, -1, keepdims=True)
        p = jnp.exp(s - top)
        total = jnp.sum(p, -1, keepdims=True)
        w = lax.dot_general(
            p.astype(BF16), prompt[:lat], (((1,), (1,)), ((), ())), preferred_element_type=F32
        )
        w = w * (1.0 / total)
        hi = w.astype(BF16)
        lo = (w - hi.astype(F32)).astype(BF16)
        part = top + jnp.log(total)
        uv[c].wait()
        for i, h in enumerate(own):
            at = slice(i * rows, (i + 1) * rows)
            v = jnp.dot(jnp.concatenate([hi[at], lo[at]], 0), wuv[h], preferred_element_type=F32)
            rows_scr[:, h * vdim : (h + 1) * vdim] = v[:rows] + v[rows:]
            lse = jnp.where(lane == h, part[at], lse)
    rows_scr[:, width:] = lse
    keep[...] = rows_scr[pl.ds(pl.multiple_of(core * half, half), half)]
    out = rows_scr[pl.ds(pl.multiple_of((1 - core) * half, half), half)]
    send[:, :width] = out[:, :width].astype(BF16)
    send[:, width:] = pack_lse(out[:, width:], heads)


def merge_values(heads, own, others):
    width = own.shape[1] - LANES
    vdim = width // heads
    levels = [own[:, width:]] + [unpack_lse(o[:, width:], heads) for o in others]
    top = levels[0]
    for x in levels[1:]:
        top = jnp.maximum(top, x)
    raised = [jnp.exp(x - top) for x in levels]
    total = sum(raised)
    shares = [x / total for x in raised]
    cols = []
    for h in range(heads):
        at = slice(h * vdim, (h + 1) * vdim)
        v = own[:, at] * shares[0][:, h : h + 1]
        for share, o in zip(shares[1:], others):
            v = v + o[:, at].astype(F32) * share[:, h : h + 1]
        cols.append(v)
    lane = lax.broadcasted_iota(jnp.int32, top.shape, 1)
    return cols, jnp.where(lane < heads, top + jnp.log(total), 0.0)


def pair_body(heads, own, other, keep, send):
    width = own.shape[1] - LANES
    vdim = width // heads
    cols, lse = merge_values(heads, own, [other])
    for h, v in enumerate(cols):
        keep[:, h * vdim : (h + 1) * vdim] = v
        send[:, h * vdim : (h + 1) * vdim] = v.astype(BF16)
    keep[:, width:] = lse
    send[:, width:] = pack_lse(lse, heads)


def final_body(heads, own, *refs):
    out = refs[-1]
    vdim = (own.shape[1] - LANES) // heads
    cols, _ = merge_values(heads, own, refs[:-1])
    for h, v in enumerate(cols):
        out[:, h * vdim : (h + 1) * vdim] = v.astype(BF16)


def project_body(mine, other, routes, scores, w, keep, *refs):
    *sends, info, att, res, pad = refs
    half = mine.shape[0]
    width = w.shape[1]
    tail = sends[0].shape[1] - LANES
    count, top = routes.shape
    core = lax.axis_index("grp") & 1
    ctx = lax.axis_index("ctx")
    att[pl.ds(pl.multiple_of(core * half, half), half)] = mine[...]
    att[pl.ds(pl.multiple_of((1 - core) * half, half), half)] = other[...]
    res[...] = jnp.dot(att[...], w[...], preferred_element_type=F32)

    def block(turn, s):
        owner = ctx ^ (2 * s + turn)
        return res[pl.ds(pl.multiple_of(owner * count, count), count)]

    v = scores[...]
    v = route_factor * v / jnp.sum(v, -1, keepdims=True)
    hi, mid, lo = split3(v)
    pad[...] = jnp.zeros_like(pad)
    for i, x in enumerate((routes[...].astype(F32), hi, mid, lo)):
        pad[:count, i * top : (i + 1) * top] = x
    info[...] = pad[:count]
    wide = pad[...].astype(BF16)
    for s, send in enumerate(sends, 1):
        send[:, :width] = jnp.concatenate([block(0, s), block(1, s)], 0).astype(BF16)
        if tail > width:
            send[:, width:tail] = jnp.zeros((2 * count, tail - width), BF16)
        send[:, tail:] = wide
    keep[:count] = block(0, 0)
    keep[count:] = block(1, 0)


def rest_sum_body(distances, keep, residual, info, *refs):
    *others, own, send = refs
    count = residual.shape[0]
    width = own.shape[1]
    tail = others[0].shape[1] - LANES
    x = keep[...]
    for o in others:
        x = x + o[:, :width].astype(F32)
    own[:count] = x[:count] + residual[...].astype(F32)
    own[count:] = x[count:]
    send[:, :width] = own[...].astype(BF16)
    if tail > width:
        send[:, width:tail] = jnp.zeros((2 * count, tail - width), BF16)
    per = LANES // 32
    tables = {s: o[:, tail:].astype(F32) for s, o in zip(distances, others)}
    tables[0] = jnp.concatenate([info[...], jnp.zeros_like(info)], 0)
    for i in range((len(tables) + per - 1) // per):
        v = tables[i * per]
        for j in range(1, per):
            if i * per + j in tables:
                v = v + pltpu.roll(tables[i * per + j], 32 * j, 1)
        send[:, tail + i * LANES : tail + (i + 1) * LANES] = v.astype(BF16)


def hidden_body(own, other, hidden, moe):
    count, width = hidden.shape
    o = other[:, :width].astype(F32)
    x = own[...] + jnp.concatenate([o[count:], o[:count]], 0)
    hidden[...] = x[:count]
    moe[...] = x.astype(BF16)


def route_body(local_experts, top, width, mine, other, *refs):
    pick, mix = refs
    count = mine.shape[0] // 2
    far = lax.axis_size("ctx") // 2
    ctx = lax.axis_index("ctx")
    blocks = []
    per = LANES // 32
    for s in range(far):
        at = slice(width + s // per * LANES, width + (s // per + 1) * LANES)
        for ref in (mine, other):
            v = ref[:, at].astype(F32)[:count]
            blocks.append(pltpu.roll(v, (LANES - s % per * 32) % LANES, 1) if s % per else v)
    table = jnp.concatenate(blocks, 0)
    rows = table.shape[0]
    weights = (
        pltpu.roll(table, LANES - top, 1)
        + pltpu.roll(table, LANES - 2 * top, 1)
        + pltpu.roll(table, LANES - 3 * top, 1)
    )
    lane = lax.broadcasted_iota(jnp.int32, (rows, LANES), 1)
    hits, gains = [], []
    all_hits = jnp.zeros((rows, LANES), F32)
    for e in range(local_experts):
        named = (table == (ctx * local_experts + e).astype(F32)) & (lane < top)
        hit = jnp.sum(jnp.where(named, 1.0, 0.0), -1, keepdims=True)
        gains.append(jnp.sum(jnp.where(named, weights, 0.0), -1, keepdims=True))
        hits.append(hit)
        all_hits = jnp.where(lane == e, hit, all_hits)
    a = lax.broadcasted_iota(jnp.int32, (rows, rows), 0)
    b = lax.broadcasted_iota(jnp.int32, (rows, rows), 1)
    earlier = jnp.where((a // count == b // count) & (b < a), 1.0, 0.0).astype(BF16)
    rank = jnp.dot(earlier, all_hits.astype(BF16), preferred_element_type=F32)
    slots = mix.shape[1]
    cap = slots // local_experts
    wide = lax.broadcasted_iota(jnp.int32, (rows, slots), 1)
    start = lax.broadcasted_iota(jnp.int32, (rows, 1), 0) // count * CAP
    chosen = jnp.zeros((rows, slots), F32)
    gain = jnp.zeros((rows, slots), F32)
    for e in range(local_experts):
        slot = rank[:, e : e + 1].astype(jnp.int32) + start + e * cap
        at = (wide == slot) & (hits[e] > 0.5)
        chosen = jnp.where(at, 1.0, chosen)
        gain = jnp.where(at, gains[e], gain)
    pick[...] = jnp.transpose(chosen).astype(BF16)
    mix[...] = gain


def half_cols(hid, mine):
    core = lax.axis_index("grp") & 1
    return pl.ds(pl.multiple_of((core if mine else 1 - core) * hid, hid), hid)


def half_products(experts, mine, x, gate, up, out):
    hid = out.shape[2] // 2
    cap = out.shape[1]
    cols = half_cols(hid, mine)
    for i, e in enumerate(experts):
        xe = x[e * cap : (e + 1) * cap]
        for j, w in enumerate((gate, up)):
            v = jnp.dot(xe, w[e, :, cols], preferred_element_type=F32)
            out[i, :, j * hid : (j + 1) * hid] = v.astype(out.dtype)


def first_half_body(experts, pick, gate, up, *refs):
    *parts, x, send = refs
    rows = jnp.concatenate([p[...] for p in parts], 0)
    x[...] = jnp.dot(pick[...], rows, preferred_element_type=F32).astype(BF16)
    half_products(experts, False, x, gate, up, send)


def half_body(experts, mine, x, gate, up, out):
    half_products(experts, mine, x, gate, up, out)


def add_body(experts, x, other, keep, send):
    for i, e in enumerate(experts):
        v = x[i] + other[e].astype(F32)
        keep[i] = v
        send[i] = v.astype(BF16)


def act_body(keep, *refs):
    *others, out = refs
    hid = out.shape[2]
    for i in range(out.shape[0]):
        x = keep[i]
        for o in others:
            x = x + o[i].astype(F32)
        gate, up = x[:, :hid], x[:, hid:]
        out[i] = (gate / (1.0 + jnp.exp(-gate)) * up).astype(BF16)


def weigh(experts, cap, mix, parts):
    result = jnp.concatenate([v.astype(BF16) for v in parts], 0)
    gain = mix[:, experts[0] * cap : (experts[-1] + 1) * cap]
    hi = gain.astype(BF16)
    lo = (gain - hi.astype(F32)).astype(BF16)
    v = jnp.dot(hi, result, preferred_element_type=F32)
    return v + jnp.dot(lo, result, preferred_element_type=F32)


def down_body(experts, mine, other, down, mix, out):
    hid = mine.shape[2]
    low, high = half_cols(hid, True), half_cols(hid, False)
    parts = []
    for i, e in enumerate(experts):
        v = jnp.dot(mine[i], down[e, low], preferred_element_type=F32)
        parts.append(v + jnp.dot(other[i], down[e, high], preferred_element_type=F32))
    out[...] = weigh(experts, mine.shape[1], mix, parts)


def down_mine_body(experts, mine, down, out):
    low = half_cols(mine.shape[2], True)
    for i, e in enumerate(experts):
        out[i] = jnp.dot(mine[i], down[e, low], preferred_element_type=F32)


def down_last_body(has_before, experts, part, other, down, mix, *refs):
    high = half_cols(other.shape[2], False)
    parts = [
        part[i] + jnp.dot(other[i], down[e, high], preferred_element_type=F32)
        for i, e in enumerate(experts)
    ]
    v = weigh(experts, other.shape[1], mix, parts)
    if has_before:
        v = v + refs[0][...]
        refs = refs[1:]
    keep, *sends = refs
    n = keep.shape[0]
    keep[...] = v[:n]
    for s, send in enumerate(sends, 1):
        send[...] = v[s * n : (s + 1) * n].astype(BF16)


def last_sum_body(keep, *refs):
    *others, own, send = refs
    count = own.shape[0]
    x = keep[...]
    for o in others:
        x = x + o[...].astype(F32)
    own[...] = x[:count]
    send[...] = x[count:].astype(BF16)


def out_body(hidden, own, other, out):
    out[...] = (hidden[...] + own[...] + other[...].astype(F32)).astype(BF16)


def bind(body, *first):
    def bound(*refs):
        return body(*first, *refs)

    return bound


def per_device(
    q_nope, q_rope, w_uk, w_uv, prompt, w_out, residual, routes, route_scores,
    expert_gate, expert_up, expert_down,
):
    rows, heads, nope = q_nope.shape
    lat, vdim = w_uk.shape[2], w_uv.shape[2]
    n_grp, n_ctx = lax.axis_size("grp"), lax.axis_size("ctx")
    count, width = residual.shape
    top = routes.shape[1]
    experts, _, ff = expert_gate.shape
    cap = CAP * n_ctx
    hid = ff // 2
    half = rows // 2
    hv = heads * vdim
    tail = -(-width // LANES) * LANES
    far = n_ctx // 2
    in_vmem = lambda a: pltpu.with_memory_space_constraint(a, VMEM)

    keys = prompt.T
    keep, send = run(
        "attend", attend_body, [((half, hv + LANES), F32), ((half, hv + LANES), BF16)],
        [q_nope, q_rope, w_uk, w_uv, keys],
        scratch=[
            VMEM(q_nope.shape, BF16), VMEM(q_rope.shape, BF16), VMEM(w_uk.shape, BF16),
            VMEM(w_uv.shape, BF16), VMEM(keys.shape, BF16), VMEM((rows, hv + LANES), F32),
            pltpu.SemaphoreType.DMA((3 + 2 * (heads // min(4, heads)),)),
        ],
        us=12, limit=10, hbm=range(5),
    )
    keep, send = run(
        "pair", bind(pair_body, heads), [((half, hv + LANES), F32), ((half, hv + LANES), BF16)],
        [keep, swap(send, "grp", 1)], us=1,
    )
    (mine,) = run(
        "merge", bind(final_body, heads), [((half, hv), BF16)], [keep] + spread(send, "grp"), us=1
    )
    pair = 2 * count
    keep, *sends, info = run(
        "project", project_body,
        [((pair, width), F32)] + [((pair, tail + LANES), BF16)] * (far - 1) + [((count, LANES), F32)],
        [mine, swap(mine, "grp", 1), routes, route_scores, in_vmem(w_out)],
        scratch=[VMEM((rows, hv), BF16), VMEM((rows, width), F32), VMEM((pair, LANES), F32)], us=1,
    )
    wide = -(-32 * far // LANES) * LANES
    own, send = run(
        "rest_sum", bind(rest_sum_body, list(far_first("ctx"))),
        [((pair, width), F32), ((pair, tail + wide), BF16)],
        [keep, residual, info] + scatter(sends, "ctx"), us=1,
    )
    other = swap(send, "ctx", 1)
    hidden, moe = run(
        "hidden", hidden_body, [((count, width), F32), ((pair, width), BF16)], [own, other], us=1
    )
    parts = dict(zip(far_first("ctx"), spread(moe, "ctx")))
    parts[0] = moe
    pick, mix = run(
        "route", bind(route_body, experts, top, tail),
        [((experts * cap, rows), BF16), ((rows, experts * cap), F32)], [send, other], us=0.5,
    )
    gate, up, down = in_vmem(expert_gate), in_vmem(expert_up), in_vmem(expert_down)
    size = max(1, experts // 2)
    groups = [range(i, i + size) for i in range(0, experts, size)]
    shape = (size, cap, 2 * hid)
    whole = (experts, cap, 2 * hid)
    x, send = run(
        "other_half", bind(first_half_body, range(experts)),
        [((experts * cap, width), BF16), (whole, BF16)],
        [pick, gate, up] + [parts[s] for s in range(far)], us=0.5,
    )
    other = swap(send, "grp", 1)
    sums = []
    for g in groups:
        (part,) = run(
            "own_half", bind(half_body, g, True), [(shape, F32)], [x, gate, up], us=0.5 if sums else 0.5,
            after=[sums[-1][0] if sums else send],
        )
        keep, send = run(
            "add", bind(add_body, g), [(shape, F32), (shape, BF16)], [part, other], us=0.1
        )
        sums.append((keep, spread(send, "grp")))
    before = []
    for g, (keep, others) in zip(groups, sums):
        (act,) = run(
            "act", act_body, [((size, cap, hid), BF16)], [keep] + others, us=5, after=before if before else [sums[-1][0]]
        )
        other = swap(act, "grp", 1)
        if g is not groups[-1]:
            before = list(run(
                "down", bind(down_body, g), [((rows, width), F32)], [act, other, down, mix], us=0.5
            ))
        else:
            (part,) = run(
                "down_mine", bind(down_mine_body, g), [((size, cap, width), F32)], [act, down], us=0.5
            )
            keep, *sends = run(
                "down_last", bind(down_last_body, len(before), g),
                [((pair, width), F32)] + [((pair, width), BF16)] * (far - 1),
                [part, other, down, mix] + before, us=5,
            )
    own, send = run(
        "last_sum", last_sum_body, [((count, width), F32), ((count, width), BF16)],
        [keep] + scatter(sends, "ctx"), us=3,
    )
    (out,) = run(
        "out", out_body, [((count, width), BF16)], [hidden, own, swap(send, "ctx", 1)], us=1
    )
    return out


def solution(mesh):
    in_specs = (
        P(None, "ctx", None),
        P(None, "ctx", None),
        P("ctx", None, None),
        P("ctx", None, None),
        P("grp", None),
        P("ctx", "grp"),
        P("ctx", "grp"),
        P("ctx", None),
        P("ctx", None),
        P("ctx", "grp", None),
        P("ctx", "grp", None),
        P("ctx", None, "grp"),
    )
    return jax.shard_map(
        per_device, mesh=mesh, in_specs=in_specs, out_specs=P("ctx", "grp"), check_vma=False
    )
```

time: 82.7 us -> 68.4 us (0.83)
  waiting for transfers between devices: 34.5 us -> 27.2 us
  local copies, waits for them, and re-layouts: 5.37 us -> 0.35 us
  starting transfers between devices: 24.6 us -> 22.4 us
    ppermute x21 -> x19, waiting for transfers between devices: 34.5 us -> 27.2 us  [swap(): lax.ppermute(x, axis, [(a, a ^ bits) for a in range(lax.axis_size(axis))])]
    unnamed x36 -> x32, local copies, waits for them, and re-layouts: 5.37 us -> 0.35 us
    ppermute x21 -> x19, starting transfers between devices: 24.6 us -> 22.4 us  [swap(): lax.ppermute(x, axis, [(a, a ^ bits) for a in range(lax.axis_size(axis))])]
    pallas_call x18 -> x19, Pallas kernels: 17.8 us -> 18 us  [run(): pl.pallas_call(ordered, out_shape=[jax.ShapeDtypeStruct(s, d) for s, d in...]
  transfers between devices with their start and end apart: 21 -> 19, of which waited for: 14 -> 15; matrix products, arithmetic and copies ran while one was open for 0% -> 0% of each run, Pallas kernels for 8% -> 8%
where the time goes in v3:
time: 68.4 us; the launch traced here: 68.2 us
  waiting for transfers between devices  27.2 us (40%)
  starting transfers between devices  22.4 us (33%)
  Pallas kernels  18 us (26%)
    ppermute x19, waiting for transfers between devices, swap(): lax.ppermute(x, axis, [(a, a ^ bits) for a in range(lax.axis_size(axis))])  27.2 us
    ppermute x19, starting transfers between devices, swap(): lax.ppermute(x, axis, [(a, a ^ bits) for a in range(lax.axis_size(axis))])  22.4 us
    pallas_call x19, Pallas kernels, run(): pl.pallas_call(ordered, out_shape=[jax.ShapeDtypeStruct(s, d) for s, d in...  18 us
  transfers between devices with their start and end apart: 19, of which 15 were waited for; matrix products, arithmetic and copies ran while one was open for 0% of the time, Pallas kernels for 8%

profile of v3, /device:TPU:0, one launch (start us, length us, event | category | flops | bytes accessed | tf_op | source)
XLA Modules:
  0.0 68.2 jit_solution(14864863838639546588)
XLA Ops:
  0.0 0.0 slice-start.2
  0.0 0.0 slice-start.4
  0.0 0.0 slice-start.5
  0.1 0.0 slice-start.6
  0.1 5.7 %attend.1 = (f32[32,2176]{1,0:T(8,128)S(1)}, bf16[32,2176]{1,0:T(8,128)(2,1)S(1)}) custom-call(bf16[64,16,128]{2,1,0:T(8,128)(2,1)} %refs_0_.1, bf16[64,16,64]{2,1,0:T(8,128)(2,1)} %refs_1_.6, bf16[16,128,512]{2,1,0:T(8,128)(2,1)} %refs_2_.7, bf16[16,512,128]{2,1,0:T(8,128)(2,1)} %refs_3_.2, bf16[576,384]{1,0:T(8,128)(2,1)} %bitcast.7), custom_call_target="tpu_custom_call" | custom-call | flops 13799999488 | bytes 1024 | tf_op jit(solution)/shard_map/attend/pallas_call | solution.py:42
  5.8 0.0 copy-start.3
  5.8 0.5 collective-permute-start
  6.4 1.0 %collective-permute-done.refs_1_ = bf16[32,2176]{1,0:T(8,128)(2,1)S(1)} collective-permute-done((bf16[32,2176]{1,0:T(8,128)(2,1)S(1)}, bf16[32,2176]{1,0:T(8,128)(2,1)S(1)}, u32[]{:S(2)}, u32[]{:S(2)}) %collective-permute-start) | collective-permute-done | bytes 139296 | tf_op jit(solution)/shard_map/ppermute | solution.py:17
  7.4 0.3 pair.1
  7.7 2.9 %collective-permute-start.1 = (bf16[32,2176]{1,0:T(8,128)(2,1)S(1)}, bf16[32,2176]{1,0:T(8,128)(2,1)S(1)}, u32[]{:S(2)}, u32[]{:S(2)}) collective-permute-start(bf16[32,2176]{1,0:T(8,128)(2,1)S(1)} %get-tuple-element.35), channel_id=1, source_target_pairs={{0,2},{1,3},{2,0},{3,1},{4,6},{5,7},{6,4},{7,5},{8,10},{9,11},{10,... | collective-permute-start | bytes 417800 | tf_op jit(solution)/shard_map/ppermute | solution.py:17
  10.6 4.0 %collective-permute-done.1.refs_1_ = bf16[32,2176]{1,0:T(8,128)(2,1)S(1)} collective-permute-done((bf16[32,2176]{1,0:T(8,128)(2,1)S(1)}, bf16[32,2176]{1,0:T(8,128)(2,1)S(1)}, u32[]{:S(2)}, u32[]{:S(2)}) %collective-permute-start.1) | collective-permute-done | bytes 139296 | tf_op jit(solution)/shard_map/ppermute | solution.py:17
  14.6 0.3 merge.1.refs_0_
  14.9 0.1 collective-permute-start.2
  15.0 1.3 %collective-permute-done.2.refs_1_ = bf16[32,2048]{1,0:T(8,128)(2,1)S(1)} collective-permute-done((bf16[32,2048]{1,0:T(8,128)(2,1)S(1)}, bf16[32,2048]{1,0:T(8,128)(2,1)S(1)}, u32[]{:S(2)}, u32[]{:S(2)}) %collective-permute-start.2) | collective-permute-done | bytes 131104 | tf_op jit(solution)/shard_map/ppermute | solution.py:17
  16.3 0.0 copy-done
  16.3 0.0 copy-done.1
  16.3 1.4 %project.1 = (f32[16,1792]{1,0:T(8,128)S(1)}, bf16[16,1920]{1,0:T(8,128)(2,1)S(1)}, bf16[16,1920]{1,0:T(8,128)(2,1)S(1)}, bf16[16,1920]{1,0:T(8,128)(2,1)S(1)}, f32[8,128]{1,0:T(8,128)S(1)}) custom-call(bf16[32,2048]{1,0:T(8,128)(2,1)S(1)} %merge.1.refs_0_, bf16[32,2048]{1,0:T(8,128)(2,1)S(1)} %collective-permute-done.2.refs_1_, s32[8,8]{1,0:T(8,128)S(1)} %copy-done.1, ...), custom_call_target="tpu_custom_call" | custom-call | flops 1150000000 | bytes 1024 | tf_op jit(solution)/shard_map/project/pallas_call | solution.py:42
  17.8 3.9 %collective-permute-start.3 = (bf16[16,1920]{1,0:T(8,128)(2,1)S(1)}, bf16[16,1920]{1,0:T(8,128)(2,1)S(1)}, u32[]{:S(2)}, u32[]{:S(2)}) collective-permute-start(bf16[16,1920]{1,0:T(8,128)(2,1)S(1)} %get-tuple-element.38), channel_id=1, source_target_pairs={{0,24},{4,28},{8,16},{12,20},{16,8},{20,12},{24,0},{28,4},{1,25},{... | collective-permute-start | bytes 184328 | tf_op jit(solution)/shard_map/ppermute | solution.py:17
  21.7 0.0 collective-permute-start.4
  21.7 0.6 collective-permute-start.5
  22.3 1.8 %collective-permute-done.3.refs_3_ = bf16[16,1920]{1,0:T(8,128)(2,1)S(1)} collective-permute-done((bf16[16,1920]{1,0:T(8,128)(2,1)S(1)}, bf16[16,1920]{1,0:T(8,128)(2,1)S(1)}, u32[]{:S(2)}, u32[]{:S(2)}) %collective-permute-start.3) | collective-permute-done | bytes 61472 | tf_op jit(solution)/shard_map/ppermute | solution.py:17
  24.1 3.1 %collective-permute-done.4.refs_4_ = bf16[16,1920]{1,0:T(8,128)(2,1)S(1)} collective-permute-done((bf16[16,1920]{1,0:T(8,128)(2,1)S(1)}, bf16[16,1920]{1,0:T(8,128)(2,1)S(1)}, u32[]{:S(2)}, u32[]{:S(2)}) %collective-permute-start.4) | collective-permute-done | bytes 61472 | tf_op jit(solution)/shard_map/ppermute | solution.py:17
  27.2 0.0 collective-permute-done.5.refs_5_
  27.2 0.1 rest_sum.1
  27.3 1.6 %collective-permute-start.6 = (bf16[16,1920]{1,0:T(8,128)(2,1)S(1)}, bf16[16,1920]{1,0:T(8,128)(2,1)S(1)}, u32[]{:S(2)}, u32[]{:S(2)}) collective-permute-start(bf16[16,1920]{1,0:T(8,128)(2,1)S(1)} %get-tuple-element.42.refs_0_), channel_id=1, source_target_pairs={{0,4},{4,0},{8,12},{12,8},{16,20},{20,16},{24,28},{28,24},{1,5},{5... | collective-permute-start | bytes 184328 | tf_op jit(solution)/shard_map/ppermute | solution.py:17
  28.9 2.7 %collective-permute-done.6.refs_1_ = bf16[16,1920]{1,0:T(8,128)(2,1)S(1)} collective-permute-done((bf16[16,1920]{1,0:T(8,128)(2,1)S(1)}, bf16[16,1920]{1,0:T(8,128)(2,1)S(1)}, u32[]{:S(2)}, u32[]{:S(2)}) %collective-permute-start.6) | collective-permute-done | bytes 61472 | tf_op jit(solution)/shard_map/ppermute | solution.py:17
  31.6 2.5 %collective-permute-start.9 = (bf16[16,1792]{1,0:T(8,128)(2,1)S(1)}, bf16[16,1792]{1,0:T(8,128)(2,1)S(1)}, u32[]{:S(2)}, u32[]{:S(2)}) collective-permute-start(bf16[16,1792]{1,0:T(8,128)(2,1)S(1)} %get-tuple-element.45.refs_3_), channel_id=1, source_target_pairs={{0,24},{4,28},{8,16},{12,20},{16,8},{20,12},{24,0},{28,4},{1,25},{... | collective-permute-start | bytes 172040 | tf_op jit(solution)/shard_map/ppermute | solution.py:17
  34.2 0.1 collective-permute-start.8
  34.3 1.8 %collective-permute-start.7 = (bf16[16,1792]{1,0:T(8,128)(2,1)S(1)}, bf16[16,1792]{1,0:T(8,128)(2,1)S(1)}, u32[]{:S(2)}, u32[]{:S(2)}) collective-permute-start(bf16[16,1792]{1,0:T(8,128)(2,1)S(1)} %get-tuple-element.45.refs_3_), channel_id=1, source_target_pairs={{0,8},{4,12},{8,0},{12,4},{16,24},{20,28},{24,16},{28,20},{1,9},{5... | collective-permute-start | bytes 172040 | tf_op jit(solution)/shard_map/ppermute | solution.py:17
  36.1 0.5 route.1
  36.6 1.4 %collective-permute-done.9.refs_6_ = bf16[16,1792]{1,0:T(8,128)(2,1)S(1)} collective-permute-done((bf16[16,1792]{1,0:T(8,128)(2,1)S(1)}, bf16[16,1792]{1,0:T(8,128)(2,1)S(1)}, u32[]{:S(2)}, u32[]{:S(2)}) %collective-permute-start.9) | collective-permute-done | bytes 57376 | tf_op jit(solution)/shard_map/ppermute | solution.py:17
  38.0 1.2 %collective-permute-done.8.refs_5_ = bf16[16,1792]{1,0:T(8,128)(2,1)S(1)} collective-permute-done((bf16[16,1792]{1,0:T(8,128)(2,1)S(1)}, bf16[16,1792]{1,0:T(8,128)(2,1)S(1)}, u32[]{:S(2)}, u32[]{:S(2)}) %collective-permute-start.8) | collective-permute-done | bytes 57376 | tf_op jit(solution)/shard_map/ppermute | solution.py:17
  39.2 0.0 collective-permute-done.7.refs_4_
  39.2 0.0 slice-done
  39.3 2.7 %other_half.1 = (bf16[128,1792]{1,0:T(8,128)(2,1)S(1)}, bf16[4,32,1024]{2,1,0:T(8,128)(2,1)S(1)}) custom-call(bf16[128,64]{1,0:T(8,128)(2,1)S(1)} %get-tuple-element.44.refs_0_, bf16[4,1792,1024]{2,1,0:T(8,128)(2,1)S(1)} %bitcast.2, bf16[4,1792,1024]{2,1,0:T(8,128)(2,1)S(1)} %bitcast.4, bf16[16,1792]{1,0:T(8,128)(2,1)S(1)} %get-tuple-element.45.refs_3_, ...), custom_call_target="tpu_custom_call" | custom-call | flops 575000000 | bytes 1024 | tf_op jit(solution)/shard_map/other_half/pallas_call | solution.py:42
  42.1 0.0 collective-permute-start.10
  42.1 1.4 %own_half.2.refs_0_ = f32[2,32,1024]{2,1,0:T(8,128)S(1)} custom-call(bf16[128,1792]{1,0:T(8,128)(2,1)S(1)} %get-tuple-element.46.refs_0_, bf16[4,1792,1024]{2,1,0:T(8,128)(2,1)S(1)} %bitcast.2, bf16[4,1792,1024]{2,1,0:T(8,128)(2,1)S(1)} %bitcast.4, bf16[4,32,1024]{2,1,0:T(8,128)(2,1)S(1)} %get-tuple-element.47.refs_3_), custom_call_target="tpu_custom_call" | custom-call | flops 575000000 | bytes 1024 | tf_op jit(solution)/shard_map/own_half/pallas_call | solution.py:42
  43.5 0.1 collective-permute-done.10.refs_1_
  43.7 1.6 %collective-permute-start.12 = (bf16[2,32,1024]{2,1,0:T(8,128)(2,1)S(1)}, bf16[2,32,1024]{2,1,0:T(8,128)(2,1)S(1)}, u32[]{:S(2)}, u32[]{:S(2)}) collective-permute-start(bf16[2,32,1024]{2,1,0:T(8,128)(2,1)S(1)} %get-tuple-element.51), channel_id=1, source_target_pairs={{0,2},{1,3},{2,0},{3,1},{4,6},{5,7},{6,4},{7,5},{8,10},{9,11},{10,... | collective-permute-start | bytes 393224 | tf_op jit(solution)/shard_map/ppermute | solution.py:17
  45.2 1.4 %own_half.3.refs_0_ = f32[2,32,1024]{2,1,0:T(8,128)S(1)} custom-call(bf16[128,1792]{1,0:T(8,128)(2,1)S(1)} %get-tuple-element.46.refs_0_, bf16[4,1792,1024]{2,1,0:T(8,128)(2,1)S(1)} %bitcast.2, bf16[4,1792,1024]{2,1,0:T(8,128)(2,1)S(1)} %bitcast.4, f32[2,32,1024]{2,1,0:T(8,128)S(1)} %get-tuple-element.48.refs_3_.refs_0_), custom_call_target="tpu_custom_call" | custom-call | flops 575000000 | bytes 1024 | tf_op jit(solution)/shard_map/own_half/pallas_call | solution.py:42
  46.6 0.6 collective-permute-start.11
  47.2 2.3 %collective-permute-done.12.refs_1_ = bf16[2,32,1024]{2,1,0:T(8,128)(2,1)S(1)} collective-permute-done((bf16[2,32,1024]{2,1,0:T(8,128)(2,1)S(1)}, bf16[2,32,1024]{2,1,0:T(8,128)(2,1)S(1)}, u32[]{:S(2)}, u32[]{:S(2)}) %collective-permute-start.12) | collective-permute-done | bytes 131104 | tf_op jit(solution)/shard_map/ppermute | solution.py:17
  49.5 0.1 act.2.refs_0_
  49.6 0.1 collective-permute-start.13
  49.7 1.2 %collective-permute-done.13.refs_1_ = bf16[2,32,512]{2,1,0:T(8,128)(2,1)S(1)} collective-permute-done((bf16[2,32,512]{2,1,0:T(8,128)(2,1)S(1)}, bf16[2,32,512]{2,1,0:T(8,128)(2,1)S(1)}, u32[]{:S(2)}, u32[]{:S(2)}) %collective-permute-start.13) | collective-permute-done | bytes 65568 | tf_op jit(solution)/shard_map/ppermute | solution.py:17
  50.9 0.0 slice-done.8
  50.9 0.0 slice-done.10
  50.9 0.3 slice-done.11
  51.2 1.6 %down.1.refs_2_.refs_4_ = f32[64,1792]{1,0:T(8,128)S(1)} custom-call(bf16[2,32,512]{2,1,0:T(8,128)(2,1)S(1)} %act.2.refs_0_, bf16[2,32,512]{2,1,0:T(8,128)(2,1)S(1)} %collective-permute-done.13.refs_1_, bf16[4,1024,1792]{2,1,0:T(8,128)(2,1)S(1)} %bitcast.6, f32[64,128]{1,0:T(8,128)S(1)} %get-tuple-element.52.refs_3_), custom_call_target="tpu_custom_call" | custom-call | flops 575000000 | bytes 1024 | tf_op jit(solution)/shard_map/down/pallas_call | solution.py:42
  52.8 0.0 collective-permute-done.11.refs_1_
  52.8 0.1 act.3.refs_0_
  52.9 0.1 collective-permute-start.14
  52.9 0.7 %down_mine.1.refs_0_ = f32[2,32,1792]{2,1,0:T(8,128)S(1)} custom-call(bf16[2,32,512]{2,1,0:T(8,128)(2,1)S(1)} %act.3.refs_0_, bf16[4,1024,1792]{2,1,0:T(8,128)(2,1)S(1)} %bitcast.6), custom_call_target="tpu_custom_call" | custom-call | flops 575000000 | bytes 1024 | tf_op jit(solution)/shard_map/down_mine/pallas_call | solution.py:42
  53.7 0.5 collective-permute-done.14.refs_1_
  54.2 1.0 %down_last.1 = (f32[16,1792]{1,0:T(8,128)S(1)}, bf16[16,1792]{1,0:T(8,128)(2,1)S(1)}, bf16[16,1792]{1,0:T(8,128)(2,1)S(1)}, bf16[16,1792]{1,0:T(8,128)(2,1)S(1)}) custom-call(f32[2,32,1792]{2,1,0:T(8,128)S(1)} %down_mine.1.refs_0_, bf16[2,32,512]{2,1,0:T(8,128)(2,1)S(1)} %collective-permute-done.14.refs_1_, bf16[4,1024,1792]{2,1,0:T(8,128)(2,1)S(1)} %bitcast.6, ...), custom_call_target="tpu_custom_call" | custom-call | flops 5750000128 | bytes 1024 | tf_op jit(solution)/shard_map/down_last/pallas_call | solution.py:42
  55.1 2.2 %collective-permute-start.15 = (bf16[16,1792]{1,0:T(8,128)(2,1)S(1)}, bf16[16,1792]{1,0:T(8,128)(2,1)S(1)}, u32[]{:S(2)}, u32[]{:S(2)}) collective-permute-start(bf16[16,1792]{1,0:T(8,128)(2,1)S(1)} %get-tuple-element.54), channel_id=1, source_target_pairs={{0,24},{4,28},{8,16},{12,20},{16,8},{20,12},{24,0},{28,4},{1,25},{... | collective-permute-start | bytes 172040 | tf_op jit(solution)/shard_map/ppermute | solution.py:17
  57.3 0.3 collective-permute-start.16
  57.7 1.9 %collective-permute-start.17 = (bf16[16,1792]{1,0:T(8,128)(2,1)S(1)}, bf16[16,1792]{1,0:T(8,128)(2,1)S(1)}, u32[]{:S(2)}, u32[]{:S(2)}) collective-permute-start(bf16[16,1792]{1,0:T(8,128)(2,1)S(1)} %get-tuple-element.56), channel_id=1, source_target_pairs={{0,8},{4,12},{8,0},{12,4},{16,24},{20,28},{24,16},{28,20},{1,9},{5... | collective-permute-start | bytes 172040 | tf_op jit(solution)/shard_map/ppermute | solution.py:17
  59.6 2.2 %collective-permute-done.15.refs_1_ = bf16[16,1792]{1,0:T(8,128)(2,1)S(1)} collective-permute-done((bf16[16,1792]{1,0:T(8,128)(2,1)S(1)}, bf16[16,1792]{1,0:T(8,128)(2,1)S(1)}, u32[]{:S(2)}, u32[]{:S(2)}) %collective-permute-start.15) | collective-permute-done | bytes 57376 | tf_op jit(solution)/shard_map/ppermute | solution.py:17
  61.8 1.8 %collective-permute-done.16.refs_2_ = bf16[16,1792]{1,0:T(8,128)(2,1)S(1)} collective-permute-done((bf16[16,1792]{1,0:T(8,128)(2,1)S(1)}, bf16[16,1792]{1,0:T(8,128)(2,1)S(1)}, u32[]{:S(2)}, u32[]{:S(2)}) %collective-permute-start.16) | collective-permute-done | bytes 57376 | tf_op jit(solution)/shard_map/ppermute | solution.py:17
  63.6 0.0 collective-permute-done.17.refs_3_
  63.7 1.6 %collective-permute-start.18 = (bf16[8,1792]{1,0:T(8,128)(2,1)S(1)}, bf16[8,1792]{1,0:T(8,128)(2,1)S(1)}, u32[]{:S(2)}, u32[]{:S(2)}) collective-permute-start(bf16[8,1792]{1,0:T(8,128)(2,1)S(1)} %get-tuple-element.58), channel_id=1, source_target_pairs={{0,4},{4,0},{8,12},{12,8},{16,20},{20,16},{24,28},{28,24},{1,5},{5... | collective-permute-start | bytes 86024 | tf_op jit(solution)/shard_map/ppermute | solution.py:17
  65.3 2.4 %collective-permute-done.18.refs_2_ = bf16[8,1792]{1,0:T(8,128)(2,1)S(1)} collective-permute-done((bf16[8,1792]{1,0:T(8,128)(2,1)S(1)}, bf16[8,1792]{1,0:T(8,128)(2,1)S(1)}, u32[]{:S(2)}, u32[]{:S(2)}) %collective-permute-start.18) | collective-permute-done | bytes 28704 | tf_op jit(solution)/shard_map/ppermute | solution.py:17
  67.6 0.6 out.1
  (28 shorter events, 0.2 us)
Async XLA Ops:
  0.0 16.3 %copy-start = (bf16[2048,1792]{1,0:T(8,128)(2,1)S(1)}, bf16[2048,1792]{1,0:T(8,128)(2,1)}, u32[]{:S(2)}) copy-start(bf16[2048,1792]{1,0:T(8,128)(2,1)} %refs_4_.1) | copy-start | bytes 22020100
  0.0 16.3 %copy-start.1 = (s32[8,8]{1,0:T(8,128)S(1)}, s32[8,8]{1,0:T(8,128)}, u32[]{:S(2)}) copy-start(s32[8,8]{1,0:T(8,128)} %refs_2_.8) | copy-start | bytes 772
  0.0 16.3 %copy-start.2 = (f32[8,8]{1,0:T(8,128)S(1)}, f32[8,8]{1,0:T(8,128)}, u32[]{:S(2)}) copy-start(f32[8,8]{1,0:T(8,128)} %refs_3_.3) | copy-start | bytes 772
  0.0 39.2 %slice-start = ((s8[14680064]{0:T(1024)(128)(4,1)}), s8[4194304]{0:T(1024)(128)(4,1)S(1)}, s32[]{:S(2)}) async-start(s8[14680064]{0:T(1024)(128)(4,1)} %bitcast.1), calls=%async_computation | async-start | bytes 8388608
  0.0 39.2 %slice-start.1 = ((s8[14680064]{0:T(1024)(128)(4,1)}), s8[4194304]{0:T(1024)(128)(4,1)S(1)}, s32[]{:S(2)}) async-start(s8[14680064]{0:T(1024)(128)(4,1)} %bitcast.1), calls=%async_computation.1 | async-start | bytes 8388608
  0.0 39.2 %slice-start.2 = ((s8[14680064]{0:T(1024)(128)(4,1)}), s8[4194304]{0:T(1024)(128)(4,1)S(1)}, s32[]{:S(2)}) async-start(s8[14680064]{0:T(1024)(128)(4,1)} %bitcast.1), calls=%async_computation.2 | async-start | bytes 8388608
  0.0 39.2 %slice-start.4 = ((s8[14680064]{0:T(1024)(128)(4,1)}), s8[4194304]{0:T(1024)(128)(4,1)S(1)}, s32[]{:S(2)}) async-start(s8[14680064]{0:T(1024)(128)(4,1)} %bitcast.3), calls=%async_computation.4 | async-start | bytes 8388608
  0.0 39.2 %slice-start.5 = ((s8[14680064]{0:T(1024)(128)(4,1)}), s8[4194304]{0:T(1024)(128)(4,1)S(1)}, s32[]{:S(2)}) async-start(s8[14680064]{0:T(1024)(128)(4,1)} %bitcast.3), calls=%async_computation.5 | async-start | bytes 8388608
  0.1 39.2 %slice-start.6 = ((s8[14680064]{0:T(1024)(128)(4,1)}), s8[4194304]{0:T(1024)(128)(4,1)S(1)}, s32[]{:S(2)}) async-start(s8[14680064]{0:T(1024)(128)(4,1)} %bitcast.3), calls=%async_computation.6 | async-start | bytes 8388608
  5.8 21.4 %copy-start.3 = (bf16[8,1792]{1,0:T(8,128)(2,1)S(1)}, bf16[8,1792]{1,0:T(8,128)(2,1)}, u32[]{:S(2)}) copy-start(bf16[8,1792]{1,0:T(8,128)(2,1)} %refs_1_.7) | copy-start | bytes 86020
  5.8 1.5 %collective-permute-start = (bf16[32,2176]{1,0:T(8,128)(2,1)S(1)}, bf16[32,2176]{1,0:T(8,128)(2,1)S(1)}, u32[]{:S(2)}, u32[]{:S(2)}) collective-permute-start(bf16[32,2176]{1,0:T(8,128)(2,1)S(1)} %get-tuple-element.33), channel_id=1, source_target_pairs={{0,1},{1,0},{2,3},{3,2},{4,5},{5,4},{6,7},{7,6},{8,9},{9,8},{10,11... | collective-permute-start | bytes 417800 | tf_op jit(solution)/shard_map/ppermute | solution.py:17
  7.7 6.9 %collective-permute-start.1 = (bf16[32,2176]{1,0:T(8,128)(2,1)S(1)}, bf16[32,2176]{1,0:T(8,128)(2,1)S(1)}, u32[]{:S(2)}, u32[]{:S(2)}) collective-permute-start(bf16[32,2176]{1,0:T(8,128)(2,1)S(1)} %get-tuple-element.35), channel_id=1, source_target_pairs={{0,2},{1,3},{2,0},{3,1},{4,6},{5,7},{6,4},{7,5},{8,10},{9,11},{10,... | collective-permute-start | bytes 417800 | tf_op jit(solution)/shard_map/ppermute | solution.py:17
  14.6 24.7 %slice-start.3 = ((s8[14680064]{0:T(1024)(128)(4,1)}), s8[2097152]{0:T(1024)(128)(4,1)S(1)}, s32[]{:S(2)}) async-start(s8[14680064]{0:T(1024)(128)(4,1)} %bitcast.1), calls=%async_computation.3 | async-start | bytes 4194304
  14.6 24.7 %slice-start.7 = ((s8[14680064]{0:T(1024)(128)(4,1)}), s8[2097152]{0:T(1024)(128)(4,1)S(1)}, s32[]{:S(2)}) async-start(s8[14680064]{0:T(1024)(128)(4,1)} %bitcast.3), calls=%async_computation.7 | async-start | bytes 4194304
  14.9 1.4 %collective-permute-start.2 = (bf16[32,2048]{1,0:T(8,128)(2,1)S(1)}, bf16[32,2048]{1,0:T(8,128)(2,1)S(1)}, u32[]{:S(2)}, u32[]{:S(2)}) collective-permute-start(bf16[32,2048]{1,0:T(8,128)(2,1)S(1)} %merge.1.refs_0_), channel_id=1, source_target_pairs={{0,1},{1,0},{2,3},{3,2},{4,5},{5,4},{6,7},{7,6},{8,9},{9,8},{10,11... | collective-permute-start | bytes 393224 | tf_op jit(solution)/shard_map/ppermute | solution.py:17
  17.8 6.4 %collective-permute-start.3 = (bf16[16,1920]{1,0:T(8,128)(2,1)S(1)}, bf16[16,1920]{1,0:T(8,128)(2,1)S(1)}, u32[]{:S(2)}, u32[]{:S(2)}) collective-permute-start(bf16[16,1920]{1,0:T(8,128)(2,1)S(1)} %get-tuple-element.38), channel_id=1, source_target_pairs={{0,24},{4,28},{8,16},{12,20},{16,8},{20,12},{24,0},{28,4},{1,25},{... | collective-permute-start | bytes 184328 | tf_op jit(solution)/shard_map/ppermute | solution.py:17
  21.7 5.6 %collective-permute-start.4 = (bf16[16,1920]{1,0:T(8,128)(2,1)S(1)}, bf16[16,1920]{1,0:T(8,128)(2,1)S(1)}, u32[]{:S(2)}, u32[]{:S(2)}) collective-permute-start(bf16[16,1920]{1,0:T(8,128)(2,1)S(1)} %get-tuple-element.39), channel_id=1, source_target_pairs={{0,16},{4,20},{8,24},{12,28},{16,0},{20,4},{24,8},{28,12},{1,17},{... | collective-permute-start | bytes 184328 | tf_op jit(solution)/shard_map/ppermute | solution.py:17
  21.7 5.6 %collective-permute-start.5 = (bf16[16,1920]{1,0:T(8,128)(2,1)S(1)}, bf16[16,1920]{1,0:T(8,128)(2,1)S(1)}, u32[]{:S(2)}, u32[]{:S(2)}) collective-permute-start(bf16[16,1920]{1,0:T(8,128)(2,1)S(1)} %get-tuple-element.40), channel_id=1, source_target_pairs={{0,8},{4,12},{8,0},{12,4},{16,24},{20,28},{24,16},{28,20},{1,9},{5... | collective-permute-start | bytes 184328 | tf_op jit(solution)/shard_map/ppermute | solution.py:17
  27.3 4.3 %collective-permute-start.6 = (bf16[16,1920]{1,0:T(8,128)(2,1)S(1)}, bf16[16,1920]{1,0:T(8,128)(2,1)S(1)}, u32[]{:S(2)}, u32[]{:S(2)}) collective-permute-start(bf16[16,1920]{1,0:T(8,128)(2,1)S(1)} %get-tuple-element.42.refs_0_), channel_id=1, source_target_pairs={{0,4},{4,0},{8,12},{12,8},{16,20},{20,16},{24,28},{28,24},{1,5},{5... | collective-permute-start | bytes 184328 | tf_op jit(solution)/shard_map/ppermute | solution.py:17
  31.6 6.4 %collective-permute-start.9 = (bf16[16,1792]{1,0:T(8,128)(2,1)S(1)}, bf16[16,1792]{1,0:T(8,128)(2,1)S(1)}, u32[]{:S(2)}, u32[]{:S(2)}) collective-permute-start(bf16[16,1792]{1,0:T(8,128)(2,1)S(1)} %get-tuple-element.45.refs_3_), channel_id=1, source_target_pairs={{0,24},{4,28},{8,16},{12,20},{16,8},{20,12},{24,0},{28,4},{1,25},{... | collective-permute-start | bytes 172040 | tf_op jit(solution)/shard_map/ppermute | solution.py:17
  34.2 5.1 %collective-permute-start.8 = (bf16[16,1792]{1,0:T(8,128)(2,1)S(1)}, bf16[16,1792]{1,0:T(8,128)(2,1)S(1)}, u32[]{:S(2)}, u32[]{:S(2)}) collective-permute-start(bf16[16,1792]{1,0:T(8,128)(2,1)S(1)} %get-tuple-element.45.refs_3_), channel_id=1, source_target_pairs={{0,16},{4,20},{8,24},{12,28},{16,0},{20,4},{24,8},{28,12},{1,17},{... | collective-permute-start | bytes 172040 | tf_op jit(solution)/shard_map/ppermute | solution.py:17
  34.3 4.9 %collective-permute-start.7 = (bf16[16,1792]{1,0:T(8,128)(2,1)S(1)}, bf16[16,1792]{1,0:T(8,128)(2,1)S(1)}, u32[]{:S(2)}, u32[]{:S(2)}) collective-permute-start(bf16[16,1792]{1,0:T(8,128)(2,1)S(1)} %get-tuple-element.45.refs_3_), channel_id=1, source_target_pairs={{0,8},{4,12},{8,0},{12,4},{16,24},{20,28},{24,16},{28,20},{1,9},{5... | collective-permute-start | bytes 172040 | tf_op jit(solution)/shard_map/ppermute | solution.py:17
  42.1 1.6 %collective-permute-start.10 = (bf16[4,32,1024]{2,1,0:T(8,128)(2,1)S(1)}, bf16[4,32,1024]{2,1,0:T(8,128)(2,1)S(1)}, u32[]{:S(2)}, u32[]{:S(2)}) collective-permute-start(bf16[4,32,1024]{2,1,0:T(8,128)(2,1)S(1)} %get-tuple-element.47.refs_3_), channel_id=1, source_target_pairs={{0,1},{1,0},{2,3},{3,2},{4,5},{5,4},{6,7},{7,6},{8,9},{9,8},{10,11... | collective-permute-start | bytes 786440 | tf_op jit(solution)/shard_map/ppermute | solution.py:17
  43.7 5.9 %collective-permute-start.12 = (bf16[2,32,1024]{2,1,0:T(8,128)(2,1)S(1)}, bf16[2,32,1024]{2,1,0:T(8,128)(2,1)S(1)}, u32[]{:S(2)}, u32[]{:S(2)}) collective-permute-start(bf16[2,32,1024]{2,1,0:T(8,128)(2,1)S(1)} %get-tuple-element.51), channel_id=1, source_target_pairs={{0,2},{1,3},{2,0},{3,1},{4,6},{5,7},{6,4},{7,5},{8,10},{9,11},{10,... | collective-permute-start | bytes 393224 | tf_op jit(solution)/shard_map/ppermute | solution.py:17
  45.2 5.7 %slice-start.8 = ((s8[14680064]{0:T(1024)(128)(4,1)}), s8[4194304]{0:T(1024)(128)(4,1)S(1)}, s32[]{:S(2)}) async-start(s8[14680064]{0:T(1024)(128)(4,1)} %bitcast.5), calls=%async_computation.8 | async-start | bytes 8388608
  45.2 5.7 %slice-start.9 = ((s8[14680064]{0:T(1024)(128)(4,1)}), s8[4194304]{0:T(1024)(128)(4,1)S(1)}, s32[]{:S(2)}) async-start(s8[14680064]{0:T(1024)(128)(4,1)} %bitcast.5), calls=%async_computation.9 | async-start | bytes 8388608
  45.2 5.7 %slice-start.10 = ((s8[14680064]{0:T(1024)(128)(4,1)}), s8[4194304]{0:T(1024)(128)(4,1)S(1)}, s32[]{:S(2)}) async-start(s8[14680064]{0:T(1024)(128)(4,1)} %bitcast.5), calls=%async_computation.10 | async-start | bytes 8388608
  46.6 6.1 %collective-permute-start.11 = (bf16[2,32,1024]{2,1,0:T(8,128)(2,1)S(1)}, bf16[2,32,1024]{2,1,0:T(8,128)(2,1)S(1)}, u32[]{:S(2)}, u32[]{:S(2)}) collective-permute-start(bf16[2,32,1024]{2,1,0:T(8,128)(2,1)S(1)} %get-tuple-element.50), channel_id=1, source_target_pairs={{0,2},{1,3},{2,0},{3,1},{4,6},{5,7},{6,4},{7,5},{8,10},{9,11},{10,... | collective-permute-start | bytes 393224 | tf_op jit(solution)/shard_map/ppermute | solution.py:17
  49.5 1.7 %slice-start.11 = ((s8[14680064]{0:T(1024)(128)(4,1)}), s8[2097152]{0:T(1024)(128)(4,1)S(1)}, s32[]{:S(2)}) async-start(s8[14680064]{0:T(1024)(128)(4,1)} %bitcast.5), calls=%async_computation.11 | async-start | bytes 4194304
  49.6 1.3 %collective-permute-start.13 = (bf16[2,32,512]{2,1,0:T(8,128)(2,1)S(1)}, bf16[2,32,512]{2,1,0:T(8,128)(2,1)S(1)}, u32[]{:S(2)}, u32[]{:S(2)}) collective-permute-start(bf16[2,32,512]{2,1,0:T(8,128)(2,1)S(1)} %act.2.refs_0_), channel_id=1, source_target_pairs={{0,1},{1,0},{2,3},{3,2},{4,5},{5,4},{6,7},{7,6},{8,9},{9,8},{10,11... | collective-permute-start | bytes 196616 | tf_op jit(solution)/shard_map/ppermute | solution.py:17
  52.9 1.3 %collective-permute-start.14 = (bf16[2,32,512]{2,1,0:T(8,128)(2,1)S(1)}, bf16[2,32,512]{2,1,0:T(8,128)(2,1)S(1)}, u32[]{:S(2)}, u32[]{:S(2)}) collective-permute-start(bf16[2,32,512]{2,1,0:T(8,128)(2,1)S(1)} %act.3.refs_0_), channel_id=1, source_target_pairs={{0,1},{1,0},{2,3},{3,2},{4,5},{5,4},{6,7},{7,6},{8,9},{9,8},{10,11... | collective-permute-start | bytes 196616 | tf_op jit(solution)/shard_map/ppermute | solution.py:17
  55.1 6.7 %collective-permute-start.15 = (bf16[16,1792]{1,0:T(8,128)(2,1)S(1)}, bf16[16,1792]{1,0:T(8,128)(2,1)S(1)}, u32[]{:S(2)}, u32[]{:S(2)}) collective-permute-start(bf16[16,1792]{1,0:T(8,128)(2,1)S(1)} %get-tuple-element.54), channel_id=1, source_target_pairs={{0,24},{4,28},{8,16},{12,20},{16,8},{20,12},{24,0},{28,4},{1,25},{... | collective-permute-start | bytes 172040 | tf_op jit(solution)/shard_map/ppermute | solution.py:17
  57.3 6.3 %collective-permute-start.16 = (bf16[16,1792]{1,0:T(8,128)(2,1)S(1)}, bf16[16,1792]{1,0:T(8,128)(2,1)S(1)}, u32[]{:S(2)}, u32[]{:S(2)}) collective-permute-start(bf16[16,1792]{1,0:T(8,128)(2,1)S(1)} %get-tuple-element.55), channel_id=1, source_target_pairs={{0,16},{4,20},{8,24},{12,28},{16,0},{20,4},{24,8},{28,12},{1,17},{... | collective-permute-start | bytes 172040 | tf_op jit(solution)/shard_map/ppermute | solution.py:17
  57.7 6.0 %collective-permute-start.17 = (bf16[16,1792]{1,0:T(8,128)(2,1)S(1)}, bf16[16,1792]{1,0:T(8,128)(2,1)S(1)}, u32[]{:S(2)}, u32[]{:S(2)}) collective-permute-start(bf16[16,1792]{1,0:T(8,128)(2,1)S(1)} %get-tuple-element.56), channel_id=1, source_target_pairs={{0,8},{4,12},{8,0},{12,4},{16,24},{20,28},{24,16},{28,20},{1,9},{5... | collective-permute-start | bytes 172040 | tf_op jit(solution)/shard_map/ppermute | solution.py:17
  63.7 3.9 %collective-permute-start.18 = (bf16[8,1792]{1,0:T(8,128)(2,1)S(1)}, bf16[8,1792]{1,0:T(8,128)(2,1)S(1)}, u32[]{:S(2)}, u32[]{:S(2)}) collective-permute-start(bf16[8,1792]{1,0:T(8,128)(2,1)S(1)} %get-tuple-element.58), channel_id=1, source_target_pairs={{0,4},{4,0},{8,12},{12,8},{16,20},{20,16},{24,28},{28,24},{1,5},{5... | collective-permute-start | bytes 86024 | tf_op jit(solution)/shard_map/ppermute | solution.py:17

commit v4 on v3

--- a/solution.py
+++ b/solution.py
@@ -74,81 +74,80 @@
     return jnp.where(lane < heads, x, 0.0)
 
 
-def attend_body(qn_h, qr_h, wuk_h, wuv_h, prompt_h, keep, send, qn, qr, wuk, wuv, prompt, rows_scr, sems):
-    rows, heads, nope = qn.shape
-    lat, vdim = wuk.shape[2], wuv.shape[2]
-    half, width = rows // 2, heads * vdim
-    group = min(4, heads)
-    steps = heads // group
-    core = lax.axis_index("grp") & 1
+def query_body(qn_h, qr_h, wuk_h, keys_h, queries, turned, keys, qn, qr, wuk, nope_scr, rope_scr, sems):
+    rows, heads, _ = qn.shape
+    half = heads // 2
+    group = min(4, half)
+    steps = half // group
+    first = (lax.axis_index("grp") & 1) * half
     copies = [
         pltpu.make_async_copy(qn_h, qn, sems.at[0]),
         pltpu.make_async_copy(qr_h, qr, sems.at[1]),
-        pltpu.make_async_copy(prompt_h, prompt, sems.at[2]),
+        pltpu.make_async_copy(keys_h, keys, sems.at[2]),
     ]
     uk = [
         pltpu.make_async_copy(
-            wuk_h.at[pl.ds(c * group, group)], wuk.at[pl.ds(c * group, group)], sems.at[3 + c]
+            wuk_h.at[pl.ds(first + c * group, group)], wuk.at[pl.ds(c * group, group)], sems.at[3 + c]
         )
         for c in range(steps)
     ]
-    uv = [
-        pltpu.make_async_copy(
-            wuv_h.at[pl.ds(c * group, group)], wuv.at[pl.ds(c * group, group)], sems.at[3 + steps + c]
+    for copy in [copies[0], uk[0], copies[1]] + uk[1:] + [copies[2]]:
+        copy.start()
+    copies[0].wait()
+    nope_scr[...] = jnp.swapaxes(qn[...], 0, 1)
+    copies[1].wait()
+    rope_scr[...] = jnp.swapaxes(qr[...], 0, 1)
+    for h in range(half):
+        turned[h * rows : (h + 1) * rows] = rope_scr[first + h]
+        if h % group == 0:
+            uk[h // group].wait()
+        q = jnp.dot(nope_scr[first + h], wuk[h], preferred_element_type=F32)
+        queries[h * rows : (h + 1) * rows] = q.astype(BF16)
+    copies[2].wait()
+
+
+def attend_body(scale, queries, turned, mine, other, wuv_h, keep, send, wuv, sems):
+    heads, lat, vdim = wuv.shape
+    rows = keep.shape[0]
+    width = heads * vdim
+    first = (lax.axis_index("grp") & 1) * heads
+    copy = pltpu.make_async_copy(wuv_h.at[pl.ds(first, heads)], wuv, sems.at[0])
+    copy.start()
+    q, r = queries[...], turned[...]
+    keys = (mine, other)
+    scores = []
+    for k in keys:
+        s = jnp.dot(q, k[:lat], preferred_element_type=F32)
+        scores.append((s + jnp.dot(r, k[lat:], preferred_element_type=F32)) * scale)
+    top = jnp.max(jnp.maximum(*scores), -1, keepdims=True)
+    total, w = 0.0, 0.0
+    for s, k in zip(scores, keys):
+        p = jnp.exp(s - top)
+        total = total + jnp.sum(p, -1, keepdims=True)
+        w = w + lax.dot_general(
+            p.astype(BF16), k[:lat], (((1,), (1,)), ((), ())), preferred_element_type=F32
         )
-        for c in range(steps)
-    ]
-    copies[0].start()
-    uk[0].start()
-    copies[1].start()
-    copies[2].start()
-    for c in range(steps):
-        if c:
-            uk[c].start()
-        uv[c].start()
-    scale = (nope + qr.shape[2]) ** (-0.5)
-    copies[0].wait()
-    queries = jnp.swapaxes(qn[...], 0, 1)
-    copies[1].wait()
-    turned = jnp.swapaxes(qr[...], 0, 1)
+    w = w * (1.0 / total)
+    hi = w.astype(BF16)
+    lo = (w - hi.astype(F32)).astype(BF16)
+    level = top + jnp.log(total)
     lane = lax.broadcasted_iota(jnp.int32, (rows, LANES), 1)
     lse = jnp.zeros((rows, LANES), F32)
-    for c in range(steps):
-        own = range(c * group, (c + 1) * group)
-        uk[c].wait()
-        q = jnp.concatenate(
-            [jnp.dot(queries[h], wuk[h], preferred_element_type=F32).astype(BF16) for h in own], 0
-        )
-        r = jnp.concatenate([turned[h] for h in own], 0)
-        if c == 0:
-            copies[2].wait()
-        s = jnp.dot(q, prompt[:lat], preferred_element_type=F32)
-        s = (s + jnp.dot(r, prompt[lat:], preferred_element_type=F32)) * scale
-        top = jnp.max(s, -1, keepdims=True)
-        p = jnp.exp(s - top)
-        total = jnp.sum(p, -1, keepdims=True)
-        w = lax.dot_general(
-            p.astype(BF16), prompt[:lat], (((1,), (1,)), ((), ())), preferred_element_type=F32
-        )
-        w = w * (1.0 / total)
-        hi = w.astype(BF16)
-        lo = (w - hi.astype(F32)).astype(BF16)
-        part = top + jnp.log(total)
-        uv[c].wait()
-        for i, h in enumerate(own):
-            at = slice(i * rows, (i + 1) * rows)
-            v = jnp.dot(jnp.concatenate([hi[at], lo[at]], 0), wuv[h], preferred_element_type=F32)
-            rows_scr[:, h * vdim : (h + 1) * vdim] = v[:rows] + v[rows:]
-            lse = jnp.where(lane == h, part[at], lse)
-    rows_scr[:, width:] = lse
-    keep[...] = rows_scr[pl.ds(pl.multiple_of(core * half, half), half)]
-    out = rows_scr[pl.ds(pl.multiple_of((1 - core) * half, half), half)]
-    send[:, :width] = out[:, :width].astype(BF16)
-    send[:, width:] = pack_lse(out[:, width:], heads)
-
-
-def merge_values(heads, own, others):
-    width = own.shape[1] - LANES
+    copy.wait()
+    for h in range(heads):
+        at = slice(h * rows, (h + 1) * rows)
+        v = jnp.dot(jnp.concatenate([hi[at], lo[at]], 0), wuv[h], preferred_element_type=F32)
+        v = v[:rows] + v[rows:]
+        keep[:, h * vdim : (h + 1) * vdim] = v
+        send[:, h * vdim : (h + 1) * vdim] = v.astype(BF16)
+        lse = jnp.where(lane == h, level[at], lse)
+    keep[:, width:] = lse
+    send[:, width:] = pack_lse(lse, heads)
+
+
+def merge_body(heads, own, *refs):
+    *others, out = refs
+    width = out.shape[1]
     vdim = width // heads
     levels = [own[:, width:]] + [unpack_lse(o[:, width:], heads) for o in others]
     top = levels[0]
@@ -157,47 +156,32 @@
     raised = [jnp.exp(x - top) for x in levels]
     total = sum(raised)
     shares = [x / total for x in raised]
-    cols = []
     for h in range(heads):
         at = slice(h * vdim, (h + 1) * vdim)
         v = own[:, at] * shares[0][:, h : h + 1]
         for share, o in zip(shares[1:], others):
             v = v + o[:, at].astype(F32) * share[:, h : h + 1]
-        cols.append(v)
-    lane = lax.broadcasted_iota(jnp.int32, top.shape, 1)
-    return cols, jnp.where(lane < heads, top + jnp.log(total), 0.0)
-
-
-def pair_body(heads, own, other, keep, send):
-    width = own.shape[1] - LANES
-    vdim = width // heads
-    cols, lse = merge_values(heads, own, [other])
-    for h, v in enumerate(cols):
-        keep[:, h * vdim : (h + 1) * vdim] = v
-        send[:, h * vdim : (h + 1) * vdim] = v.astype(BF16)
-    keep[:, width:] = lse
-    send[:, width:] = pack_lse(lse, heads)
-
-
-def final_body(heads, own, *refs):
-    out = refs[-1]
-    vdim = (own.shape[1] - LANES) // heads
-    cols, _ = merge_values(heads, own, refs[:-1])
-    for h, v in enumerate(cols):
-        out[:, h * vdim : (h + 1) * vdim] = v.astype(BF16)
-
-
-def project_body(mine, other, routes, scores, w, keep, *refs):
-    *sends, info, att, res, pad = refs
-    half = mine.shape[0]
+        out[:, at] = v.astype(BF16)
+
+
+def head_rows(width, mine):
+    core = lax.axis_index("grp") & 1
+    return pl.ds(pl.multiple_of((core if mine else 1 - core) * width, width), width)
+
+
+def project_mine_body(mine, w, out):
+    out[...] = jnp.dot(mine[...], w[head_rows(mine.shape[1], True)], preferred_element_type=F32)
+
+
+def project_body(part, other, routes, scores, w, keep, *refs):
+    *sends, info, res, pad = refs
     width = w.shape[1]
     tail = sends[0].shape[1] - LANES
     count, top = routes.shape
-    core = lax.axis_index("grp") & 1
     ctx = lax.axis_index("ctx")
-    att[pl.ds(pl.multiple_of(core * half, half), half)] = mine[...]
-    att[pl.ds(pl.multiple_of((1 - core) * half, half), half)] = other[...]
-    res[...] = jnp.dot(att[...], w[...], preferred_element_type=F32)
+    res[...] = part[...] + jnp.dot(
+        other[...], w[head_rows(other.shape[1], False)], preferred_element_type=F32
+    )
 
     def block(turn, s):
         owner = ctx ^ (2 * s + turn)
@@ -353,20 +337,21 @@
     return v + jnp.dot(lo, result, preferred_element_type=F32)
 
 
-def down_body(experts, mine, other, down, mix, out):
-    hid = mine.shape[2]
-    low, high = half_cols(hid, True), half_cols(hid, False)
-    parts = []
-    for i, e in enumerate(experts):
-        v = jnp.dot(mine[i], down[e, low], preferred_element_type=F32)
-        parts.append(v + jnp.dot(other[i], down[e, high], preferred_element_type=F32))
-    out[...] = weigh(experts, mine.shape[1], mix, parts)
-
-
 def down_mine_body(experts, mine, down, out):
     low = half_cols(mine.shape[2], True)
     for i, e in enumerate(experts):
         out[i] = jnp.dot(mine[i], down[e, low], preferred_element_type=F32)
+
+
+def down_next_body(experts, later, part, other, mine, down, mix, out, ahead):
+    low, high = half_cols(mine.shape[2], True), half_cols(mine.shape[2], False)
+    parts = [
+        part[i] + jnp.dot(other[i], down[e, high], preferred_element_type=F32)
+        for i, e in enumerate(experts)
+    ]
+    for i, e in enumerate(later):
+        ahead[i] = jnp.dot(mine[i], down[e, low], preferred_element_type=F32)
+    out[...] = weigh(experts, other.shape[1], mix, parts)
 
 
 def down_last_body(has_before, experts, part, other, down, mix, *refs):
@@ -419,36 +404,44 @@
     experts, _, ff = expert_gate.shape
     cap = CAP * n_ctx
     hid = ff // 2
-    half = rows // 2
-    hv = heads * vdim
+    hv = heads // 2 * vdim
     tail = -(-width // LANES) * LANES
     far = n_ctx // 2
     in_vmem = lambda a: pltpu.with_memory_space_constraint(a, VMEM)
 
     keys = prompt.T
+    far_keys = swap(keys, "grp", 1)
+    many = heads // 2 * rows
+    queries, turned, keys = run(
+        "queries", query_body,
+        [((many, lat), BF16), ((many, q_rope.shape[2]), BF16), (keys.shape, BF16)],
+        [q_nope, q_rope, w_uk, keys],
+        scratch=[
+            VMEM(q_nope.shape, BF16), VMEM(q_rope.shape, BF16), VMEM((heads // 2,) + w_uk.shape[1:], BF16),
+            VMEM((heads, rows, nope), BF16), VMEM((heads, rows, q_rope.shape[2]), BF16),
+            pltpu.SemaphoreType.DMA((3 + max(1, heads // 8),)),
+        ],
+        us=2, limit=6, hbm=range(4),
+    )
+    scale = (nope + q_rope.shape[2]) ** (-0.5)
     keep, send = run(
-        "attend", attend_body, [((half, hv + LANES), F32), ((half, hv + LANES), BF16)],
-        [q_nope, q_rope, w_uk, w_uv, keys],
-        scratch=[
-            VMEM(q_nope.shape, BF16), VMEM(q_rope.shape, BF16), VMEM(w_uk.shape, BF16),
-            VMEM(w_uv.shape, BF16), VMEM(keys.shape, BF16), VMEM((rows, hv + LANES), F32),
-            pltpu.SemaphoreType.DMA((3 + 2 * (heads // min(4, heads)),)),
-        ],
-        us=12, limit=10, hbm=range(5),
-    )
-    keep, send = run(
-        "pair", bind(pair_body, heads), [((half, hv + LANES), F32), ((half, hv + LANES), BF16)],
-        [keep, swap(send, "grp", 1)], us=1,
+        "attend", bind(attend_body, scale), [((rows, hv + LANES), F32), ((rows, hv + LANES), BF16)],
+        [queries, turned, keys, far_keys, w_uv],
+        scratch=[VMEM((heads // 2,) + w_uv.shape[1:], BF16), pltpu.SemaphoreType.DMA((1,))],
+        us=12, limit=12, hbm=(4,),
     )
     (mine,) = run(
-        "merge", bind(final_body, heads), [((half, hv), BF16)], [keep] + spread(send, "grp"), us=1
-    )
+        "merge", bind(merge_body, heads // 2), [((rows, hv), BF16)], [keep] + spread(send, "grp"), us=1
+    )
+    other = swap(mine, "grp", 1)
+    w_out = in_vmem(w_out)
+    (part,) = run("project_mine", project_mine_body, [((rows, width), F32)], [mine, w_out], us=0.5)
     pair = 2 * count
     keep, *sends, info = run(
         "project", project_body,
         [((pair, width), F32)] + [((pair, tail + LANES), BF16)] * (far - 1) + [((count, LANES), F32)],
-        [mine, swap(mine, "grp", 1), routes, route_scores, in_vmem(w_out)],
-        scratch=[VMEM((rows, hv), BF16), VMEM((rows, width), F32), VMEM((pair, LANES), F32)], us=1,
+        [part, other, routes, route_scores, w_out],
+        scratch=[VMEM((rows, width), F32), VMEM((pair, LANES), F32)], us=1,
     )
     wide = -(-32 * far // LANES) * LANES
     own, send = run(
@@ -464,10 +457,10 @@
     parts[0] = moe
     pick, mix = run(
         "route", bind(route_body, experts, top, tail),
-        [((experts * cap, rows), BF16), ((rows, experts * cap), F32)], [send, other], us=0.5,
+        [((experts * cap, rows), BF16), ((rows, experts * cap), F32)], [send, other], us=0.5, after=[parts[far - 1]],
     )
     gate, up, down = in_vmem(expert_gate), in_vmem(expert_up), in_vmem(expert_down)
-    size = max(1, experts // 2)
+    size = -(-experts // 2)
     groups = [range(i, i + size) for i in range(0, experts, size)]
     shape = (size, cap, 2 * hid)
     whole = (experts, cap, 2 * hid)
@@ -487,25 +480,30 @@
             "add", bind(add_body, g), [(shape, F32), (shape, BF16)], [part, other], us=0.1
         )
         sums.append((keep, spread(send, "grp")))
-    before = []
+    before, later = [], []
     for g, (keep, others) in zip(groups, sums):
         (act,) = run(
-            "act", act_body, [((size, cap, hid), BF16)], [keep] + others, us=5, after=before if before else [sums[-1][0]]
+            "act", act_body, [((size, cap, hid), BF16)], [keep] + others, us=5,
+            after=later or [sums[-1][0]],
         )
-        other = swap(act, "grp", 1)
-        if g is not groups[-1]:
-            before = list(run(
-                "down", bind(down_body, g), [((rows, width), F32)], [act, other, down, mix], us=0.5
-            ))
+        other_act = swap(act, "grp", 1)
+        if later:
+            before, part = run(
+                "down_next", bind(down_next_body, groups[0], g),
+                [((rows, width), F32), ((size, cap, width), F32)],
+                [later[0], last_act, act, down, mix], us=1,
+            )
+            before = [before]
         else:
             (part,) = run(
                 "down_mine", bind(down_mine_body, g), [((size, cap, width), F32)], [act, down], us=0.5
             )
-            keep, *sends = run(
-                "down_last", bind(down_last_body, len(before), g),
-                [((pair, width), F32)] + [((pair, width), BF16)] * (far - 1),
-                [part, other, down, mix] + before, us=5,
-            )
+            later, last_act = [part], other_act
+    keep, *sends = run(
+        "down_last", bind(down_last_body, len(before), groups[-1]),
+        [((pair, width), F32)] + [((pair, width), BF16)] * (far - 1),
+        [part, other_act, down, mix] + before, us=1,
+    )
     own, send = run(
         "last_sum", last_sum_body, [((count, width), F32), ((count, width), BF16)],
         [keep] + scatter(sends, "ctx"), us=3,

time: 68.4 us -> 66.3 us (0.969)
  waiting for transfers between devices: 27.2 us -> 24.7 us
  local copies, waits for them, and re-layouts: 0.35 us -> 1.6 us
    ppermute x19, waiting for transfers between devices: 27.2 us -> 24.7 us  [swap(): lax.ppermute(x, axis, [(a, a ^ bits) for a in range(lax.axis_size(axis))])]
    unnamed x32 -> x34, local copies, waits for them, and re-layouts: 0.35 us -> 1.6 us
    pallas_call x19 -> x20, Pallas kernels: 18 us -> 17.5 us  [run(): pl.pallas_call(ordered, out_shape=[jax.ShapeDtypeStruct(s, d) for s, d in...]
  transfers between devices with their start and end apart: 19 -> 19, of which waited for: 15 -> 13; matrix products, arithmetic and copies ran while one was open for 0% -> 0% of each run, Pallas kernels for 8% -> 13%
where the time goes in v4:
time: 66.3 us; the launch traced here: 66.2 us
  waiting for transfers between devices  24.7 us (37%)
  starting transfers between devices  22 us (33%)
  Pallas kernels  17.5 us (26%)
  local copies, waits for them, and re-layouts  1.6 us (2%)
    ppermute x19, waiting for transfers between devices, swap(): lax.ppermute(x, axis, [(a, a ^ bits) for a in range(lax.axis_size(axis))])  24.7 us
    ppermute x19, starting transfers between devices, swap(): lax.ppermute(x, axis, [(a, a ^ bits) for a in range(lax.axis_size(axis))])  22 us
    pallas_call x20, Pallas kernels, run(): pl.pallas_call(ordered, out_shape=[jax.ShapeDtypeStruct(s, d) for s, d in...  17.5 us
    unnamed x34, local copies, waits for them, and re-layouts  1.6 us
  transfers between devices with their start and end apart: 19, of which 13 were waited for; matrix products, arithmetic and copies ran while one was open for 0% of the time, Pallas kernels for 13%

profile of v4, /device:TPU:0, one launch (start us, length us, event | category | flops | bytes accessed | tf_op | source)
XLA Modules:
  0.0 66.2 jit_solution(10486572445154843947)
XLA Ops:
  0.0 0.5 collective-permute-start
  0.5 2.0 %queries.1 = (bf16[512,512]{1,0:T(8,128)(2,1)S(1)}, bf16[512,64]{1,0:T(8,128)(2,1)S(1)}, bf16[576,384]{1,0:T(8,128)(2,1)S(1)}) custom-call(bf16[64,16,128]{2,1,0:T(8,128)(2,1)} %refs_0_.1, bf16[64,16,64]{2,1,0:T(8,128)(2,1)} %refs_1_.7, bf16[16,128,512]{2,1,0:T(8,128)(2,1)} %refs_2_.6, bf16[576,384]{1,0:T(8,128)(2,1)} %bitcast.10), custom_call_target="tpu_custom_call" | custom-call | flops 2300000000 | bytes 1024 | tf_op jit(solution)/shard_map/queries/pallas_call | solution.py:42
  2.4 0.0 slice-start.13
  2.4 0.0 copy-start
  2.5 0.0 copy-start.1
  2.5 0.0 slice-start.4
  2.5 0.0 slice-start.5
  2.5 0.0 slice-start.6
  2.5 3.6 %attend.1 = (f32[64,1152]{1,0:T(8,128)S(1)}, bf16[64,1152]{1,0:T(8,128)(2,1)S(1)}) custom-call(bf16[512,512]{1,0:T(8,128)(2,1)S(1)} %get-tuple-element.35.refs_0_, bf16[512,64]{1,0:T(8,128)(2,1)S(1)} %get-tuple-element.36.refs_1_, bf16[576,384]{1,0:T(8,128)(2,1)S(1)} %get-tuple-element.37.refs_2_, bf16[576,384]{1,0:T(8,128)(2,1)S(1)} %collective-permute-done.refs_3_, ...), custom_call_target="tpu_custom_call" | custom-call | flops 13799999488 | bytes 1024 | tf_op jit(solution)/shard_map/attend/pallas_call | solution.py:42
  6.1 0.0 copy-start.2
  6.1 2.5 %collective-permute-start.1 = (bf16[64,1152]{1,0:T(8,128)(2,1)S(1)}, bf16[64,1152]{1,0:T(8,128)(2,1)S(1)}, u32[]{:S(2)}, u32[]{:S(2)}) collective-permute-start(bf16[64,1152]{1,0:T(8,128)(2,1)S(1)} %get-tuple-element.39), channel_id=1, source_target_pairs={{0,2},{1,3},{2,0},{3,1},{4,6},{5,7},{6,4},{7,5},{8,10},{9,11},{10,... | collective-permute-start | bytes 442376 | tf_op jit(solution)/shard_map/ppermute | solution.py:17
  8.6 4.5 %collective-permute-done.1.refs_1_ = bf16[64,1152]{1,0:T(8,128)(2,1)S(1)} collective-permute-done((bf16[64,1152]{1,0:T(8,128)(2,1)S(1)}, bf16[64,1152]{1,0:T(8,128)(2,1)S(1)}, u32[]{:S(2)}, u32[]{:S(2)}) %collective-permute-start.1) | collective-permute-done | bytes 147488 | tf_op jit(solution)/shard_map/ppermute | solution.py:17
  13.2 0.3 merge.1.refs_0_
  13.5 0.0 slice-start.1
  13.5 0.0 slice-start.7
  13.5 0.1 collective-permute-start.2
  13.6 0.8 %project_mine.1.refs_0_ = f32[64,1792]{1,0:T(8,128)S(1)} custom-call(bf16[64,1024]{1,0:T(8,128)(2,1)S(1)} %merge.1.refs_0_, bf16[2048,1792]{1,0:T(8,128)(2,1)S(1)} %bitcast.8), custom_call_target="tpu_custom_call" | custom-call | flops 575000000 | bytes 1024 | tf_op jit(solution)/shard_map/project_mine/pallas_call | solution.py:42
  14.4 0.0 slice-start.2
  14.4 0.5 collective-permute-done.2.refs_1_
  14.9 0.8 %project.1 = (f32[16,1792]{1,0:T(8,128)S(1)}, bf16[16,1920]{1,0:T(8,128)(2,1)S(1)}, bf16[16,1920]{1,0:T(8,128)(2,1)S(1)}, bf16[16,1920]{1,0:T(8,128)(2,1)S(1)}, f32[8,128]{1,0:T(8,128)S(1)}) custom-call(f32[64,1792]{1,0:T(8,128)S(1)} %project_mine.1.refs_0_, bf16[64,1024]{1,0:T(8,128)(2,1)S(1)} %collective-permute-done.2.refs_1_, s32[8,8]{1,0:T(8,128)S(1)} %copy-done, ...), custom_call_target="tpu_custom_call" | custom-call | flops 1150000000 | bytes 1024 | tf_op jit(solution)/shard_map/project/pallas_call | solution.py:42
  15.7 3.9 %collective-permute-start.3 = (bf16[16,1920]{1,0:T(8,128)(2,1)S(1)}, bf16[16,1920]{1,0:T(8,128)(2,1)S(1)}, u32[]{:S(2)}, u32[]{:S(2)}) collective-permute-start(bf16[16,1920]{1,0:T(8,128)(2,1)S(1)} %get-tuple-element.42), channel_id=1, source_target_pairs={{0,24},{4,28},{8,16},{12,20},{16,8},{20,12},{24,0},{28,4},{1,25},{... | collective-permute-start | bytes 184328 | tf_op jit(solution)/shard_map/ppermute | solution.py:17
  19.6 0.0 collective-permute-start.4
  19.6 0.6 collective-permute-start.5
  20.3 1.8 %collective-permute-done.3.refs_3_ = bf16[16,1920]{1,0:T(8,128)(2,1)S(1)} collective-permute-done((bf16[16,1920]{1,0:T(8,128)(2,1)S(1)}, bf16[16,1920]{1,0:T(8,128)(2,1)S(1)}, u32[]{:S(2)}, u32[]{:S(2)}) %collective-permute-start.3) | collective-permute-done | bytes 61472 | tf_op jit(solution)/shard_map/ppermute | solution.py:17
  22.1 3.1 %collective-permute-done.4.refs_4_ = bf16[16,1920]{1,0:T(8,128)(2,1)S(1)} collective-permute-done((bf16[16,1920]{1,0:T(8,128)(2,1)S(1)}, bf16[16,1920]{1,0:T(8,128)(2,1)S(1)}, u32[]{:S(2)}, u32[]{:S(2)}) %collective-permute-start.4) | collective-permute-done | bytes 61472 | tf_op jit(solution)/shard_map/ppermute | solution.py:17
  25.2 0.0 collective-permute-done.5.refs_5_
  25.2 0.1 rest_sum.1
  25.3 1.6 %collective-permute-start.6 = (bf16[16,1920]{1,0:T(8,128)(2,1)S(1)}, bf16[16,1920]{1,0:T(8,128)(2,1)S(1)}, u32[]{:S(2)}, u32[]{:S(2)}) collective-permute-start(bf16[16,1920]{1,0:T(8,128)(2,1)S(1)} %get-tuple-element.46.refs_0_), channel_id=1, source_target_pairs={{0,4},{4,0},{8,12},{12,8},{16,20},{20,16},{24,28},{28,24},{1,5},{5... | collective-permute-start | bytes 184328 | tf_op jit(solution)/shard_map/ppermute | solution.py:17
  26.8 2.7 %collective-permute-done.6.refs_1_ = bf16[16,1920]{1,0:T(8,128)(2,1)S(1)} collective-permute-done((bf16[16,1920]{1,0:T(8,128)(2,1)S(1)}, bf16[16,1920]{1,0:T(8,128)(2,1)S(1)}, u32[]{:S(2)}, u32[]{:S(2)}) %collective-permute-start.6) | collective-permute-done | bytes 61472 | tf_op jit(solution)/shard_map/ppermute | solution.py:17
  29.6 2.5 %collective-permute-start.7 = (bf16[16,1792]{1,0:T(8,128)(2,1)S(1)}, bf16[16,1792]{1,0:T(8,128)(2,1)S(1)}, u32[]{:S(2)}, u32[]{:S(2)}) collective-permute-start(bf16[16,1792]{1,0:T(8,128)(2,1)S(1)} %get-tuple-element.48.refs_3_), channel_id=1, source_target_pairs={{0,24},{4,28},{8,16},{12,20},{16,8},{20,12},{24,0},{28,4},{1,25},{... | collective-permute-start | bytes 172040 | tf_op jit(solution)/shard_map/ppermute | solution.py:17
  32.1 0.1 collective-permute-start.9
  32.2 1.8 %collective-permute-start.8 = (bf16[16,1792]{1,0:T(8,128)(2,1)S(1)}, bf16[16,1792]{1,0:T(8,128)(2,1)S(1)}, u32[]{:S(2)}, u32[]{:S(2)}) collective-permute-start(bf16[16,1792]{1,0:T(8,128)(2,1)S(1)} %get-tuple-element.48.refs_3_), channel_id=1, source_target_pairs={{0,8},{4,12},{8,0},{12,4},{16,24},{20,28},{24,16},{28,20},{1,9},{5... | collective-permute-start | bytes 172040 | tf_op jit(solution)/shard_map/ppermute | solution.py:17
  34.0 1.9 %collective-permute-done.7.refs_2_.refs_6_ = bf16[16,1792]{1,0:T(8,128)(2,1)S(1)} collective-permute-done((bf16[16,1792]{1,0:T(8,128)(2,1)S(1)}, bf16[16,1792]{1,0:T(8,128)(2,1)S(1)}, u32[]{:S(2)}, u32[]{:S(2)}) %collective-permute-start.7) | collective-permute-done | bytes 57376 | tf_op jit(solution)/shard_map/ppermute | solution.py:17
  36.0 0.5 route.1
  36.5 0.7 %collective-permute-done.9.refs_5_ = bf16[16,1792]{1,0:T(8,128)(2,1)S(1)} collective-permute-done((bf16[16,1792]{1,0:T(8,128)(2,1)S(1)}, bf16[16,1792]{1,0:T(8,128)(2,1)S(1)}, u32[]{:S(2)}, u32[]{:S(2)}) %collective-permute-start.9) | collective-permute-done | bytes 57376 | tf_op jit(solution)/shard_map/ppermute | solution.py:17
  37.2 0.0 collective-permute-done.8.refs_4_
  37.3 2.8 %other_half.1 = (bf16[128,1792]{1,0:T(8,128)(2,1)S(1)}, bf16[4,32,1024]{2,1,0:T(8,128)(2,1)S(1)}) custom-call(bf16[128,64]{1,0:T(8,128)(2,1)S(1)} %get-tuple-element.49.refs_0_, bf16[4,1792,1024]{2,1,0:T(8,128)(2,1)S(1)} %bitcast.2, bf16[4,1792,1024]{2,1,0:T(8,128)(2,1)S(1)} %bitcast.4, bf16[16,1792]{1,0:T(8,128)(2,1)S(1)} %get-tuple-element.48.refs_3_, ...), custom_call_target="tpu_custom_call" | custom-call | flops 575000000 | bytes 1024 | tf_op jit(solution)/shard_map/other_half/pallas_call | solution.py:42
  40.0 0.0 collective-permute-start.10
  40.1 1.4 %own_half.2.refs_0_ = f32[2,32,1024]{2,1,0:T(8,128)S(1)} custom-call(bf16[128,1792]{1,0:T(8,128)(2,1)S(1)} %get-tuple-element.50.refs_0_, bf16[4,1792,1024]{2,1,0:T(8,128)(2,1)S(1)} %bitcast.2, bf16[4,1792,1024]{2,1,0:T(8,128)(2,1)S(1)} %bitcast.4, bf16[4,32,1024]{2,1,0:T(8,128)(2,1)S(1)} %get-tuple-element.51.refs_3_), custom_call_target="tpu_custom_call" | custom-call | flops 575000000 | bytes 1024 | tf_op jit(solution)/shard_map/own_half/pallas_call | solution.py:42
  41.4 0.2 collective-permute-done.10.refs_1_
  41.6 1.6 %collective-permute-start.11 = (bf16[2,32,1024]{2,1,0:T(8,128)(2,1)S(1)}, bf16[2,32,1024]{2,1,0:T(8,128)(2,1)S(1)}, u32[]{:S(2)}, u32[]{:S(2)}) collective-permute-start(bf16[2,32,1024]{2,1,0:T(8,128)(2,1)S(1)} %get-tuple-element.53), channel_id=1, source_target_pairs={{0,2},{1,3},{2,0},{3,1},{4,6},{5,7},{6,4},{7,5},{8,10},{9,11},{10,... | collective-permute-start | bytes 393224 | tf_op jit(solution)/shard_map/ppermute | solution.py:17
  43.2 1.3 %own_half.3.refs_0_ = f32[2,32,1024]{2,1,0:T(8,128)S(1)} custom-call(bf16[128,1792]{1,0:T(8,128)(2,1)S(1)} %get-tuple-element.50.refs_0_, bf16[4,1792,1024]{2,1,0:T(8,128)(2,1)S(1)} %bitcast.2, bf16[4,1792,1024]{2,1,0:T(8,128)(2,1)S(1)} %bitcast.4, f32[2,32,1024]{2,1,0:T(8,128)S(1)} %get-tuple-element.52.refs_3_.refs_0_), custom_call_target="tpu_custom_call" | custom-call | flops 575000000 | bytes 1024 | tf_op jit(solution)/shard_map/own_half/pallas_call | solution.py:42
  44.6 0.6 collective-permute-start.13
  45.2 2.3 %collective-permute-done.11.refs_1_ = bf16[2,32,1024]{2,1,0:T(8,128)(2,1)S(1)} collective-permute-done((bf16[2,32,1024]{2,1,0:T(8,128)(2,1)S(1)}, bf16[2,32,1024]{2,1,0:T(8,128)(2,1)S(1)}, u32[]{:S(2)}, u32[]{:S(2)}) %collective-permute-start.11) | collective-permute-done | bytes 131104 | tf_op jit(solution)/shard_map/ppermute | solution.py:17
  47.5 0.1 act.2.refs_0_
  47.6 0.1 collective-permute-start.12
  47.7 0.2 slice-done.10
  47.9 1.3 %slice-done.11 = s8[2097152]{0:T(1024)(128)(4,1)S(1)} async-done(((s8[14680064]{0:T(1024)(128)(4,1)}), s8[2097152]{0:T(1024)(128)(4,1)S(1)}, s32[]{:S(2)}) %slice-start.11) | async-done | bytes 2097176
  49.2 0.7 %down_mine.1.refs_2_.refs_0_ = f32[2,32,1792]{2,1,0:T(8,128)S(1)} custom-call(bf16[2,32,512]{2,1,0:T(8,128)(2,1)S(1)} %act.2.refs_0_, bf16[4,1024,1792]{2,1,0:T(8,128)(2,1)S(1)} %bitcast.6), custom_call_target="tpu_custom_call" | custom-call | flops 575000000 | bytes 1024 | tf_op jit(solution)/shard_map/down_mine/pallas_call | solution.py:42
  49.9 0.4 collective-permute-done.13.refs_1_
  50.3 0.1 act.3.refs_2_
  50.3 0.1 collective-permute-start.14
  50.4 0.0 collective-permute-done.12.refs_1_
  50.4 1.5 %down_next.1 = (f32[64,1792]{1,0:T(8,128)S(1)}, f32[2,32,1792]{2,1,0:T(8,128)S(1)}) custom-call(f32[2,32,1792]{2,1,0:T(8,128)S(1)} %down_mine.1.refs_2_.refs_0_, bf16[2,32,512]{2,1,0:T(8,128)(2,1)S(1)} %collective-permute-done.12.refs_1_, bf16[2,32,512]{2,1,0:T(8,128)(2,1)S(1)} %act.3.refs_2_, bf16[4,1024,1792]{2,1,0:T(8,128)(2,1)S(1)} %bitcast.6, ...), custom_call_target="tpu_custom_call" | custom-call | flops 1150000000 | bytes 1024 | tf_op jit(solution)/shard_map/down_next/pallas_call | solution.py:42
  52.0 1.0 %down_last.1 = (f32[16,1792]{1,0:T(8,128)S(1)}, bf16[16,1792]{1,0:T(8,128)(2,1)S(1)}, bf16[16,1792]{1,0:T(8,128)(2,1)S(1)}, bf16[16,1792]{1,0:T(8,128)(2,1)S(1)}) custom-call(f32[2,32,1792]{2,1,0:T(8,128)S(1)} %get-tuple-element.57.refs_0_, bf16[2,32,512]{2,1,0:T(8,128)(2,1)S(1)} %collective-permute-done.14.refs_1_, bf16[4,1024,1792]{2,1,0:T(8,128)(2,1)S(1)} %bitcast.6, ...), custom_call_target="tpu_custom_call" | custom-call | flops 1150000000 | bytes 1024 | tf_op jit(solution)/shard_map/down_last/pallas_call | solution.py:42
  52.9 2.2 %collective-permute-start.15 = (bf16[16,1792]{1,0:T(8,128)(2,1)S(1)}, bf16[16,1792]{1,0:T(8,128)(2,1)S(1)}, u32[]{:S(2)}, u32[]{:S(2)}) collective-permute-start(bf16[16,1792]{1,0:T(8,128)(2,1)S(1)} %get-tuple-element.60), channel_id=1, source_target_pairs={{0,24},{4,28},{8,16},{12,20},{16,8},{20,12},{24,0},{28,4},{1,25},{... | collective-permute-start | bytes 172040 | tf_op jit(solution)/shard_map/ppermute | solution.py:17
  55.1 0.3 collective-permute-start.16
  55.5 1.9 %collective-permute-start.17 = (bf16[16,1792]{1,0:T(8,128)(2,1)S(1)}, bf16[16,1792]{1,0:T(8,128)(2,1)S(1)}, u32[]{:S(2)}, u32[]{:S(2)}) collective-permute-start(bf16[16,1792]{1,0:T(8,128)(2,1)S(1)} %get-tuple-element.62), channel_id=1, source_target_pairs={{0,8},{4,12},{8,0},{12,4},{16,24},{20,28},{24,16},{28,20},{1,9},{5... | collective-permute-start | bytes 172040 | tf_op jit(solution)/shard_map/ppermute | solution.py:17
  57.4 2.2 %collective-permute-done.15.refs_1_ = bf16[16,1792]{1,0:T(8,128)(2,1)S(1)} collective-permute-done((bf16[16,1792]{1,0:T(8,128)(2,1)S(1)}, bf16[16,1792]{1,0:T(8,128)(2,1)S(1)}, u32[]{:S(2)}, u32[]{:S(2)}) %collective-permute-start.15) | collective-permute-done | bytes 57376 | tf_op jit(solution)/shard_map/ppermute | solution.py:17
  59.5 2.0 %collective-permute-done.16.refs_2_ = bf16[16,1792]{1,0:T(8,128)(2,1)S(1)} collective-permute-done((bf16[16,1792]{1,0:T(8,128)(2,1)S(1)}, bf16[16,1792]{1,0:T(8,128)(2,1)S(1)}, u32[]{:S(2)}, u32[]{:S(2)}) %collective-permute-start.16) | collective-permute-done | bytes 57376 | tf_op jit(solution)/shard_map/ppermute | solution.py:17
  61.6 0.0 collective-permute-done.17.refs_3_
  61.6 1.6 %collective-permute-start.18 = (bf16[8,1792]{1,0:T(8,128)(2,1)S(1)}, bf16[8,1792]{1,0:T(8,128)(2,1)S(1)}, u32[]{:S(2)}, u32[]{:S(2)}) collective-permute-start(bf16[8,1792]{1,0:T(8,128)(2,1)S(1)} %get-tuple-element.64), channel_id=1, source_target_pairs={{0,4},{4,0},{8,12},{12,8},{16,20},{20,16},{24,28},{28,24},{1,5},{5... | collective-permute-start | bytes 86024 | tf_op jit(solution)/shard_map/ppermute | solution.py:17
  63.2 2.3 %collective-permute-done.18.refs_2_ = bf16[8,1792]{1,0:T(8,128)(2,1)S(1)} collective-permute-done((bf16[8,1792]{1,0:T(8,128)(2,1)S(1)}, bf16[8,1792]{1,0:T(8,128)(2,1)S(1)}, u32[]{:S(2)}, u32[]{:S(2)}) %collective-permute-start.18) | collective-permute-done | bytes 28704 | tf_op jit(solution)/shard_map/ppermute | solution.py:17
  65.5 0.6 out.1
  (32 shorter events, 0.2 us)
Async XLA Ops:
  0.0 2.4 %collective-permute-start = (bf16[576,384]{1,0:T(8,128)(2,1)}, bf16[576,384]{1,0:T(8,128)(2,1)S(1)}, u32[]{:S(2)}, u32[]{:S(2)}) collective-permute-start(bf16[576,384]{1,0:T(8,128)(2,1)} %bitcast.9), channel_id=1, source_target_pairs={{0,1},{1,0},{2,3},{3,2},{4,5},{5,4},{6,7},{7,6},{8,9},{9,8},{10,11... | collective-permute-start | bytes 1327112 | tf_op jit(solution)/shard_map/ppermute | solution.py:17
  0.5 13.1 %slice-start.12 = ((s8[7340032]{0:T(1024)(128)(4,1)}), s8[4194304]{0:T(1024)(128)(4,1)S(1)}, s32[]{:S(2)}) async-start(s8[7340032]{0:T(1024)(128)(4,1)} %bitcast.7), calls=%async_computation.12 | async-start | bytes 8388608
  2.4 11.2 %slice-start.13 = ((s8[7340032]{0:T(1024)(128)(4,1)}), s8[3145728]{0:T(1024)(128)(4,1)S(1)}, s32[]{:S(2)}) async-start(s8[7340032]{0:T(1024)(128)(4,1)} %bitcast.7), calls=%async_computation.13 | async-start | bytes 6291456
  2.4 12.5 %copy-start = (s32[8,8]{1,0:T(8,128)S(1)}, s32[8,8]{1,0:T(8,128)}, u32[]{:S(2)}) copy-start(s32[8,8]{1,0:T(8,128)} %refs_2_.7) | copy-start | bytes 772
  2.5 12.5 %copy-start.1 = (f32[8,8]{1,0:T(8,128)S(1)}, f32[8,8]{1,0:T(8,128)}, u32[]{:S(2)}) copy-start(f32[8,8]{1,0:T(8,128)} %refs_3_.2) | copy-start | bytes 772
  2.5 34.7 %slice-start.4 = ((s8[14680064]{0:T(1024)(128)(4,1)}), s8[4194304]{0:T(1024)(128)(4,1)S(1)}, s32[]{:S(2)}) async-start(s8[14680064]{0:T(1024)(128)(4,1)} %bitcast.3), calls=%async_computation.4 | async-start | bytes 8388608
  2.5 34.7 %slice-start.5 = ((s8[14680064]{0:T(1024)(128)(4,1)}), s8[4194304]{0:T(1024)(128)(4,1)S(1)}, s32[]{:S(2)}) async-start(s8[14680064]{0:T(1024)(128)(4,1)} %bitcast.3), calls=%async_computation.5 | async-start | bytes 8388608
  2.5 34.7 %slice-start.6 = ((s8[14680064]{0:T(1024)(128)(4,1)}), s8[4194304]{0:T(1024)(128)(4,1)S(1)}, s32[]{:S(2)}) async-start(s8[14680064]{0:T(1024)(128)(4,1)} %bitcast.3), calls=%async_computation.6 | async-start | bytes 8388608
  6.1 19.1 %copy-start.2 = (bf16[8,1792]{1,0:T(8,128)(2,1)S(1)}, bf16[8,1792]{1,0:T(8,128)(2,1)}, u32[]{:S(2)}) copy-start(bf16[8,1792]{1,0:T(8,128)(2,1)} %refs_1_.9) | copy-start | bytes 86020
  6.1 7.1 %collective-permute-start.1 = (bf16[64,1152]{1,0:T(8,128)(2,1)S(1)}, bf16[64,1152]{1,0:T(8,128)(2,1)S(1)}, u32[]{:S(2)}, u32[]{:S(2)}) collective-permute-start(bf16[64,1152]{1,0:T(8,128)(2,1)S(1)} %get-tuple-element.39), channel_id=1, source_target_pairs={{0,2},{1,3},{2,0},{3,1},{4,6},{5,7},{6,4},{7,5},{8,10},{9,11},{10,... | collective-permute-start | bytes 442376 | tf_op jit(solution)/shard_map/ppermute | solution.py:17
  13.2 24.1 %slice-start = ((s8[14680064]{0:T(1024)(128)(4,1)}), s8[4194304]{0:T(1024)(128)(4,1)S(1)}, s32[]{:S(2)}) async-start(s8[14680064]{0:T(1024)(128)(4,1)} %bitcast.1), calls=%async_computation | async-start | bytes 8388608
  13.5 23.8 %slice-start.1 = ((s8[14680064]{0:T(1024)(128)(4,1)}), s8[4194304]{0:T(1024)(128)(4,1)S(1)}, s32[]{:S(2)}) async-start(s8[14680064]{0:T(1024)(128)(4,1)} %bitcast.1), calls=%async_computation.1 | async-start | bytes 8388608
  13.5 23.8 %slice-start.7 = ((s8[14680064]{0:T(1024)(128)(4,1)}), s8[2097152]{0:T(1024)(128)(4,1)S(1)}, s32[]{:S(2)}) async-start(s8[14680064]{0:T(1024)(128)(4,1)} %bitcast.3), calls=%async_computation.7 | async-start | bytes 4194304
  13.5 1.4 %collective-permute-start.2 = (bf16[64,1024]{1,0:T(8,128)(2,1)S(1)}, bf16[64,1024]{1,0:T(8,128)(2,1)S(1)}, u32[]{:S(2)}, u32[]{:S(2)}) collective-permute-start(bf16[64,1024]{1,0:T(8,128)(2,1)S(1)} %merge.1.refs_0_), channel_id=1, source_target_pairs={{0,1},{1,0},{2,3},{3,2},{4,5},{5,4},{6,7},{7,6},{8,9},{9,8},{10,11... | collective-permute-start | bytes 393224 | tf_op jit(solution)/shard_map/ppermute | solution.py:17
  14.4 22.9 %slice-start.2 = ((s8[14680064]{0:T(1024)(128)(4,1)}), s8[4194304]{0:T(1024)(128)(4,1)S(1)}, s32[]{:S(2)}) async-start(s8[14680064]{0:T(1024)(128)(4,1)} %bitcast.1), calls=%async_computation.2 | async-start | bytes 8388608
  15.7 6.4 %collective-permute-start.3 = (bf16[16,1920]{1,0:T(8,128)(2,1)S(1)}, bf16[16,1920]{1,0:T(8,128)(2,1)S(1)}, u32[]{:S(2)}, u32[]{:S(2)}) collective-permute-start(bf16[16,1920]{1,0:T(8,128)(2,1)S(1)} %get-tuple-element.42), channel_id=1, source_target_pairs={{0,24},{4,28},{8,16},{12,20},{16,8},{20,12},{24,0},{28,4},{1,25},{... | collective-permute-start | bytes 184328 | tf_op jit(solution)/shard_map/ppermute | solution.py:17
  19.6 5.6 %collective-permute-start.4 = (bf16[16,1920]{1,0:T(8,128)(2,1)S(1)}, bf16[16,1920]{1,0:T(8,128)(2,1)S(1)}, u32[]{:S(2)}, u32[]{:S(2)}) collective-permute-start(bf16[16,1920]{1,0:T(8,128)(2,1)S(1)} %get-tuple-element.43), channel_id=1, source_target_pairs={{0,16},{4,20},{8,24},{12,28},{16,0},{20,4},{24,8},{28,12},{1,17},{... | collective-permute-start | bytes 184328 | tf_op jit(solution)/shard_map/ppermute | solution.py:17
  19.6 5.6 %collective-permute-start.5 = (bf16[16,1920]{1,0:T(8,128)(2,1)S(1)}, bf16[16,1920]{1,0:T(8,128)(2,1)S(1)}, u32[]{:S(2)}, u32[]{:S(2)}) collective-permute-start(bf16[16,1920]{1,0:T(8,128)(2,1)S(1)} %get-tuple-element.44), channel_id=1, source_target_pairs={{0,8},{4,12},{8,0},{12,4},{16,24},{20,28},{24,16},{28,20},{1,9},{5... | collective-permute-start | bytes 184328 | tf_op jit(solution)/shard_map/ppermute | solution.py:17
  25.2 12.1 %slice-start.3 = ((s8[14680064]{0:T(1024)(128)(4,1)}), s8[2097152]{0:T(1024)(128)(4,1)S(1)}, s32[]{:S(2)}) async-start(s8[14680064]{0:T(1024)(128)(4,1)} %bitcast.1), calls=%async_computation.3 | async-start | bytes 4194304
  25.3 4.3 %collective-permute-start.6 = (bf16[16,1920]{1,0:T(8,128)(2,1)S(1)}, bf16[16,1920]{1,0:T(8,128)(2,1)S(1)}, u32[]{:S(2)}, u32[]{:S(2)}) collective-permute-start(bf16[16,1920]{1,0:T(8,128)(2,1)S(1)} %get-tuple-element.46.refs_0_), channel_id=1, source_target_pairs={{0,4},{4,0},{8,12},{12,8},{16,20},{20,16},{24,28},{28,24},{1,5},{5... | collective-permute-start | bytes 184328 | tf_op jit(solution)/shard_map/ppermute | solution.py:17
  29.6 6.4 %collective-permute-start.7 = (bf16[16,1792]{1,0:T(8,128)(2,1)S(1)}, bf16[16,1792]{1,0:T(8,128)(2,1)S(1)}, u32[]{:S(2)}, u32[]{:S(2)}) collective-permute-start(bf16[16,1792]{1,0:T(8,128)(2,1)S(1)} %get-tuple-element.48.refs_3_), channel_id=1, source_target_pairs={{0,24},{4,28},{8,16},{12,20},{16,8},{20,12},{24,0},{28,4},{1,25},{... | collective-permute-start | bytes 172040 | tf_op jit(solution)/shard_map/ppermute | solution.py:17
  32.1 5.1 %collective-permute-start.9 = (bf16[16,1792]{1,0:T(8,128)(2,1)S(1)}, bf16[16,1792]{1,0:T(8,128)(2,1)S(1)}, u32[]{:S(2)}, u32[]{:S(2)}) collective-permute-start(bf16[16,1792]{1,0:T(8,128)(2,1)S(1)} %get-tuple-element.48.refs_3_), channel_id=1, source_target_pairs={{0,16},{4,20},{8,24},{12,28},{16,0},{20,4},{24,8},{28,12},{1,17},{... | collective-permute-start | bytes 172040 | tf_op jit(solution)/shard_map/ppermute | solution.py:17
  32.2 5.0 %collective-permute-start.8 = (bf16[16,1792]{1,0:T(8,128)(2,1)S(1)}, bf16[16,1792]{1,0:T(8,128)(2,1)S(1)}, u32[]{:S(2)}, u32[]{:S(2)}) collective-permute-start(bf16[16,1792]{1,0:T(8,128)(2,1)S(1)} %get-tuple-element.48.refs_3_), channel_id=1, source_target_pairs={{0,8},{4,12},{8,0},{12,4},{16,24},{20,28},{24,16},{28,20},{1,9},{5... | collective-permute-start | bytes 172040 | tf_op jit(solution)/shard_map/ppermute | solution.py:17
  40.0 1.6 %collective-permute-start.10 = (bf16[4,32,1024]{2,1,0:T(8,128)(2,1)S(1)}, bf16[4,32,1024]{2,1,0:T(8,128)(2,1)S(1)}, u32[]{:S(2)}, u32[]{:S(2)}) collective-permute-start(bf16[4,32,1024]{2,1,0:T(8,128)(2,1)S(1)} %get-tuple-element.51.refs_3_), channel_id=1, source_target_pairs={{0,1},{1,0},{2,3},{3,2},{4,5},{5,4},{6,7},{7,6},{8,9},{9,8},{10,11... | collective-permute-start | bytes 786440 | tf_op jit(solution)/shard_map/ppermute | solution.py:17
  41.6 5.9 %collective-permute-start.11 = (bf16[2,32,1024]{2,1,0:T(8,128)(2,1)S(1)}, bf16[2,32,1024]{2,1,0:T(8,128)(2,1)S(1)}, u32[]{:S(2)}, u32[]{:S(2)}) collective-permute-start(bf16[2,32,1024]{2,1,0:T(8,128)(2,1)S(1)} %get-tuple-element.53), channel_id=1, source_target_pairs={{0,2},{1,3},{2,0},{3,1},{4,6},{5,7},{6,4},{7,5},{8,10},{9,11},{10,... | collective-permute-start | bytes 393224 | tf_op jit(solution)/shard_map/ppermute | solution.py:17
  43.2 4.5 %slice-start.8 = ((s8[14680064]{0:T(1024)(128)(4,1)}), s8[4194304]{0:T(1024)(128)(4,1)S(1)}, s32[]{:S(2)}) async-start(s8[14680064]{0:T(1024)(128)(4,1)} %bitcast.5), calls=%async_computation.8 | async-start | bytes 8388608
  43.2 4.5 %slice-start.9 = ((s8[14680064]{0:T(1024)(128)(4,1)}), s8[4194304]{0:T(1024)(128)(4,1)S(1)}, s32[]{:S(2)}) async-start(s8[14680064]{0:T(1024)(128)(4,1)} %bitcast.5), calls=%async_computation.9 | async-start | bytes 8388608
  43.2 4.7 %slice-start.10 = ((s8[14680064]{0:T(1024)(128)(4,1)}), s8[4194304]{0:T(1024)(128)(4,1)S(1)}, s32[]{:S(2)}) async-start(s8[14680064]{0:T(1024)(128)(4,1)} %bitcast.5), calls=%async_computation.10 | async-start | bytes 8388608
  44.6 5.7 %collective-permute-start.13 = (bf16[2,32,1024]{2,1,0:T(8,128)(2,1)S(1)}, bf16[2,32,1024]{2,1,0:T(8,128)(2,1)S(1)}, u32[]{:S(2)}, u32[]{:S(2)}) collective-permute-start(bf16[2,32,1024]{2,1,0:T(8,128)(2,1)S(1)} %get-tuple-element.55), channel_id=1, source_target_pairs={{0,2},{1,3},{2,0},{3,1},{4,6},{5,7},{6,4},{7,5},{8,10},{9,11},{10,... | collective-permute-start | bytes 393224 | tf_op jit(solution)/shard_map/ppermute | solution.py:17
  47.5 1.7 %slice-start.11 = ((s8[14680064]{0:T(1024)(128)(4,1)}), s8[2097152]{0:T(1024)(128)(4,1)S(1)}, s32[]{:S(2)}) async-start(s8[14680064]{0:T(1024)(128)(4,1)} %bitcast.5), calls=%async_computation.11 | async-start | bytes 4194304
  47.6 2.8 %collective-permute-start.12 = (bf16[2,32,512]{2,1,0:T(8,128)(2,1)S(1)}, bf16[2,32,512]{2,1,0:T(8,128)(2,1)S(1)}, u32[]{:S(2)}, u32[]{:S(2)}) collective-permute-start(bf16[2,32,512]{2,1,0:T(8,128)(2,1)S(1)} %act.2.refs_0_), channel_id=1, source_target_pairs={{0,1},{1,0},{2,3},{3,2},{4,5},{5,4},{6,7},{7,6},{8,9},{9,8},{10,11... | collective-permute-start | bytes 196616 | tf_op jit(solution)/shard_map/ppermute | solution.py:17
  50.3 1.6 %collective-permute-start.14 = (bf16[2,32,512]{2,1,0:T(8,128)(2,1)S(1)}, bf16[2,32,512]{2,1,0:T(8,128)(2,1)S(1)}, u32[]{:S(2)}, u32[]{:S(2)}) collective-permute-start(bf16[2,32,512]{2,1,0:T(8,128)(2,1)S(1)} %act.3.refs_2_), channel_id=1, source_target_pairs={{0,1},{1,0},{2,3},{3,2},{4,5},{5,4},{6,7},{7,6},{8,9},{9,8},{10,11... | collective-permute-start | bytes 196616 | tf_op jit(solution)/shard_map/ppermute | solution.py:17
  52.9 6.6 %collective-permute-start.15 = (bf16[16,1792]{1,0:T(8,128)(2,1)S(1)}, bf16[16,1792]{1,0:T(8,128)(2,1)S(1)}, u32[]{:S(2)}, u32[]{:S(2)}) collective-permute-start(bf16[16,1792]{1,0:T(8,128)(2,1)S(1)} %get-tuple-element.60), channel_id=1, source_target_pairs={{0,24},{4,28},{8,16},{12,20},{16,8},{20,12},{24,0},{28,4},{1,25},{... | collective-permute-start | bytes 172040 | tf_op jit(solution)/shard_map/ppermute | solution.py:17
  55.1 6.4 %collective-permute-start.16 = (bf16[16,1792]{1,0:T(8,128)(2,1)S(1)}, bf16[16,1792]{1,0:T(8,128)(2,1)S(1)}, u32[]{:S(2)}, u32[]{:S(2)}) collective-permute-start(bf16[16,1792]{1,0:T(8,128)(2,1)S(1)} %get-tuple-element.61), channel_id=1, source_target_pairs={{0,16},{4,20},{8,24},{12,28},{16,0},{20,4},{24,8},{28,12},{1,17},{... | collective-permute-start | bytes 172040 | tf_op jit(solution)/shard_map/ppermute | solution.py:17
  55.5 6.1 %collective-permute-start.17 = (bf16[16,1792]{1,0:T(8,128)(2,1)S(1)}, bf16[16,1792]{1,0:T(8,128)(2,1)S(1)}, u32[]{:S(2)}, u32[]{:S(2)}) collective-permute-start(bf16[16,1792]{1,0:T(8,128)(2,1)S(1)} %get-tuple-element.62), channel_id=1, source_target_pairs={{0,8},{4,12},{8,0},{12,4},{16,24},{20,28},{24,16},{28,20},{1,9},{5... | collective-permute-start | bytes 172040 | tf_op jit(solution)/shard_map/ppermute | solution.py:17
  61.6 3.9 %collective-permute-start.18 = (bf16[8,1792]{1,0:T(8,128)(2,1)S(1)}, bf16[8,1792]{1,0:T(8,128)(2,1)S(1)}, u32[]{:S(2)}, u32[]{:S(2)}) collective-permute-start(bf16[8,1792]{1,0:T(8,128)(2,1)S(1)} %get-tuple-element.64), channel_id=1, source_target_pairs={{0,4},{4,0},{8,12},{12,8},{16,20},{20,16},{24,28},{28,24},{1,5},{5... | collective-permute-start | bytes 86024 | tf_op jit(solution)/shard_map/ppermute | solution.py:17

commit v5 on v4

--- a/solution.py
+++ b/solution.py
@@ -106,7 +106,7 @@
     copies[2].wait()
 
 
-def attend_body(scale, queries, turned, mine, other, wuv_h, keep, send, wuv, sems):
+def attend_body(scale, queries, turned, mine, other, wuv_h, keep, send, wuv, keys, sems):
     heads, lat, vdim = wuv.shape
     rows = keep.shape[0]
     width = heads * vdim
@@ -114,19 +114,17 @@
     copy = pltpu.make_async_copy(wuv_h.at[pl.ds(first, heads)], wuv, sems.at[0])
     copy.start()
     q, r = queries[...], turned[...]
-    keys = (mine, other)
-    scores = []
-    for k in keys:
-        s = jnp.dot(q, k[:lat], preferred_element_type=F32)
-        scores.append((s + jnp.dot(r, k[lat:], preferred_element_type=F32)) * scale)
-    top = jnp.max(jnp.maximum(*scores), -1, keepdims=True)
-    total, w = 0.0, 0.0
-    for s, k in zip(scores, keys):
-        p = jnp.exp(s - top)
-        total = total + jnp.sum(p, -1, keepdims=True)
-        w = w + lax.dot_general(
-            p.astype(BF16), k[:lat], (((1,), (1,)), ((), ())), preferred_element_type=F32
-        )
+    n = mine.shape[1]
+    keys[:, :n] = mine[...]
+    keys[:, n:] = other[...]
+    s = jnp.dot(q, keys[:lat], preferred_element_type=F32)
+    s = (s + jnp.dot(r, keys[lat:], preferred_element_type=F32)) * scale
+    top = jnp.max(s, -1, keepdims=True)
+    p = jnp.exp(s - top)
+    total = jnp.sum(p, -1, keepdims=True)
+    w = lax.dot_general(
+        p.astype(BF16), keys[:lat], (((1,), (1,)), ((), ())), preferred_element_type=F32
+    )
     w = w * (1.0 / total)
     hi = w.astype(BF16)
     lo = (w - hi.astype(F32)).astype(BF16)
@@ -310,6 +308,19 @@
     half_products(experts, mine, x, gate, up, out)
 
 
+def own_sum_body(experts, x, gate, up, other, keep, send):
+    hid = send.shape[2] // 2
+    cap = send.shape[1]
+    cols = half_cols(hid, True)
+    for i, e in enumerate(experts):
+        xe = x[e * cap : (e + 1) * cap]
+        for j, w in enumerate((gate, up)):
+            at = slice(j * hid, (j + 1) * hid)
+            v = jnp.dot(xe, w[e, :, cols], preferred_element_type=F32) + other[e, :, at].astype(F32)
+            keep[i, :, at] = v
+            send[i, :, at] = v.astype(BF16)
+
+
 def add_body(experts, x, other, keep, send):
     for i, e in enumerate(experts):
         v = x[i] + other[e].astype(F32)
@@ -328,13 +339,13 @@
         out[i] = (gate / (1.0 + jnp.exp(-gate)) * up).astype(BF16)
 
 
-def weigh(experts, cap, mix, parts):
-    result = jnp.concatenate([v.astype(BF16) for v in parts], 0)
-    gain = mix[:, experts[0] * cap : (experts[-1] + 1) * cap]
+def weigh(mix, result):
+    gain = mix[...]
+    rows = gain.shape[0]
     hi = gain.astype(BF16)
     lo = (gain - hi.astype(F32)).astype(BF16)
-    v = jnp.dot(hi, result, preferred_element_type=F32)
-    return v + jnp.dot(lo, result, preferred_element_type=F32)
+    v = jnp.dot(jnp.concatenate([hi, lo], 0), result, preferred_element_type=F32)
+    return v[:rows] + v[rows:]
 
 
 def down_mine_body(experts, mine, down, out):
@@ -343,28 +354,23 @@
         out[i] = jnp.dot(mine[i], down[e, low], preferred_element_type=F32)
 
 
-def down_next_body(experts, later, part, other, mine, down, mix, out, ahead):
+def down_next_body(experts, later, part, other, mine, down, out, ahead):
     low, high = half_cols(mine.shape[2], True), half_cols(mine.shape[2], False)
-    parts = [
-        part[i] + jnp.dot(other[i], down[e, high], preferred_element_type=F32)
-        for i, e in enumerate(experts)
-    ]
+    for i, e in enumerate(experts):
+        v = part[i] + jnp.dot(other[i], down[e, high], preferred_element_type=F32)
+        out[i] = v.astype(BF16)
     for i, e in enumerate(later):
         ahead[i] = jnp.dot(mine[i], down[e, low], preferred_element_type=F32)
-    out[...] = weigh(experts, other.shape[1], mix, parts)
-
-
-def down_last_body(has_before, experts, part, other, down, mix, *refs):
+
+
+def down_last_body(n_before, experts, part, other, down, mix, *refs):
     high = half_cols(other.shape[2], False)
-    parts = [
-        part[i] + jnp.dot(other[i], down[e, high], preferred_element_type=F32)
-        for i, e in enumerate(experts)
-    ]
-    v = weigh(experts, other.shape[1], mix, parts)
-    if has_before:
-        v = v + refs[0][...]
-        refs = refs[1:]
-    keep, *sends = refs
+    parts = [r[i] for r in refs[:n_before] for i in range(r.shape[0])]
+    for i, e in enumerate(experts):
+        v = part[i] + jnp.dot(other[i], down[e, high], preferred_element_type=F32)
+        parts.append(v.astype(BF16))
+    keep, *sends = refs[n_before:]
+    v = weigh(mix, jnp.concatenate(parts, 0))
     n = keep.shape[0]
     keep[...] = v[:n]
     for s, send in enumerate(sends, 1):
@@ -427,7 +433,10 @@
     keep, send = run(
         "attend", bind(attend_body, scale), [((rows, hv + LANES), F32), ((rows, hv + LANES), BF16)],
         [queries, turned, keys, far_keys, w_uv],
-        scratch=[VMEM((heads // 2,) + w_uv.shape[1:], BF16), pltpu.SemaphoreType.DMA((1,))],
+        scratch=[
+            VMEM((heads // 2,) + w_uv.shape[1:], BF16), VMEM((keys.shape[0], 2 * keys.shape[1]), BF16),
+            pltpu.SemaphoreType.DMA((1,)),
+        ],
         us=12, limit=12, hbm=(4,),
     )
     (mine,) = run(
@@ -472,13 +481,18 @@
     other = swap(send, "grp", 1)
     sums = []
     for g in groups:
-        (part,) = run(
-            "own_half", bind(half_body, g, True), [(shape, F32)], [x, gate, up], us=0.5 if sums else 0.5,
-            after=[sums[-1][0] if sums else send],
-        )
-        keep, send = run(
-            "add", bind(add_body, g), [(shape, F32), (shape, BF16)], [part, other], us=0.1
-        )
+        if sums:
+            keep, send = run(
+                "own_sum", bind(own_sum_body, g), [(shape, F32), (shape, BF16)],
+                [x, gate, up, other], us=0.5, after=[sums[-1][0]],
+            )
+        else:
+            (part,) = run(
+                "own_half", bind(half_body, g, True), [(shape, F32)], [x, gate, up], us=0.5, after=[send]
+            )
+            keep, send = run(
+                "add", bind(add_body, g), [(shape, F32), (shape, BF16)], [part, other], us=0.1
+            )
         sums.append((keep, spread(send, "grp")))
     before, later = [], []
     for g, (keep, others) in zip(groups, sums):
@@ -490,8 +504,8 @@
         if later:
             before, part = run(
                 "down_next", bind(down_next_body, groups[0], g),
-                [((rows, width), F32), ((size, cap, width), F32)],
-                [later[0], last_act, act, down, mix], us=1,
+                [((size, cap, width), BF16), ((size, cap, width), F32)],
+                [later[0], last_act, act, down], us=1,
             )
             before = [before]
         else:

time: 66.3 us -> 65.7 us (level)
    pallas_call x20 -> x19, Pallas kernels: 17.5 us -> 16.9 us  [run(): pl.pallas_call(ordered, out_shape=[jax.ShapeDtypeStruct(s, d) for s, d in...]
  transfers between devices with their start and end apart: 19 -> 19, of which waited for: 13 -> 13; matrix products, arithmetic and copies ran while one was open for 0% -> 0% of each run, Pallas kernels for 13% -> 12%
where the time goes in v5:
time: 65.7 us; the launch traced here: 65.6 us
  waiting for transfers between devices  24.8 us (38%)
  starting transfers between devices  22 us (33%)
  Pallas kernels  16.9 us (26%)
  local copies, waits for them, and re-layouts  1.59 us (2%)
    ppermute x19, waiting for transfers between devices, swap(): lax.ppermute(x, axis, [(a, a ^ bits) for a in range(lax.axis_size(axis))])  24.8 us
    ppermute x19, starting transfers between devices, swap(): lax.ppermute(x, axis, [(a, a ^ bits) for a in range(lax.axis_size(axis))])  22 us
    pallas_call x19, Pallas kernels, run(): pl.pallas_call(ordered, out_shape=[jax.ShapeDtypeStruct(s, d) for s, d in...  16.9 us
    unnamed x34, local copies, waits for them, and re-layouts  1.59 us
  transfers between devices with their start and end apart: 19, of which 13 were waited for; matrix products, arithmetic and copies ran while one was open for 0% of the time, Pallas kernels for 12%

profile of v5, /device:TPU:0, one launch (start us, length us, event | category | flops | bytes accessed | tf_op | source)
XLA Modules:
  0.0 65.6 jit_solution(6190726662838600265)
XLA Ops:
  0.0 0.5 collective-permute-start
  0.5 2.0 %queries.1 = (bf16[512,512]{1,0:T(8,128)(2,1)S(1)}, bf16[512,64]{1,0:T(8,128)(2,1)S(1)}, bf16[576,384]{1,0:T(8,128)(2,1)S(1)}) custom-call(bf16[64,16,128]{2,1,0:T(8,128)(2,1)} %refs_0_.1, bf16[64,16,64]{2,1,0:T(8,128)(2,1)} %refs_1_.7, bf16[16,128,512]{2,1,0:T(8,128)(2,1)} %refs_2_.6, bf16[576,384]{1,0:T(8,128)(2,1)} %bitcast.10), custom_call_target="tpu_custom_call" | custom-call | flops 2300000000 | bytes 1024 | tf_op jit(solution)/shard_map/queries/pallas_call | solution.py:42
  2.4 0.0 collective-permute-done.refs_3_
  2.4 0.0 slice-start.13
  2.4 0.0 copy-start
  2.5 0.0 copy-start.1
  2.5 0.0 slice-start.4
  2.5 0.0 slice-start.5
  2.5 0.0 slice-start.6
  2.5 3.2 %attend.1 = (f32[64,1152]{1,0:T(8,128)S(1)}, bf16[64,1152]{1,0:T(8,128)(2,1)S(1)}) custom-call(bf16[512,512]{1,0:T(8,128)(2,1)S(1)} %get-tuple-element.35.refs_0_, bf16[512,64]{1,0:T(8,128)(2,1)S(1)} %get-tuple-element.36.refs_1_, bf16[576,384]{1,0:T(8,128)(2,1)S(1)} %get-tuple-element.37.refs_2_, bf16[576,384]{1,0:T(8,128)(2,1)S(1)} %collective-permute-done.refs_3_, ...), custom_call_target="tpu_custom_call" | custom-call | flops 13799999488 | bytes 1024 | tf_op jit(solution)/shard_map/attend/pallas_call | solution.py:42
  5.7 0.0 copy-start.2
  5.7 2.5 %collective-permute-start.1 = (bf16[64,1152]{1,0:T(8,128)(2,1)S(1)}, bf16[64,1152]{1,0:T(8,128)(2,1)S(1)}, u32[]{:S(2)}, u32[]{:S(2)}) collective-permute-start(bf16[64,1152]{1,0:T(8,128)(2,1)S(1)} %get-tuple-element.39), channel_id=1, source_target_pairs={{0,2},{1,3},{2,0},{3,1},{4,6},{5,7},{6,4},{7,5},{8,10},{9,11},{10,... | collective-permute-start | bytes 442376 | tf_op jit(solution)/shard_map/ppermute | solution.py:17
  8.2 4.5 %collective-permute-done.1.refs_1_ = bf16[64,1152]{1,0:T(8,128)(2,1)S(1)} collective-permute-done((bf16[64,1152]{1,0:T(8,128)(2,1)S(1)}, bf16[64,1152]{1,0:T(8,128)(2,1)S(1)}, u32[]{:S(2)}, u32[]{:S(2)}) %collective-permute-start.1) | collective-permute-done | bytes 147488 | tf_op jit(solution)/shard_map/ppermute | solution.py:17
  12.8 0.3 merge.1.refs_0_
  13.1 0.0 slice-start.1
  13.1 0.0 slice-start.7
  13.1 0.1 collective-permute-start.2
  13.2 0.8 %project_mine.1.refs_0_ = f32[64,1792]{1,0:T(8,128)S(1)} custom-call(bf16[64,1024]{1,0:T(8,128)(2,1)S(1)} %merge.1.refs_0_, bf16[2048,1792]{1,0:T(8,128)(2,1)S(1)} %bitcast.8), custom_call_target="tpu_custom_call" | custom-call | flops 575000000 | bytes 1024 | tf_op jit(solution)/shard_map/project_mine/pallas_call | solution.py:42
  14.0 0.0 slice-start.2
  14.0 0.5 collective-permute-done.2.refs_1_
  14.5 0.8 %project.1 = (f32[16,1792]{1,0:T(8,128)S(1)}, bf16[16,1920]{1,0:T(8,128)(2,1)S(1)}, bf16[16,1920]{1,0:T(8,128)(2,1)S(1)}, bf16[16,1920]{1,0:T(8,128)(2,1)S(1)}, f32[8,128]{1,0:T(8,128)S(1)}) custom-call(f32[64,1792]{1,0:T(8,128)S(1)} %project_mine.1.refs_0_, bf16[64,1024]{1,0:T(8,128)(2,1)S(1)} %collective-permute-done.2.refs_1_, s32[8,8]{1,0:T(8,128)S(1)} %copy-done, ...), custom_call_target="tpu_custom_call" | custom-call | flops 1150000000 | bytes 1024 | tf_op jit(solution)/shard_map/project/pallas_call | solution.py:42
  15.3 3.9 %collective-permute-start.3 = (bf16[16,1920]{1,0:T(8,128)(2,1)S(1)}, bf16[16,1920]{1,0:T(8,128)(2,1)S(1)}, u32[]{:S(2)}, u32[]{:S(2)}) collective-permute-start(bf16[16,1920]{1,0:T(8,128)(2,1)S(1)} %get-tuple-element.42), channel_id=1, source_target_pairs={{0,24},{4,28},{8,16},{12,20},{16,8},{20,12},{24,0},{28,4},{1,25},{... | collective-permute-start | bytes 184328 | tf_op jit(solution)/shard_map/ppermute | solution.py:17
  19.2 0.0 collective-permute-start.4
  19.2 0.6 collective-permute-start.5
  19.9 1.8 %collective-permute-done.3.refs_3_ = bf16[16,1920]{1,0:T(8,128)(2,1)S(1)} collective-permute-done((bf16[16,1920]{1,0:T(8,128)(2,1)S(1)}, bf16[16,1920]{1,0:T(8,128)(2,1)S(1)}, u32[]{:S(2)}, u32[]{:S(2)}) %collective-permute-start.3) | collective-permute-done | bytes 61472 | tf_op jit(solution)/shard_map/ppermute | solution.py:17
  21.7 3.1 %collective-permute-done.4.refs_4_ = bf16[16,1920]{1,0:T(8,128)(2,1)S(1)} collective-permute-done((bf16[16,1920]{1,0:T(8,128)(2,1)S(1)}, bf16[16,1920]{1,0:T(8,128)(2,1)S(1)}, u32[]{:S(2)}, u32[]{:S(2)}) %collective-permute-start.4) | collective-permute-done | bytes 61472 | tf_op jit(solution)/shard_map/ppermute | solution.py:17
  24.8 0.0 collective-permute-done.5.refs_5_
  24.8 0.1 rest_sum.1
  24.9 1.6 %collective-permute-start.6 = (bf16[16,1920]{1,0:T(8,128)(2,1)S(1)}, bf16[16,1920]{1,0:T(8,128)(2,1)S(1)}, u32[]{:S(2)}, u32[]{:S(2)}) collective-permute-start(bf16[16,1920]{1,0:T(8,128)(2,1)S(1)} %get-tuple-element.46.refs_0_), channel_id=1, source_target_pairs={{0,4},{4,0},{8,12},{12,8},{16,20},{20,16},{24,28},{28,24},{1,5},{5... | collective-permute-start | bytes 184328 | tf_op jit(solution)/shard_map/ppermute | solution.py:17
  26.5 2.7 %collective-permute-done.6.refs_1_ = bf16[16,1920]{1,0:T(8,128)(2,1)S(1)} collective-permute-done((bf16[16,1920]{1,0:T(8,128)(2,1)S(1)}, bf16[16,1920]{1,0:T(8,128)(2,1)S(1)}, u32[]{:S(2)}, u32[]{:S(2)}) %collective-permute-start.6) | collective-permute-done | bytes 61472 | tf_op jit(solution)/shard_map/ppermute | solution.py:17
  29.2 2.5 %collective-permute-start.7 = (bf16[16,1792]{1,0:T(8,128)(2,1)S(1)}, bf16[16,1792]{1,0:T(8,128)(2,1)S(1)}, u32[]{:S(2)}, u32[]{:S(2)}) collective-permute-start(bf16[16,1792]{1,0:T(8,128)(2,1)S(1)} %get-tuple-element.48.refs_3_), channel_id=1, source_target_pairs={{0,24},{4,28},{8,16},{12,20},{16,8},{20,12},{24,0},{28,4},{1,25},{... | collective-permute-start | bytes 172040 | tf_op jit(solution)/shard_map/ppermute | solution.py:17
  31.7 0.1 collective-permute-start.9
  31.9 1.8 %collective-permute-start.8 = (bf16[16,1792]{1,0:T(8,128)(2,1)S(1)}, bf16[16,1792]{1,0:T(8,128)(2,1)S(1)}, u32[]{:S(2)}, u32[]{:S(2)}) collective-permute-start(bf16[16,1792]{1,0:T(8,128)(2,1)S(1)} %get-tuple-element.48.refs_3_), channel_id=1, source_target_pairs={{0,8},{4,12},{8,0},{12,4},{16,24},{20,28},{24,16},{28,20},{1,9},{5... | collective-permute-start | bytes 172040 | tf_op jit(solution)/shard_map/ppermute | solution.py:17
  33.6 1.9 %collective-permute-done.7.refs_2_.refs_6_ = bf16[16,1792]{1,0:T(8,128)(2,1)S(1)} collective-permute-done((bf16[16,1792]{1,0:T(8,128)(2,1)S(1)}, bf16[16,1792]{1,0:T(8,128)(2,1)S(1)}, u32[]{:S(2)}, u32[]{:S(2)}) %collective-permute-start.7) | collective-permute-done | bytes 57376 | tf_op jit(solution)/shard_map/ppermute | solution.py:17
  35.5 0.5 route.1
  36.0 0.8 %collective-permute-done.9.refs_5_ = bf16[16,1792]{1,0:T(8,128)(2,1)S(1)} collective-permute-done((bf16[16,1792]{1,0:T(8,128)(2,1)S(1)}, bf16[16,1792]{1,0:T(8,128)(2,1)S(1)}, u32[]{:S(2)}, u32[]{:S(2)}) %collective-permute-start.9) | collective-permute-done | bytes 57376 | tf_op jit(solution)/shard_map/ppermute | solution.py:17
  36.8 0.0 collective-permute-done.8.refs_4_
  36.9 2.8 %other_half.1 = (bf16[128,1792]{1,0:T(8,128)(2,1)S(1)}, bf16[4,32,1024]{2,1,0:T(8,128)(2,1)S(1)}) custom-call(bf16[128,64]{1,0:T(8,128)(2,1)S(1)} %get-tuple-element.49.refs_0_, bf16[4,1792,1024]{2,1,0:T(8,128)(2,1)S(1)} %bitcast.2, bf16[4,1792,1024]{2,1,0:T(8,128)(2,1)S(1)} %bitcast.4, bf16[16,1792]{1,0:T(8,128)(2,1)S(1)} %get-tuple-element.48.refs_3_, ...), custom_call_target="tpu_custom_call" | custom-call | flops 575000000 | bytes 1024 | tf_op jit(solution)/shard_map/other_half/pallas_call | solution.py:42
  39.7 0.0 collective-permute-start.10
  39.7 1.4 %own_half.1.refs_0_ = f32[2,32,1024]{2,1,0:T(8,128)S(1)} custom-call(bf16[128,1792]{1,0:T(8,128)(2,1)S(1)} %get-tuple-element.50.refs_0_, bf16[4,1792,1024]{2,1,0:T(8,128)(2,1)S(1)} %bitcast.2, bf16[4,1792,1024]{2,1,0:T(8,128)(2,1)S(1)} %bitcast.4, bf16[4,32,1024]{2,1,0:T(8,128)(2,1)S(1)} %get-tuple-element.51.refs_3_), custom_call_target="tpu_custom_call" | custom-call | flops 575000000 | bytes 1024 | tf_op jit(solution)/shard_map/own_half/pallas_call | solution.py:42
  41.1 0.2 collective-permute-done.10.refs_1_.refs_3_
  41.3 1.6 %collective-permute-start.11 = (bf16[2,32,1024]{2,1,0:T(8,128)(2,1)S(1)}, bf16[2,32,1024]{2,1,0:T(8,128)(2,1)S(1)}, u32[]{:S(2)}, u32[]{:S(2)}) collective-permute-start(bf16[2,32,1024]{2,1,0:T(8,128)(2,1)S(1)} %get-tuple-element.53), channel_id=1, source_target_pairs={{0,2},{1,3},{2,0},{3,1},{4,6},{5,7},{6,4},{7,5},{8,10},{9,11},{10,... | collective-permute-start | bytes 393224 | tf_op jit(solution)/shard_map/ppermute | solution.py:17
  42.8 1.3 %own_sum.1 = (f32[2,32,1024]{2,1,0:T(8,128)S(1)}, bf16[2,32,1024]{2,1,0:T(8,128)(2,1)S(1)}) custom-call(bf16[128,1792]{1,0:T(8,128)(2,1)S(1)} %get-tuple-element.50.refs_0_, bf16[4,1792,1024]{2,1,0:T(8,128)(2,1)S(1)} %bitcast.2, bf16[4,1792,1024]{2,1,0:T(8,128)(2,1)S(1)} %bitcast.4, bf16[4,32,1024]{2,1,0:T(8,128)(2,1)S(1)} %collective-permute-done.10.refs_1_.refs_3_, ...), custom_call_target="tpu_custom_call" | custom-call | flops 575000000 | bytes 1024 | tf_op jit(solution)/shard_map/own_sum/pallas_call | solution.py:42
  44.2 0.6 collective-permute-start.13
  44.8 2.4 %collective-permute-done.11.refs_1_ = bf16[2,32,1024]{2,1,0:T(8,128)(2,1)S(1)} collective-permute-done((bf16[2,32,1024]{2,1,0:T(8,128)(2,1)S(1)}, bf16[2,32,1024]{2,1,0:T(8,128)(2,1)S(1)}, u32[]{:S(2)}, u32[]{:S(2)}) %collective-permute-start.11) | collective-permute-done | bytes 131104 | tf_op jit(solution)/shard_map/ppermute | solution.py:17
  47.2 0.1 act.2.refs_0_
  47.2 0.1 collective-permute-start.12
  47.3 0.1 slice-done.10
  47.5 1.4 %slice-done.11 = s8[2097152]{0:T(1024)(128)(4,1)S(1)} async-done(((s8[14680064]{0:T(1024)(128)(4,1)}), s8[2097152]{0:T(1024)(128)(4,1)S(1)}, s32[]{:S(2)}) %slice-start.11) | async-done | bytes 2097176
  48.8 0.7 %down_mine.1.refs_2_.refs_0_ = f32[2,32,1792]{2,1,0:T(8,128)S(1)} custom-call(bf16[2,32,512]{2,1,0:T(8,128)(2,1)S(1)} %act.2.refs_0_, bf16[4,1024,1792]{2,1,0:T(8,128)(2,1)S(1)} %bitcast.6), custom_call_target="tpu_custom_call" | custom-call | flops 575000000 | bytes 1024 | tf_op jit(solution)/shard_map/down_mine/pallas_call | solution.py:42
  49.6 0.3 collective-permute-done.13.refs_1_
  49.9 0.1 act.3.refs_2_
  50.0 0.1 collective-permute-start.14
  50.1 1.4 %down_next.1 = (bf16[2,32,1792]{2,1,0:T(8,128)(2,1)S(1)}, f32[2,32,1792]{2,1,0:T(8,128)S(1)}) custom-call(f32[2,32,1792]{2,1,0:T(8,128)S(1)} %down_mine.1.refs_2_.refs_0_, bf16[2,32,512]{2,1,0:T(8,128)(2,1)S(1)} %collective-permute-done.12.refs_1_, bf16[2,32,512]{2,1,0:T(8,128)(2,1)S(1)} %act.3.refs_2_, bf16[4,1024,1792]{2,1,0:T(8,128)(2,1)S(1)} %bitcast.6), custom_call_target="tpu_custom_call" | custom-call | flops 1150000000 | bytes 1024 | tf_op jit(solution)/shard_map/down_next/pallas_call | solution.py:42
  51.4 0.0 collective-permute-done.14.refs_1_
  51.4 0.9 %down_last.1 = (f32[16,1792]{1,0:T(8,128)S(1)}, bf16[16,1792]{1,0:T(8,128)(2,1)S(1)}, bf16[16,1792]{1,0:T(8,128)(2,1)S(1)}, bf16[16,1792]{1,0:T(8,128)(2,1)S(1)}) custom-call(f32[2,32,1792]{2,1,0:T(8,128)S(1)} %get-tuple-element.56.refs_0_, bf16[2,32,512]{2,1,0:T(8,128)(2,1)S(1)} %collective-permute-done.14.refs_1_, bf16[4,1024,1792]{2,1,0:T(8,128)(2,1)S(1)} %bitcast.6, ...), custom_call_target="tpu_custom_call" | custom-call | flops 1150000000 | bytes 1024 | tf_op jit(solution)/shard_map/down_last/pallas_call | solution.py:42
  52.4 2.2 %collective-permute-start.15 = (bf16[16,1792]{1,0:T(8,128)(2,1)S(1)}, bf16[16,1792]{1,0:T(8,128)(2,1)S(1)}, u32[]{:S(2)}, u32[]{:S(2)}) collective-permute-start(bf16[16,1792]{1,0:T(8,128)(2,1)S(1)} %get-tuple-element.60), channel_id=1, source_target_pairs={{0,24},{4,28},{8,16},{12,20},{16,8},{20,12},{24,0},{28,4},{1,25},{... | collective-permute-start | bytes 172040 | tf_op jit(solution)/shard_map/ppermute | solution.py:17
  54.5 0.4 collective-permute-start.16
  54.9 1.9 %collective-permute-start.17 = (bf16[16,1792]{1,0:T(8,128)(2,1)S(1)}, bf16[16,1792]{1,0:T(8,128)(2,1)S(1)}, u32[]{:S(2)}, u32[]{:S(2)}) collective-permute-start(bf16[16,1792]{1,0:T(8,128)(2,1)S(1)} %get-tuple-element.62), channel_id=1, source_target_pairs={{0,8},{4,12},{8,0},{12,4},{16,24},{20,28},{24,16},{28,20},{1,9},{5... | collective-permute-start | bytes 172040 | tf_op jit(solution)/shard_map/ppermute | solution.py:17
  56.8 2.2 %collective-permute-done.15.refs_1_ = bf16[16,1792]{1,0:T(8,128)(2,1)S(1)} collective-permute-done((bf16[16,1792]{1,0:T(8,128)(2,1)S(1)}, bf16[16,1792]{1,0:T(8,128)(2,1)S(1)}, u32[]{:S(2)}, u32[]{:S(2)}) %collective-permute-start.15) | collective-permute-done | bytes 57376 | tf_op jit(solution)/shard_map/ppermute | solution.py:17
  59.0 2.0 %collective-permute-done.16.refs_2_ = bf16[16,1792]{1,0:T(8,128)(2,1)S(1)} collective-permute-done((bf16[16,1792]{1,0:T(8,128)(2,1)S(1)}, bf16[16,1792]{1,0:T(8,128)(2,1)S(1)}, u32[]{:S(2)}, u32[]{:S(2)}) %collective-permute-start.16) | collective-permute-done | bytes 57376 | tf_op jit(solution)/shard_map/ppermute | solution.py:17
  61.0 1.6 %collective-permute-start.18 = (bf16[8,1792]{1,0:T(8,128)(2,1)S(1)}, bf16[8,1792]{1,0:T(8,128)(2,1)S(1)}, u32[]{:S(2)}, u32[]{:S(2)}) collective-permute-start(bf16[8,1792]{1,0:T(8,128)(2,1)S(1)} %get-tuple-element.64), channel_id=1, source_target_pairs={{0,4},{4,0},{8,12},{12,8},{16,20},{20,16},{24,28},{28,24},{1,5},{5... | collective-permute-start | bytes 86024 | tf_op jit(solution)/shard_map/ppermute | solution.py:17
  62.6 2.4 %collective-permute-done.18.refs_2_ = bf16[8,1792]{1,0:T(8,128)(2,1)S(1)} collective-permute-done((bf16[8,1792]{1,0:T(8,128)(2,1)S(1)}, bf16[8,1792]{1,0:T(8,128)(2,1)S(1)}, u32[]{:S(2)}, u32[]{:S(2)}) %collective-permute-start.18) | collective-permute-done | bytes 28704 | tf_op jit(solution)/shard_map/ppermute | solution.py:17
  65.0 0.6 out.1
  (31 shorter events, 0.1 us)
Async XLA Ops:
  0.0 2.4 %collective-permute-start = (bf16[576,384]{1,0:T(8,128)(2,1)}, bf16[576,384]{1,0:T(8,128)(2,1)S(1)}, u32[]{:S(2)}, u32[]{:S(2)}) collective-permute-start(bf16[576,384]{1,0:T(8,128)(2,1)} %bitcast.9), channel_id=1, source_target_pairs={{0,1},{1,0},{2,3},{3,2},{4,5},{5,4},{6,7},{7,6},{8,9},{9,8},{10,11... | collective-permute-start | bytes 1327112 | tf_op jit(solution)/shard_map/ppermute | solution.py:17
  0.5 12.7 %slice-start.12 = ((s8[7340032]{0:T(1024)(128)(4,1)}), s8[4194304]{0:T(1024)(128)(4,1)S(1)}, s32[]{:S(2)}) async-start(s8[7340032]{0:T(1024)(128)(4,1)} %bitcast.7), calls=%async_computation.12 | async-start | bytes 8388608
  2.4 10.8 %slice-start.13 = ((s8[7340032]{0:T(1024)(128)(4,1)}), s8[3145728]{0:T(1024)(128)(4,1)S(1)}, s32[]{:S(2)}) async-start(s8[7340032]{0:T(1024)(128)(4,1)} %bitcast.7), calls=%async_computation.13 | async-start | bytes 6291456
  2.4 12.1 %copy-start = (s32[8,8]{1,0:T(8,128)S(1)}, s32[8,8]{1,0:T(8,128)}, u32[]{:S(2)}) copy-start(s32[8,8]{1,0:T(8,128)} %refs_2_.7) | copy-start | bytes 772
  2.5 12.1 %copy-start.1 = (f32[8,8]{1,0:T(8,128)S(1)}, f32[8,8]{1,0:T(8,128)}, u32[]{:S(2)}) copy-start(f32[8,8]{1,0:T(8,128)} %refs_3_.2) | copy-start | bytes 772
  2.5 34.3 %slice-start.4 = ((s8[14680064]{0:T(1024)(128)(4,1)}), s8[4194304]{0:T(1024)(128)(4,1)S(1)}, s32[]{:S(2)}) async-start(s8[14680064]{0:T(1024)(128)(4,1)} %bitcast.3), calls=%async_computation.4 | async-start | bytes 8388608
  2.5 34.3 %slice-start.5 = ((s8[14680064]{0:T(1024)(128)(4,1)}), s8[4194304]{0:T(1024)(128)(4,1)S(1)}, s32[]{:S(2)}) async-start(s8[14680064]{0:T(1024)(128)(4,1)} %bitcast.3), calls=%async_computation.5 | async-start | bytes 8388608
  2.5 34.3 %slice-start.6 = ((s8[14680064]{0:T(1024)(128)(4,1)}), s8[4194304]{0:T(1024)(128)(4,1)S(1)}, s32[]{:S(2)}) async-start(s8[14680064]{0:T(1024)(128)(4,1)} %bitcast.3), calls=%async_computation.6 | async-start | bytes 8388608
  5.7 19.1 %copy-start.2 = (bf16[8,1792]{1,0:T(8,128)(2,1)S(1)}, bf16[8,1792]{1,0:T(8,128)(2,1)}, u32[]{:S(2)}) copy-start(bf16[8,1792]{1,0:T(8,128)(2,1)} %refs_1_.9) | copy-start | bytes 86020
  5.7 7.1 %collective-permute-start.1 = (bf16[64,1152]{1,0:T(8,128)(2,1)S(1)}, bf16[64,1152]{1,0:T(8,128)(2,1)S(1)}, u32[]{:S(2)}, u32[]{:S(2)}) collective-permute-start(bf16[64,1152]{1,0:T(8,128)(2,1)S(1)} %get-tuple-element.39), channel_id=1, source_target_pairs={{0,2},{1,3},{2,0},{3,1},{4,6},{5,7},{6,4},{7,5},{8,10},{9,11},{10,... | collective-permute-start | bytes 442376 | tf_op jit(solution)/shard_map/ppermute | solution.py:17
  12.8 24.1 %slice-start = ((s8[14680064]{0:T(1024)(128)(4,1)}), s8[4194304]{0:T(1024)(128)(4,1)S(1)}, s32[]{:S(2)}) async-start(s8[14680064]{0:T(1024)(128)(4,1)} %bitcast.1), calls=%async_computation | async-start | bytes 8388608
  13.1 23.8 %slice-start.1 = ((s8[14680064]{0:T(1024)(128)(4,1)}), s8[4194304]{0:T(1024)(128)(4,1)S(1)}, s32[]{:S(2)}) async-start(s8[14680064]{0:T(1024)(128)(4,1)} %bitcast.1), calls=%async_computation.1 | async-start | bytes 8388608
  13.1 23.8 %slice-start.7 = ((s8[14680064]{0:T(1024)(128)(4,1)}), s8[2097152]{0:T(1024)(128)(4,1)S(1)}, s32[]{:S(2)}) async-start(s8[14680064]{0:T(1024)(128)(4,1)} %bitcast.3), calls=%async_computation.7 | async-start | bytes 4194304
  13.1 1.4 %collective-permute-start.2 = (bf16[64,1024]{1,0:T(8,128)(2,1)S(1)}, bf16[64,1024]{1,0:T(8,128)(2,1)S(1)}, u32[]{:S(2)}, u32[]{:S(2)}) collective-permute-start(bf16[64,1024]{1,0:T(8,128)(2,1)S(1)} %merge.1.refs_0_), channel_id=1, source_target_pairs={{0,1},{1,0},{2,3},{3,2},{4,5},{5,4},{6,7},{7,6},{8,9},{9,8},{10,11... | collective-permute-start | bytes 393224 | tf_op jit(solution)/shard_map/ppermute | solution.py:17
  14.0 22.9 %slice-start.2 = ((s8[14680064]{0:T(1024)(128)(4,1)}), s8[4194304]{0:T(1024)(128)(4,1)S(1)}, s32[]{:S(2)}) async-start(s8[14680064]{0:T(1024)(128)(4,1)} %bitcast.1), calls=%async_computation.2 | async-start | bytes 8388608
  15.3 6.4 %collective-permute-start.3 = (bf16[16,1920]{1,0:T(8,128)(2,1)S(1)}, bf16[16,1920]{1,0:T(8,128)(2,1)S(1)}, u32[]{:S(2)}, u32[]{:S(2)}) collective-permute-start(bf16[16,1920]{1,0:T(8,128)(2,1)S(1)} %get-tuple-element.42), channel_id=1, source_target_pairs={{0,24},{4,28},{8,16},{12,20},{16,8},{20,12},{24,0},{28,4},{1,25},{... | collective-permute-start | bytes 184328 | tf_op jit(solution)/shard_map/ppermute | solution.py:17
  19.2 5.6 %collective-permute-start.4 = (bf16[16,1920]{1,0:T(8,128)(2,1)S(1)}, bf16[16,1920]{1,0:T(8,128)(2,1)S(1)}, u32[]{:S(2)}, u32[]{:S(2)}) collective-permute-start(bf16[16,1920]{1,0:T(8,128)(2,1)S(1)} %get-tuple-element.43), channel_id=1, source_target_pairs={{0,16},{4,20},{8,24},{12,28},{16,0},{20,4},{24,8},{28,12},{1,17},{... | collective-permute-start | bytes 184328 | tf_op jit(solution)/shard_map/ppermute | solution.py:17
  19.2 5.6 %collective-permute-start.5 = (bf16[16,1920]{1,0:T(8,128)(2,1)S(1)}, bf16[16,1920]{1,0:T(8,128)(2,1)S(1)}, u32[]{:S(2)}, u32[]{:S(2)}) collective-permute-start(bf16[16,1920]{1,0:T(8,128)(2,1)S(1)} %get-tuple-element.44), channel_id=1, source_target_pairs={{0,8},{4,12},{8,0},{12,4},{16,24},{20,28},{24,16},{28,20},{1,9},{5... | collective-permute-start | bytes 184328 | tf_op jit(solution)/shard_map/ppermute | solution.py:17
  24.8 12.0 %slice-start.3 = ((s8[14680064]{0:T(1024)(128)(4,1)}), s8[2097152]{0:T(1024)(128)(4,1)S(1)}, s32[]{:S(2)}) async-start(s8[14680064]{0:T(1024)(128)(4,1)} %bitcast.1), calls=%async_computation.3 | async-start | bytes 4194304
  24.9 4.3 %collective-permute-start.6 = (bf16[16,1920]{1,0:T(8,128)(2,1)S(1)}, bf16[16,1920]{1,0:T(8,128)(2,1)S(1)}, u32[]{:S(2)}, u32[]{:S(2)}) collective-permute-start(bf16[16,1920]{1,0:T(8,128)(2,1)S(1)} %get-tuple-element.46.refs_0_), channel_id=1, source_target_pairs={{0,4},{4,0},{8,12},{12,8},{16,20},{20,16},{24,28},{28,24},{1,5},{5... | collective-permute-start | bytes 184328 | tf_op jit(solution)/shard_map/ppermute | solution.py:17
  29.2 6.3 %collective-permute-start.7 = (bf16[16,1792]{1,0:T(8,128)(2,1)S(1)}, bf16[16,1792]{1,0:T(8,128)(2,1)S(1)}, u32[]{:S(2)}, u32[]{:S(2)}) collective-permute-start(bf16[16,1792]{1,0:T(8,128)(2,1)S(1)} %get-tuple-element.48.refs_3_), channel_id=1, source_target_pairs={{0,24},{4,28},{8,16},{12,20},{16,8},{20,12},{24,0},{28,4},{1,25},{... | collective-permute-start | bytes 172040 | tf_op jit(solution)/shard_map/ppermute | solution.py:17
  31.7 5.1 %collective-permute-start.9 = (bf16[16,1792]{1,0:T(8,128)(2,1)S(1)}, bf16[16,1792]{1,0:T(8,128)(2,1)S(1)}, u32[]{:S(2)}, u32[]{:S(2)}) collective-permute-start(bf16[16,1792]{1,0:T(8,128)(2,1)S(1)} %get-tuple-element.48.refs_3_), channel_id=1, source_target_pairs={{0,16},{4,20},{8,24},{12,28},{16,0},{20,4},{24,8},{28,12},{1,17},{... | collective-permute-start | bytes 172040 | tf_op jit(solution)/shard_map/ppermute | solution.py:17
  31.9 4.9 %collective-permute-start.8 = (bf16[16,1792]{1,0:T(8,128)(2,1)S(1)}, bf16[16,1792]{1,0:T(8,128)(2,1)S(1)}, u32[]{:S(2)}, u32[]{:S(2)}) collective-permute-start(bf16[16,1792]{1,0:T(8,128)(2,1)S(1)} %get-tuple-element.48.refs_3_), channel_id=1, source_target_pairs={{0,8},{4,12},{8,0},{12,4},{16,24},{20,28},{24,16},{28,20},{1,9},{5... | collective-permute-start | bytes 172040 | tf_op jit(solution)/shard_map/ppermute | solution.py:17
  39.7 1.6 %collective-permute-start.10 = (bf16[4,32,1024]{2,1,0:T(8,128)(2,1)S(1)}, bf16[4,32,1024]{2,1,0:T(8,128)(2,1)S(1)}, u32[]{:S(2)}, u32[]{:S(2)}) collective-permute-start(bf16[4,32,1024]{2,1,0:T(8,128)(2,1)S(1)} %get-tuple-element.51.refs_3_), channel_id=1, source_target_pairs={{0,1},{1,0},{2,3},{3,2},{4,5},{5,4},{6,7},{7,6},{8,9},{9,8},{10,11... | collective-permute-start | bytes 786440 | tf_op jit(solution)/shard_map/ppermute | solution.py:17
  41.3 5.9 %collective-permute-start.11 = (bf16[2,32,1024]{2,1,0:T(8,128)(2,1)S(1)}, bf16[2,32,1024]{2,1,0:T(8,128)(2,1)S(1)}, u32[]{:S(2)}, u32[]{:S(2)}) collective-permute-start(bf16[2,32,1024]{2,1,0:T(8,128)(2,1)S(1)} %get-tuple-element.53), channel_id=1, source_target_pairs={{0,2},{1,3},{2,0},{3,1},{4,6},{5,7},{6,4},{7,5},{8,10},{9,11},{10,... | collective-permute-start | bytes 393224 | tf_op jit(solution)/shard_map/ppermute | solution.py:17
  42.8 4.5 %slice-start.8 = ((s8[14680064]{0:T(1024)(128)(4,1)}), s8[4194304]{0:T(1024)(128)(4,1)S(1)}, s32[]{:S(2)}) async-start(s8[14680064]{0:T(1024)(128)(4,1)} %bitcast.5), calls=%async_computation.8 | async-start | bytes 8388608
  42.8 4.5 %slice-start.9 = ((s8[14680064]{0:T(1024)(128)(4,1)}), s8[4194304]{0:T(1024)(128)(4,1)S(1)}, s32[]{:S(2)}) async-start(s8[14680064]{0:T(1024)(128)(4,1)} %bitcast.5), calls=%async_computation.9 | async-start | bytes 8388608
  42.8 4.7 %slice-start.10 = ((s8[14680064]{0:T(1024)(128)(4,1)}), s8[4194304]{0:T(1024)(128)(4,1)S(1)}, s32[]{:S(2)}) async-start(s8[14680064]{0:T(1024)(128)(4,1)} %bitcast.5), calls=%async_computation.10 | async-start | bytes 8388608
  44.2 5.7 %collective-permute-start.13 = (bf16[2,32,1024]{2,1,0:T(8,128)(2,1)S(1)}, bf16[2,32,1024]{2,1,0:T(8,128)(2,1)S(1)}, u32[]{:S(2)}, u32[]{:S(2)}) collective-permute-start(bf16[2,32,1024]{2,1,0:T(8,128)(2,1)S(1)} %get-tuple-element.55), channel_id=1, source_target_pairs={{0,2},{1,3},{2,0},{3,1},{4,6},{5,7},{6,4},{7,5},{8,10},{9,11},{10,... | collective-permute-start | bytes 393224 | tf_op jit(solution)/shard_map/ppermute | solution.py:17
  47.2 1.7 %slice-start.11 = ((s8[14680064]{0:T(1024)(128)(4,1)}), s8[2097152]{0:T(1024)(128)(4,1)S(1)}, s32[]{:S(2)}) async-start(s8[14680064]{0:T(1024)(128)(4,1)} %bitcast.5), calls=%async_computation.11 | async-start | bytes 4194304
  47.2 2.8 %collective-permute-start.12 = (bf16[2,32,512]{2,1,0:T(8,128)(2,1)S(1)}, bf16[2,32,512]{2,1,0:T(8,128)(2,1)S(1)}, u32[]{:S(2)}, u32[]{:S(2)}) collective-permute-start(bf16[2,32,512]{2,1,0:T(8,128)(2,1)S(1)} %act.2.refs_0_), channel_id=1, source_target_pairs={{0,1},{1,0},{2,3},{3,2},{4,5},{5,4},{6,7},{7,6},{8,9},{9,8},{10,11... | collective-permute-start | bytes 196616 | tf_op jit(solution)/shard_map/ppermute | solution.py:17
  50.0 1.5 %collective-permute-start.14 = (bf16[2,32,512]{2,1,0:T(8,128)(2,1)S(1)}, bf16[2,32,512]{2,1,0:T(8,128)(2,1)S(1)}, u32[]{:S(2)}, u32[]{:S(2)}) collective-permute-start(bf16[2,32,512]{2,1,0:T(8,128)(2,1)S(1)} %act.3.refs_2_), channel_id=1, source_target_pairs={{0,1},{1,0},{2,3},{3,2},{4,5},{5,4},{6,7},{7,6},{8,9},{9,8},{10,11... | collective-permute-start | bytes 196616 | tf_op jit(solution)/shard_map/ppermute | solution.py:17
  52.4 6.6 %collective-permute-start.15 = (bf16[16,1792]{1,0:T(8,128)(2,1)S(1)}, bf16[16,1792]{1,0:T(8,128)(2,1)S(1)}, u32[]{:S(2)}, u32[]{:S(2)}) collective-permute-start(bf16[16,1792]{1,0:T(8,128)(2,1)S(1)} %get-tuple-element.60), channel_id=1, source_target_pairs={{0,24},{4,28},{8,16},{12,20},{16,8},{20,12},{24,0},{28,4},{1,25},{... | collective-permute-start | bytes 172040 | tf_op jit(solution)/shard_map/ppermute | solution.py:17
  54.5 6.4 %collective-permute-start.16 = (bf16[16,1792]{1,0:T(8,128)(2,1)S(1)}, bf16[16,1792]{1,0:T(8,128)(2,1)S(1)}, u32[]{:S(2)}, u32[]{:S(2)}) collective-permute-start(bf16[16,1792]{1,0:T(8,128)(2,1)S(1)} %get-tuple-element.61), channel_id=1, source_target_pairs={{0,16},{4,20},{8,24},{12,28},{16,0},{20,4},{24,8},{28,12},{1,17},{... | collective-permute-start | bytes 172040 | tf_op jit(solution)/shard_map/ppermute | solution.py:17
  54.9 6.1 %collective-permute-start.17 = (bf16[16,1792]{1,0:T(8,128)(2,1)S(1)}, bf16[16,1792]{1,0:T(8,128)(2,1)S(1)}, u32[]{:S(2)}, u32[]{:S(2)}) collective-permute-start(bf16[16,1792]{1,0:T(8,128)(2,1)S(1)} %get-tuple-element.62), channel_id=1, source_target_pairs={{0,8},{4,12},{8,0},{12,4},{16,24},{20,28},{24,16},{28,20},{1,9},{5... | collective-permute-start | bytes 172040 | tf_op jit(solution)/shard_map/ppermute | solution.py:17
  61.0 3.9 %collective-permute-start.18 = (bf16[8,1792]{1,0:T(8,128)(2,1)S(1)}, bf16[8,1792]{1,0:T(8,128)(2,1)S(1)}, u32[]{:S(2)}, u32[]{:S(2)}) collective-permute-start(bf16[8,1792]{1,0:T(8,128)(2,1)S(1)} %get-tuple-element.64), channel_id=1, source_target_pairs={{0,4},{4,0},{8,12},{12,8},{16,20},{20,16},{24,28},{28,24},{1,5},{5... | collective-permute-start | bytes 86024 | tf_op jit(solution)/shard_map/ppermute | solution.py:17

commit v6 on v5

--- a/solution.py
+++ b/solution.py
@@ -125,17 +125,15 @@
     w = lax.dot_general(
         p.astype(BF16), keys[:lat], (((1,), (1,)), ((), ())), preferred_element_type=F32
     )
-    w = w * (1.0 / total)
-    hi = w.astype(BF16)
-    lo = (w - hi.astype(F32)).astype(BF16)
+    w = w.astype(BF16)
+    share = 1.0 / total
     level = top + jnp.log(total)
     lane = lax.broadcasted_iota(jnp.int32, (rows, LANES), 1)
     lse = jnp.zeros((rows, LANES), F32)
     copy.wait()
     for h in range(heads):
         at = slice(h * rows, (h + 1) * rows)
-        v = jnp.dot(jnp.concatenate([hi[at], lo[at]], 0), wuv[h], preferred_element_type=F32)
-        v = v[:rows] + v[rows:]
+        v = jnp.dot(w[at], wuv[h], preferred_element_type=F32) * share[at]
         keep[:, h * vdim : (h + 1) * vdim] = v
         send[:, h * vdim : (h + 1) * vdim] = v.astype(BF16)
         lse = jnp.where(lane == h, level[at], lse)
@@ -481,23 +479,19 @@
     other = swap(send, "grp", 1)
     sums = []
     for g in groups:
-        if sums:
-            keep, send = run(
-                "own_sum", bind(own_sum_body, g), [(shape, F32), (shape, BF16)],
-                [x, gate, up, other], us=0.5, after=[sums[-1][0]],
-            )
-        else:
-            (part,) = run(
-                "own_half", bind(half_body, g, True), [(shape, F32)], [x, gate, up], us=0.5, after=[send]
-            )
-            keep, send = run(
-                "add", bind(add_body, g), [(shape, F32), (shape, BF16)], [part, other], us=0.1
-            )
+        (part,) = run(
+            "own_half", bind(half_body, g, True), [(shape, F32)], [x, gate, up], us=5 if sums else 0.5,
+            after=[sums[-1][0] if sums else send],
+        )
+        keep, send = run(
+            "add", bind(add_body, g), [(shape, F32), (shape, BF16)], [part, other],
+            us=1 if sums else 0.1,
+        )
         sums.append((keep, spread(send, "grp")))
     before, later = [], []
     for g, (keep, others) in zip(groups, sums):
         (act,) = run(
-            "act", act_body, [((size, cap, hid), BF16)], [keep] + others, us=5,
+            "act", act_body, [((size, cap, hid), BF16)], [keep] + others, us=1.5,
             after=later or [sums[-1][0]],
         )
         other_act = swap(act, "grp", 1)

time: 65.7 us -> 65.4 us (level)
    pallas_call x19 -> x20, Pallas kernels: 16.9 us -> 16.6 us  [run(): pl.pallas_call(ordered, out_shape=[jax.ShapeDtypeStruct(s, d) for s, d in...]
  transfers between devices with their start and end apart: 19 -> 19, of which waited for: 13 -> 13; matrix products, arithmetic and copies ran while one was open for 0% -> 0% of each run, Pallas kernels for 12% -> 13%
where the time goes in v6:
time: 65.4 us; the launch traced here: 65.3 us
  waiting for transfers between devices  25.2 us (39%)
  starting transfers between devices  22 us (34%)
  Pallas kernels  16.6 us (25%)
  local copies, waits for them, and re-layouts  1.09 us (2%)
    ppermute x19, waiting for transfers between devices, swap(): lax.ppermute(x, axis, [(a, a ^ bits) for a in range(lax.axis_size(axis))])  25.2 us
    ppermute x19, starting transfers between devices, swap(): lax.ppermute(x, axis, [(a, a ^ bits) for a in range(lax.axis_size(axis))])  22 us
    pallas_call x20, Pallas kernels, run(): pl.pallas_call(ordered, out_shape=[jax.ShapeDtypeStruct(s, d) for s, d in...  16.6 us
  transfers between devices with their start and end apart: 19, of which 13 were waited for; matrix products, arithmetic and copies ran while one was open for 0% of the time, Pallas kernels for 13%

profile of v6, /device:TPU:0, one launch (start us, length us, event | category | flops | bytes accessed | tf_op | source)
XLA Modules:
  0.0 65.3 jit_solution(13518303441988057235)
XLA Ops:
  0.0 0.5 collective-permute-start
  0.5 2.0 %queries.1 = (bf16[512,512]{1,0:T(8,128)(2,1)S(1)}, bf16[512,64]{1,0:T(8,128)(2,1)S(1)}, bf16[576,384]{1,0:T(8,128)(2,1)S(1)}) custom-call(bf16[64,16,128]{2,1,0:T(8,128)(2,1)} %refs_0_.1, bf16[64,16,64]{2,1,0:T(8,128)(2,1)} %refs_1_.7, bf16[16,128,512]{2,1,0:T(8,128)(2,1)} %refs_2_.6, bf16[576,384]{1,0:T(8,128)(2,1)} %bitcast.10), custom_call_target="tpu_custom_call" | custom-call | flops 2300000000 | bytes 1024 | tf_op jit(solution)/shard_map/queries/pallas_call | solution.py:42
  2.4 0.0 slice-start.13
  2.4 0.0 copy-start
  2.5 0.0 copy-start.1
  2.5 0.0 slice-start.4
  2.5 0.0 slice-start.5
  2.5 0.0 slice-start.6
  2.5 2.9 %attend.1 = (f32[64,1152]{1,0:T(8,128)S(1)}, bf16[64,1152]{1,0:T(8,128)(2,1)S(1)}) custom-call(bf16[512,512]{1,0:T(8,128)(2,1)S(1)} %get-tuple-element.35.refs_0_, bf16[512,64]{1,0:T(8,128)(2,1)S(1)} %get-tuple-element.36.refs_1_, bf16[576,384]{1,0:T(8,128)(2,1)S(1)} %get-tuple-element.37.refs_2_, bf16[576,384]{1,0:T(8,128)(2,1)S(1)} %collective-permute-done.refs_3_, ...), custom_call_target="tpu_custom_call" | custom-call | flops 13799999488 | bytes 1024 | tf_op jit(solution)/shard_map/attend/pallas_call | solution.py:42
  5.4 0.0 copy-start.2
  5.4 2.5 %collective-permute-start.1 = (bf16[64,1152]{1,0:T(8,128)(2,1)S(1)}, bf16[64,1152]{1,0:T(8,128)(2,1)S(1)}, u32[]{:S(2)}, u32[]{:S(2)}) collective-permute-start(bf16[64,1152]{1,0:T(8,128)(2,1)S(1)} %get-tuple-element.39), channel_id=1, source_target_pairs={{0,2},{1,3},{2,0},{3,1},{4,6},{5,7},{6,4},{7,5},{8,10},{9,11},{10,... | collective-permute-start | bytes 442376 | tf_op jit(solution)/shard_map/ppermute | solution.py:17
  8.0 4.5 %collective-permute-done.1.refs_1_ = bf16[64,1152]{1,0:T(8,128)(2,1)S(1)} collective-permute-done((bf16[64,1152]{1,0:T(8,128)(2,1)S(1)}, bf16[64,1152]{1,0:T(8,128)(2,1)S(1)}, u32[]{:S(2)}, u32[]{:S(2)}) %collective-permute-start.1) | collective-permute-done | bytes 147488 | tf_op jit(solution)/shard_map/ppermute | solution.py:17
  12.5 0.3 merge.1.refs_0_
  12.8 0.0 slice-start.1
  12.8 0.0 slice-start.7
  12.8 0.1 collective-permute-start.2
  12.9 0.8 %project_mine.1.refs_0_ = f32[64,1792]{1,0:T(8,128)S(1)} custom-call(bf16[64,1024]{1,0:T(8,128)(2,1)S(1)} %merge.1.refs_0_, bf16[2048,1792]{1,0:T(8,128)(2,1)S(1)} %bitcast.8), custom_call_target="tpu_custom_call" | custom-call | flops 575000000 | bytes 1024 | tf_op jit(solution)/shard_map/project_mine/pallas_call | solution.py:42
  13.7 0.0 slice-start.2
  13.7 0.5 collective-permute-done.2.refs_1_
  14.2 0.8 %project.1 = (f32[16,1792]{1,0:T(8,128)S(1)}, bf16[16,1920]{1,0:T(8,128)(2,1)S(1)}, bf16[16,1920]{1,0:T(8,128)(2,1)S(1)}, bf16[16,1920]{1,0:T(8,128)(2,1)S(1)}, f32[8,128]{1,0:T(8,128)S(1)}) custom-call(f32[64,1792]{1,0:T(8,128)S(1)} %project_mine.1.refs_0_, bf16[64,1024]{1,0:T(8,128)(2,1)S(1)} %collective-permute-done.2.refs_1_, s32[8,8]{1,0:T(8,128)S(1)} %copy-done, ...), custom_call_target="tpu_custom_call" | custom-call | flops 1150000000 | bytes 1024 | tf_op jit(solution)/shard_map/project/pallas_call | solution.py:42
  15.0 3.9 %collective-permute-start.3 = (bf16[16,1920]{1,0:T(8,128)(2,1)S(1)}, bf16[16,1920]{1,0:T(8,128)(2,1)S(1)}, u32[]{:S(2)}, u32[]{:S(2)}) collective-permute-start(bf16[16,1920]{1,0:T(8,128)(2,1)S(1)} %get-tuple-element.42), channel_id=1, source_target_pairs={{0,24},{4,28},{8,16},{12,20},{16,8},{20,12},{24,0},{28,4},{1,25},{... | collective-permute-start | bytes 184328 | tf_op jit(solution)/shard_map/ppermute | solution.py:17
  18.9 0.0 collective-permute-start.4
  19.0 0.6 collective-permute-start.5
  19.6 1.8 %collective-permute-done.3.refs_3_ = bf16[16,1920]{1,0:T(8,128)(2,1)S(1)} collective-permute-done((bf16[16,1920]{1,0:T(8,128)(2,1)S(1)}, bf16[16,1920]{1,0:T(8,128)(2,1)S(1)}, u32[]{:S(2)}, u32[]{:S(2)}) %collective-permute-start.3) | collective-permute-done | bytes 61472 | tf_op jit(solution)/shard_map/ppermute | solution.py:17
  21.4 3.1 %collective-permute-done.4.refs_4_ = bf16[16,1920]{1,0:T(8,128)(2,1)S(1)} collective-permute-done((bf16[16,1920]{1,0:T(8,128)(2,1)S(1)}, bf16[16,1920]{1,0:T(8,128)(2,1)S(1)}, u32[]{:S(2)}, u32[]{:S(2)}) %collective-permute-start.4) | collective-permute-done | bytes 61472 | tf_op jit(solution)/shard_map/ppermute | solution.py:17
  24.5 0.0 collective-permute-done.5.refs_5_
  24.5 0.1 rest_sum.1
  24.6 1.6 %collective-permute-start.6 = (bf16[16,1920]{1,0:T(8,128)(2,1)S(1)}, bf16[16,1920]{1,0:T(8,128)(2,1)S(1)}, u32[]{:S(2)}, u32[]{:S(2)}) collective-permute-start(bf16[16,1920]{1,0:T(8,128)(2,1)S(1)} %get-tuple-element.46.refs_0_), channel_id=1, source_target_pairs={{0,4},{4,0},{8,12},{12,8},{16,20},{20,16},{24,28},{28,24},{1,5},{5... | collective-permute-start | bytes 184328 | tf_op jit(solution)/shard_map/ppermute | solution.py:17
  26.2 2.7 %collective-permute-done.6.refs_1_ = bf16[16,1920]{1,0:T(8,128)(2,1)S(1)} collective-permute-done((bf16[16,1920]{1,0:T(8,128)(2,1)S(1)}, bf16[16,1920]{1,0:T(8,128)(2,1)S(1)}, u32[]{:S(2)}, u32[]{:S(2)}) %collective-permute-start.6) | collective-permute-done | bytes 61472 | tf_op jit(solution)/shard_map/ppermute | solution.py:17
  28.9 2.5 %collective-permute-start.7 = (bf16[16,1792]{1,0:T(8,128)(2,1)S(1)}, bf16[16,1792]{1,0:T(8,128)(2,1)S(1)}, u32[]{:S(2)}, u32[]{:S(2)}) collective-permute-start(bf16[16,1792]{1,0:T(8,128)(2,1)S(1)} %get-tuple-element.48.refs_3_), channel_id=1, source_target_pairs={{0,24},{4,28},{8,16},{12,20},{16,8},{20,12},{24,0},{28,4},{1,25},{... | collective-permute-start | bytes 172040 | tf_op jit(solution)/shard_map/ppermute | solution.py:17
  31.4 0.1 collective-permute-start.9
  31.6 1.8 %collective-permute-start.8 = (bf16[16,1792]{1,0:T(8,128)(2,1)S(1)}, bf16[16,1792]{1,0:T(8,128)(2,1)S(1)}, u32[]{:S(2)}, u32[]{:S(2)}) collective-permute-start(bf16[16,1792]{1,0:T(8,128)(2,1)S(1)} %get-tuple-element.48.refs_3_), channel_id=1, source_target_pairs={{0,8},{4,12},{8,0},{12,4},{16,24},{20,28},{24,16},{28,20},{1,9},{5... | collective-permute-start | bytes 172040 | tf_op jit(solution)/shard_map/ppermute | solution.py:17
  33.4 1.9 %collective-permute-done.7.refs_2_.refs_6_ = bf16[16,1792]{1,0:T(8,128)(2,1)S(1)} collective-permute-done((bf16[16,1792]{1,0:T(8,128)(2,1)S(1)}, bf16[16,1792]{1,0:T(8,128)(2,1)S(1)}, u32[]{:S(2)}, u32[]{:S(2)}) %collective-permute-start.7) | collective-permute-done | bytes 57376 | tf_op jit(solution)/shard_map/ppermute | solution.py:17
  35.3 0.5 route.1
  35.8 0.7 %collective-permute-done.9.refs_5_ = bf16[16,1792]{1,0:T(8,128)(2,1)S(1)} collective-permute-done((bf16[16,1792]{1,0:T(8,128)(2,1)S(1)}, bf16[16,1792]{1,0:T(8,128)(2,1)S(1)}, u32[]{:S(2)}, u32[]{:S(2)}) %collective-permute-start.9) | collective-permute-done | bytes 57376 | tf_op jit(solution)/shard_map/ppermute | solution.py:17
  36.5 0.0 collective-permute-done.8.refs_4_
  36.6 2.8 %other_half.1 = (bf16[128,1792]{1,0:T(8,128)(2,1)S(1)}, bf16[4,32,1024]{2,1,0:T(8,128)(2,1)S(1)}) custom-call(bf16[128,64]{1,0:T(8,128)(2,1)S(1)} %get-tuple-element.49.refs_0_, bf16[4,1792,1024]{2,1,0:T(8,128)(2,1)S(1)} %bitcast.2, bf16[4,1792,1024]{2,1,0:T(8,128)(2,1)S(1)} %bitcast.4, bf16[16,1792]{1,0:T(8,128)(2,1)S(1)} %get-tuple-element.48.refs_3_, ...), custom_call_target="tpu_custom_call" | custom-call | flops 575000000 | bytes 1024 | tf_op jit(solution)/shard_map/other_half/pallas_call | solution.py:42
  39.4 0.0 collective-permute-start.10
  39.4 1.4 %own_half.2.refs_0_ = f32[2,32,1024]{2,1,0:T(8,128)S(1)} custom-call(bf16[128,1792]{1,0:T(8,128)(2,1)S(1)} %get-tuple-element.50.refs_0_, bf16[4,1792,1024]{2,1,0:T(8,128)(2,1)S(1)} %bitcast.2, bf16[4,1792,1024]{2,1,0:T(8,128)(2,1)S(1)} %bitcast.4, bf16[4,32,1024]{2,1,0:T(8,128)(2,1)S(1)} %get-tuple-element.51.refs_3_), custom_call_target="tpu_custom_call" | custom-call | flops 575000000 | bytes 1024 | tf_op jit(solution)/shard_map/own_half/pallas_call | solution.py:42
  40.8 0.2 collective-permute-done.10.refs_1_
  41.0 1.6 %collective-permute-start.11 = (bf16[2,32,1024]{2,1,0:T(8,128)(2,1)S(1)}, bf16[2,32,1024]{2,1,0:T(8,128)(2,1)S(1)}, u32[]{:S(2)}, u32[]{:S(2)}) collective-permute-start(bf16[2,32,1024]{2,1,0:T(8,128)(2,1)S(1)} %get-tuple-element.53), channel_id=1, source_target_pairs={{0,2},{1,3},{2,0},{3,1},{4,6},{5,7},{6,4},{7,5},{8,10},{9,11},{10,... | collective-permute-start | bytes 393224 | tf_op jit(solution)/shard_map/ppermute | solution.py:17
  42.5 1.3 %own_half.3.refs_0_ = f32[2,32,1024]{2,1,0:T(8,128)S(1)} custom-call(bf16[128,1792]{1,0:T(8,128)(2,1)S(1)} %get-tuple-element.50.refs_0_, bf16[4,1792,1024]{2,1,0:T(8,128)(2,1)S(1)} %bitcast.2, bf16[4,1792,1024]{2,1,0:T(8,128)(2,1)S(1)} %bitcast.4, f32[2,32,1024]{2,1,0:T(8,128)S(1)} %get-tuple-element.52.refs_3_.refs_0_), custom_call_target="tpu_custom_call" | custom-call | flops 5750000128 | bytes 1024 | tf_op jit(solution)/shard_map/own_half/pallas_call | solution.py:42
  43.9 0.6 collective-permute-start.13
  44.5 2.3 %collective-permute-done.11.refs_1_ = bf16[2,32,1024]{2,1,0:T(8,128)(2,1)S(1)} collective-permute-done((bf16[2,32,1024]{2,1,0:T(8,128)(2,1)S(1)}, bf16[2,32,1024]{2,1,0:T(8,128)(2,1)S(1)}, u32[]{:S(2)}, u32[]{:S(2)}) %collective-permute-start.11) | collective-permute-done | bytes 131104 | tf_op jit(solution)/shard_map/ppermute | solution.py:17
  46.8 0.1 act.2.refs_0_
  46.9 0.1 collective-permute-start.12
  47.0 0.2 slice-done.10
  47.2 0.8 %slice-done.11 = s8[2097152]{0:T(1024)(128)(4,1)S(1)} async-done(((s8[14680064]{0:T(1024)(128)(4,1)}), s8[2097152]{0:T(1024)(128)(4,1)S(1)}, s32[]{:S(2)}) %slice-start.11) | async-done | bytes 2097176
  48.0 0.7 %down_mine.1.refs_2_.refs_0_ = f32[2,32,1792]{2,1,0:T(8,128)S(1)} custom-call(bf16[2,32,512]{2,1,0:T(8,128)(2,1)S(1)} %act.2.refs_0_, bf16[4,1024,1792]{2,1,0:T(8,128)(2,1)S(1)} %bitcast.6), custom_call_target="tpu_custom_call" | custom-call | flops 575000000 | bytes 1024 | tf_op jit(solution)/shard_map/down_mine/pallas_call | solution.py:42
  48.7 0.9 %collective-permute-done.13.refs_1_ = bf16[2,32,1024]{2,1,0:T(8,128)(2,1)S(1)} collective-permute-done((bf16[2,32,1024]{2,1,0:T(8,128)(2,1)S(1)}, bf16[2,32,1024]{2,1,0:T(8,128)(2,1)S(1)}, u32[]{:S(2)}, u32[]{:S(2)}) %collective-permute-start.13) | collective-permute-done | bytes 131104 | tf_op jit(solution)/shard_map/ppermute | solution.py:17
  49.6 0.1 act.3.refs_2_
  49.7 0.1 collective-permute-start.14
  49.8 0.0 collective-permute-done.12.refs_1_
  49.8 1.4 %down_next.1 = (bf16[2,32,1792]{2,1,0:T(8,128)(2,1)S(1)}, f32[2,32,1792]{2,1,0:T(8,128)S(1)}) custom-call(f32[2,32,1792]{2,1,0:T(8,128)S(1)} %down_mine.1.refs_2_.refs_0_, bf16[2,32,512]{2,1,0:T(8,128)(2,1)S(1)} %collective-permute-done.12.refs_1_, bf16[2,32,512]{2,1,0:T(8,128)(2,1)S(1)} %act.3.refs_2_, bf16[4,1024,1792]{2,1,0:T(8,128)(2,1)S(1)} %bitcast.6), custom_call_target="tpu_custom_call" | custom-call | flops 1150000000 | bytes 1024 | tf_op jit(solution)/shard_map/down_next/pallas_call | solution.py:42
  51.1 0.0 collective-permute-done.14.refs_1_
  51.1 0.9 %down_last.1 = (f32[16,1792]{1,0:T(8,128)S(1)}, bf16[16,1792]{1,0:T(8,128)(2,1)S(1)}, bf16[16,1792]{1,0:T(8,128)(2,1)S(1)}, bf16[16,1792]{1,0:T(8,128)(2,1)S(1)}) custom-call(f32[2,32,1792]{2,1,0:T(8,128)S(1)} %get-tuple-element.56.refs_0_, bf16[2,32,512]{2,1,0:T(8,128)(2,1)S(1)} %collective-permute-done.14.refs_1_, bf16[4,1024,1792]{2,1,0:T(8,128)(2,1)S(1)} %bitcast.6, ...), custom_call_target="tpu_custom_call" | custom-call | flops 1150000000 | bytes 1024 | tf_op jit(solution)/shard_map/down_last/pallas_call | solution.py:42
  52.1 2.2 %collective-permute-start.15 = (bf16[16,1792]{1,0:T(8,128)(2,1)S(1)}, bf16[16,1792]{1,0:T(8,128)(2,1)S(1)}, u32[]{:S(2)}, u32[]{:S(2)}) collective-permute-start(bf16[16,1792]{1,0:T(8,128)(2,1)S(1)} %get-tuple-element.60), channel_id=1, source_target_pairs={{0,24},{4,28},{8,16},{12,20},{16,8},{20,12},{24,0},{28,4},{1,25},{... | collective-permute-start | bytes 172040 | tf_op jit(solution)/shard_map/ppermute | solution.py:17
  54.2 0.3 collective-permute-start.16
  54.6 1.9 %collective-permute-start.17 = (bf16[16,1792]{1,0:T(8,128)(2,1)S(1)}, bf16[16,1792]{1,0:T(8,128)(2,1)S(1)}, u32[]{:S(2)}, u32[]{:S(2)}) collective-permute-start(bf16[16,1792]{1,0:T(8,128)(2,1)S(1)} %get-tuple-element.62), channel_id=1, source_target_pairs={{0,8},{4,12},{8,0},{12,4},{16,24},{20,28},{24,16},{28,20},{1,9},{5... | collective-permute-start | bytes 172040 | tf_op jit(solution)/shard_map/ppermute | solution.py:17
  56.5 2.2 %collective-permute-done.15.refs_1_ = bf16[16,1792]{1,0:T(8,128)(2,1)S(1)} collective-permute-done((bf16[16,1792]{1,0:T(8,128)(2,1)S(1)}, bf16[16,1792]{1,0:T(8,128)(2,1)S(1)}, u32[]{:S(2)}, u32[]{:S(2)}) %collective-permute-start.15) | collective-permute-done | bytes 57376 | tf_op jit(solution)/shard_map/ppermute | solution.py:17
  58.7 2.0 %collective-permute-done.16.refs_2_ = bf16[16,1792]{1,0:T(8,128)(2,1)S(1)} collective-permute-done((bf16[16,1792]{1,0:T(8,128)(2,1)S(1)}, bf16[16,1792]{1,0:T(8,128)(2,1)S(1)}, u32[]{:S(2)}, u32[]{:S(2)}) %collective-permute-start.16) | collective-permute-done | bytes 57376 | tf_op jit(solution)/shard_map/ppermute | solution.py:17
  60.7 1.6 %collective-permute-start.18 = (bf16[8,1792]{1,0:T(8,128)(2,1)S(1)}, bf16[8,1792]{1,0:T(8,128)(2,1)S(1)}, u32[]{:S(2)}, u32[]{:S(2)}) collective-permute-start(bf16[8,1792]{1,0:T(8,128)(2,1)S(1)} %get-tuple-element.64), channel_id=1, source_target_pairs={{0,4},{4,0},{8,12},{12,8},{16,20},{20,16},{24,28},{28,24},{1,5},{5... | collective-permute-start | bytes 86024 | tf_op jit(solution)/shard_map/ppermute | solution.py:17
  62.3 2.4 %collective-permute-done.18.refs_2_ = bf16[8,1792]{1,0:T(8,128)(2,1)S(1)} collective-permute-done((bf16[8,1792]{1,0:T(8,128)(2,1)S(1)}, bf16[8,1792]{1,0:T(8,128)(2,1)S(1)}, u32[]{:S(2)}, u32[]{:S(2)}) %collective-permute-start.18) | collective-permute-done | bytes 28704 | tf_op jit(solution)/shard_map/ppermute | solution.py:17
  64.7 0.6 out.1
  (32 shorter events, 0.2 us)
Async XLA Ops:
  0.0 2.4 %collective-permute-start = (bf16[576,384]{1,0:T(8,128)(2,1)}, bf16[576,384]{1,0:T(8,128)(2,1)S(1)}, u32[]{:S(2)}, u32[]{:S(2)}) collective-permute-start(bf16[576,384]{1,0:T(8,128)(2,1)} %bitcast.9), channel_id=1, source_target_pairs={{0,1},{1,0},{2,3},{3,2},{4,5},{5,4},{6,7},{7,6},{8,9},{9,8},{10,11... | collective-permute-start | bytes 1327112 | tf_op jit(solution)/shard_map/ppermute | solution.py:17
  0.5 12.5 %slice-start.12 = ((s8[7340032]{0:T(1024)(128)(4,1)}), s8[4194304]{0:T(1024)(128)(4,1)S(1)}, s32[]{:S(2)}) async-start(s8[7340032]{0:T(1024)(128)(4,1)} %bitcast.7), calls=%async_computation.12 | async-start | bytes 8388608
  2.4 10.5 %slice-start.13 = ((s8[7340032]{0:T(1024)(128)(4,1)}), s8[3145728]{0:T(1024)(128)(4,1)S(1)}, s32[]{:S(2)}) async-start(s8[7340032]{0:T(1024)(128)(4,1)} %bitcast.7), calls=%async_computation.13 | async-start | bytes 6291456
  2.4 11.8 %copy-start = (s32[8,8]{1,0:T(8,128)S(1)}, s32[8,8]{1,0:T(8,128)}, u32[]{:S(2)}) copy-start(s32[8,8]{1,0:T(8,128)} %refs_2_.7) | copy-start | bytes 772
  2.5 11.8 %copy-start.1 = (f32[8,8]{1,0:T(8,128)S(1)}, f32[8,8]{1,0:T(8,128)}, u32[]{:S(2)}) copy-start(f32[8,8]{1,0:T(8,128)} %refs_3_.2) | copy-start | bytes 772
  2.5 34.1 %slice-start.4 = ((s8[14680064]{0:T(1024)(128)(4,1)}), s8[4194304]{0:T(1024)(128)(4,1)S(1)}, s32[]{:S(2)}) async-start(s8[14680064]{0:T(1024)(128)(4,1)} %bitcast.3), calls=%async_computation.4 | async-start | bytes 8388608
  2.5 34.1 %slice-start.5 = ((s8[14680064]{0:T(1024)(128)(4,1)}), s8[4194304]{0:T(1024)(128)(4,1)S(1)}, s32[]{:S(2)}) async-start(s8[14680064]{0:T(1024)(128)(4,1)} %bitcast.3), calls=%async_computation.5 | async-start | bytes 8388608
  2.5 34.0 %slice-start.6 = ((s8[14680064]{0:T(1024)(128)(4,1)}), s8[4194304]{0:T(1024)(128)(4,1)S(1)}, s32[]{:S(2)}) async-start(s8[14680064]{0:T(1024)(128)(4,1)} %bitcast.3), calls=%async_computation.6 | async-start | bytes 8388608
  5.4 19.1 %copy-start.2 = (bf16[8,1792]{1,0:T(8,128)(2,1)S(1)}, bf16[8,1792]{1,0:T(8,128)(2,1)}, u32[]{:S(2)}) copy-start(bf16[8,1792]{1,0:T(8,128)(2,1)} %refs_1_.9) | copy-start | bytes 86020
  5.4 7.1 %collective-permute-start.1 = (bf16[64,1152]{1,0:T(8,128)(2,1)S(1)}, bf16[64,1152]{1,0:T(8,128)(2,1)S(1)}, u32[]{:S(2)}, u32[]{:S(2)}) collective-permute-start(bf16[64,1152]{1,0:T(8,128)(2,1)S(1)} %get-tuple-element.39), channel_id=1, source_target_pairs={{0,2},{1,3},{2,0},{3,1},{4,6},{5,7},{6,4},{7,5},{8,10},{9,11},{10,... | collective-permute-start | bytes 442376 | tf_op jit(solution)/shard_map/ppermute | solution.py:17
  12.5 24.1 %slice-start = ((s8[14680064]{0:T(1024)(128)(4,1)}), s8[4194304]{0:T(1024)(128)(4,1)S(1)}, s32[]{:S(2)}) async-start(s8[14680064]{0:T(1024)(128)(4,1)} %bitcast.1), calls=%async_computation | async-start | bytes 8388608
  12.8 23.8 %slice-start.1 = ((s8[14680064]{0:T(1024)(128)(4,1)}), s8[4194304]{0:T(1024)(128)(4,1)S(1)}, s32[]{:S(2)}) async-start(s8[14680064]{0:T(1024)(128)(4,1)} %bitcast.1), calls=%async_computation.1 | async-start | bytes 8388608
  12.8 23.8 %slice-start.7 = ((s8[14680064]{0:T(1024)(128)(4,1)}), s8[2097152]{0:T(1024)(128)(4,1)S(1)}, s32[]{:S(2)}) async-start(s8[14680064]{0:T(1024)(128)(4,1)} %bitcast.3), calls=%async_computation.7 | async-start | bytes 4194304
  12.8 1.4 %collective-permute-start.2 = (bf16[64,1024]{1,0:T(8,128)(2,1)S(1)}, bf16[64,1024]{1,0:T(8,128)(2,1)S(1)}, u32[]{:S(2)}, u32[]{:S(2)}) collective-permute-start(bf16[64,1024]{1,0:T(8,128)(2,1)S(1)} %merge.1.refs_0_), channel_id=1, source_target_pairs={{0,1},{1,0},{2,3},{3,2},{4,5},{5,4},{6,7},{7,6},{8,9},{9,8},{10,11... | collective-permute-start | bytes 393224 | tf_op jit(solution)/shard_map/ppermute | solution.py:17
  13.7 22.9 %slice-start.2 = ((s8[14680064]{0:T(1024)(128)(4,1)}), s8[4194304]{0:T(1024)(128)(4,1)S(1)}, s32[]{:S(2)}) async-start(s8[14680064]{0:T(1024)(128)(4,1)} %bitcast.1), calls=%async_computation.2 | async-start | bytes 8388608
  15.0 6.4 %collective-permute-start.3 = (bf16[16,1920]{1,0:T(8,128)(2,1)S(1)}, bf16[16,1920]{1,0:T(8,128)(2,1)S(1)}, u32[]{:S(2)}, u32[]{:S(2)}) collective-permute-start(bf16[16,1920]{1,0:T(8,128)(2,1)S(1)} %get-tuple-element.42), channel_id=1, source_target_pairs={{0,24},{4,28},{8,16},{12,20},{16,8},{20,12},{24,0},{28,4},{1,25},{... | collective-permute-start | bytes 184328 | tf_op jit(solution)/shard_map/ppermute | solution.py:17
  18.9 5.6 %collective-permute-start.4 = (bf16[16,1920]{1,0:T(8,128)(2,1)S(1)}, bf16[16,1920]{1,0:T(8,128)(2,1)S(1)}, u32[]{:S(2)}, u32[]{:S(2)}) collective-permute-start(bf16[16,1920]{1,0:T(8,128)(2,1)S(1)} %get-tuple-element.43), channel_id=1, source_target_pairs={{0,16},{4,20},{8,24},{12,28},{16,0},{20,4},{24,8},{28,12},{1,17},{... | collective-permute-start | bytes 184328 | tf_op jit(solution)/shard_map/ppermute | solution.py:17
  19.0 5.6 %collective-permute-start.5 = (bf16[16,1920]{1,0:T(8,128)(2,1)S(1)}, bf16[16,1920]{1,0:T(8,128)(2,1)S(1)}, u32[]{:S(2)}, u32[]{:S(2)}) collective-permute-start(bf16[16,1920]{1,0:T(8,128)(2,1)S(1)} %get-tuple-element.44), channel_id=1, source_target_pairs={{0,8},{4,12},{8,0},{12,4},{16,24},{20,28},{24,16},{28,20},{1,9},{5... | collective-permute-start | bytes 184328 | tf_op jit(solution)/shard_map/ppermute | solution.py:17
  24.5 12.0 %slice-start.3 = ((s8[14680064]{0:T(1024)(128)(4,1)}), s8[2097152]{0:T(1024)(128)(4,1)S(1)}, s32[]{:S(2)}) async-start(s8[14680064]{0:T(1024)(128)(4,1)} %bitcast.1), calls=%async_computation.3 | async-start | bytes 4194304
  24.6 4.3 %collective-permute-start.6 = (bf16[16,1920]{1,0:T(8,128)(2,1)S(1)}, bf16[16,1920]{1,0:T(8,128)(2,1)S(1)}, u32[]{:S(2)}, u32[]{:S(2)}) collective-permute-start(bf16[16,1920]{1,0:T(8,128)(2,1)S(1)} %get-tuple-element.46.refs_0_), channel_id=1, source_target_pairs={{0,4},{4,0},{8,12},{12,8},{16,20},{20,16},{24,28},{28,24},{1,5},{5... | collective-permute-start | bytes 184328 | tf_op jit(solution)/shard_map/ppermute | solution.py:17
  28.9 6.4 %collective-permute-start.7 = (bf16[16,1792]{1,0:T(8,128)(2,1)S(1)}, bf16[16,1792]{1,0:T(8,128)(2,1)S(1)}, u32[]{:S(2)}, u32[]{:S(2)}) collective-permute-start(bf16[16,1792]{1,0:T(8,128)(2,1)S(1)} %get-tuple-element.48.refs_3_), channel_id=1, source_target_pairs={{0,24},{4,28},{8,16},{12,20},{16,8},{20,12},{24,0},{28,4},{1,25},{... | collective-permute-start | bytes 172040 | tf_op jit(solution)/shard_map/ppermute | solution.py:17
  31.4 5.1 %collective-permute-start.9 = (bf16[16,1792]{1,0:T(8,128)(2,1)S(1)}, bf16[16,1792]{1,0:T(8,128)(2,1)S(1)}, u32[]{:S(2)}, u32[]{:S(2)}) collective-permute-start(bf16[16,1792]{1,0:T(8,128)(2,1)S(1)} %get-tuple-element.48.refs_3_), channel_id=1, source_target_pairs={{0,16},{4,20},{8,24},{12,28},{16,0},{20,4},{24,8},{28,12},{1,17},{... | collective-permute-start | bytes 172040 | tf_op jit(solution)/shard_map/ppermute | solution.py:17
  31.6 4.9 %collective-permute-start.8 = (bf16[16,1792]{1,0:T(8,128)(2,1)S(1)}, bf16[16,1792]{1,0:T(8,128)(2,1)S(1)}, u32[]{:S(2)}, u32[]{:S(2)}) collective-permute-start(bf16[16,1792]{1,0:T(8,128)(2,1)S(1)} %get-tuple-element.48.refs_3_), channel_id=1, source_target_pairs={{0,8},{4,12},{8,0},{12,4},{16,24},{20,28},{24,16},{28,20},{1,9},{5... | collective-permute-start | bytes 172040 | tf_op jit(solution)/shard_map/ppermute | solution.py:17
  39.4 1.6 %collective-permute-start.10 = (bf16[4,32,1024]{2,1,0:T(8,128)(2,1)S(1)}, bf16[4,32,1024]{2,1,0:T(8,128)(2,1)S(1)}, u32[]{:S(2)}, u32[]{:S(2)}) collective-permute-start(bf16[4,32,1024]{2,1,0:T(8,128)(2,1)S(1)} %get-tuple-element.51.refs_3_), channel_id=1, source_target_pairs={{0,1},{1,0},{2,3},{3,2},{4,5},{5,4},{6,7},{7,6},{8,9},{9,8},{10,11... | collective-permute-start | bytes 786440 | tf_op jit(solution)/shard_map/ppermute | solution.py:17
  41.0 5.9 %collective-permute-start.11 = (bf16[2,32,1024]{2,1,0:T(8,128)(2,1)S(1)}, bf16[2,32,1024]{2,1,0:T(8,128)(2,1)S(1)}, u32[]{:S(2)}, u32[]{:S(2)}) collective-permute-start(bf16[2,32,1024]{2,1,0:T(8,128)(2,1)S(1)} %get-tuple-element.53), channel_id=1, source_target_pairs={{0,2},{1,3},{2,0},{3,1},{4,6},{5,7},{6,4},{7,5},{8,10},{9,11},{10,... | collective-permute-start | bytes 393224 | tf_op jit(solution)/shard_map/ppermute | solution.py:17
  42.5 4.4 %slice-start.8 = ((s8[14680064]{0:T(1024)(128)(4,1)}), s8[4194304]{0:T(1024)(128)(4,1)S(1)}, s32[]{:S(2)}) async-start(s8[14680064]{0:T(1024)(128)(4,1)} %bitcast.5), calls=%async_computation.8 | async-start | bytes 8388608
  42.5 4.5 %slice-start.9 = ((s8[14680064]{0:T(1024)(128)(4,1)}), s8[4194304]{0:T(1024)(128)(4,1)S(1)}, s32[]{:S(2)}) async-start(s8[14680064]{0:T(1024)(128)(4,1)} %bitcast.5), calls=%async_computation.9 | async-start | bytes 8388608
  42.5 4.7 %slice-start.10 = ((s8[14680064]{0:T(1024)(128)(4,1)}), s8[4194304]{0:T(1024)(128)(4,1)S(1)}, s32[]{:S(2)}) async-start(s8[14680064]{0:T(1024)(128)(4,1)} %bitcast.5), calls=%async_computation.10 | async-start | bytes 8388608
  43.9 4.1 %slice-start.11 = ((s8[14680064]{0:T(1024)(128)(4,1)}), s8[2097152]{0:T(1024)(128)(4,1)S(1)}, s32[]{:S(2)}) async-start(s8[14680064]{0:T(1024)(128)(4,1)} %bitcast.5), calls=%async_computation.11 | async-start | bytes 4194304
  43.9 5.7 %collective-permute-start.13 = (bf16[2,32,1024]{2,1,0:T(8,128)(2,1)S(1)}, bf16[2,32,1024]{2,1,0:T(8,128)(2,1)S(1)}, u32[]{:S(2)}, u32[]{:S(2)}) collective-permute-start(bf16[2,32,1024]{2,1,0:T(8,128)(2,1)S(1)} %get-tuple-element.55), channel_id=1, source_target_pairs={{0,2},{1,3},{2,0},{3,1},{4,6},{5,7},{6,4},{7,5},{8,10},{9,11},{10,... | collective-permute-start | bytes 393224 | tf_op jit(solution)/shard_map/ppermute | solution.py:17
  46.9 2.9 %collective-permute-start.12 = (bf16[2,32,512]{2,1,0:T(8,128)(2,1)S(1)}, bf16[2,32,512]{2,1,0:T(8,128)(2,1)S(1)}, u32[]{:S(2)}, u32[]{:S(2)}) collective-permute-start(bf16[2,32,512]{2,1,0:T(8,128)(2,1)S(1)} %act.2.refs_0_), channel_id=1, source_target_pairs={{0,1},{1,0},{2,3},{3,2},{4,5},{5,4},{6,7},{7,6},{8,9},{9,8},{10,11... | collective-permute-start | bytes 196616 | tf_op jit(solution)/shard_map/ppermute | solution.py:17
  49.7 1.5 %collective-permute-start.14 = (bf16[2,32,512]{2,1,0:T(8,128)(2,1)S(1)}, bf16[2,32,512]{2,1,0:T(8,128)(2,1)S(1)}, u32[]{:S(2)}, u32[]{:S(2)}) collective-permute-start(bf16[2,32,512]{2,1,0:T(8,128)(2,1)S(1)} %act.3.refs_2_), channel_id=1, source_target_pairs={{0,1},{1,0},{2,3},{3,2},{4,5},{5,4},{6,7},{7,6},{8,9},{9,8},{10,11... | collective-permute-start | bytes 196616 | tf_op jit(solution)/shard_map/ppermute | solution.py:17
  52.1 6.6 %collective-permute-start.15 = (bf16[16,1792]{1,0:T(8,128)(2,1)S(1)}, bf16[16,1792]{1,0:T(8,128)(2,1)S(1)}, u32[]{:S(2)}, u32[]{:S(2)}) collective-permute-start(bf16[16,1792]{1,0:T(8,128)(2,1)S(1)} %get-tuple-element.60), channel_id=1, source_target_pairs={{0,24},{4,28},{8,16},{12,20},{16,8},{20,12},{24,0},{28,4},{1,25},{... | collective-permute-start | bytes 172040 | tf_op jit(solution)/shard_map/ppermute | solution.py:17
  54.2 6.4 %collective-permute-start.16 = (bf16[16,1792]{1,0:T(8,128)(2,1)S(1)}, bf16[16,1792]{1,0:T(8,128)(2,1)S(1)}, u32[]{:S(2)}, u32[]{:S(2)}) collective-permute-start(bf16[16,1792]{1,0:T(8,128)(2,1)S(1)} %get-tuple-element.61), channel_id=1, source_target_pairs={{0,16},{4,20},{8,24},{12,28},{16,0},{20,4},{24,8},{28,12},{1,17},{... | collective-permute-start | bytes 172040 | tf_op jit(solution)/shard_map/ppermute | solution.py:17
  54.6 6.1 %collective-permute-start.17 = (bf16[16,1792]{1,0:T(8,128)(2,1)S(1)}, bf16[16,1792]{1,0:T(8,128)(2,1)S(1)}, u32[]{:S(2)}, u32[]{:S(2)}) collective-permute-start(bf16[16,1792]{1,0:T(8,128)(2,1)S(1)} %get-tuple-element.62), channel_id=1, source_target_pairs={{0,8},{4,12},{8,0},{12,4},{16,24},{20,28},{24,16},{28,20},{1,9},{5... | collective-permute-start | bytes 172040 | tf_op jit(solution)/shard_map/ppermute | solution.py:17
  60.7 3.9 %collective-permute-start.18 = (bf16[8,1792]{1,0:T(8,128)(2,1)S(1)}, bf16[8,1792]{1,0:T(8,128)(2,1)S(1)}, u32[]{:S(2)}, u32[]{:S(2)}) collective-permute-start(bf16[8,1792]{1,0:T(8,128)(2,1)S(1)} %get-tuple-element.64), channel_id=1, source_target_pairs={{0,4},{4,0},{8,12},{12,8},{16,20},{20,16},{24,28},{28,24},{1,5},{5... | collective-permute-start | bytes 86024 | tf_op jit(solution)/shard_map/ppermute | solution.py:17

commit v7 on v5

--- a/solution.py
+++ b/solution.py
@@ -77,7 +77,7 @@
 def query_body(qn_h, qr_h, wuk_h, keys_h, queries, turned, keys, qn, qr, wuk, nope_scr, rope_scr, sems):
     rows, heads, _ = qn.shape
     half = heads // 2
-    group = min(4, half)
+    group = min(8, half)
     steps = half // group
     first = (lax.axis_index("grp") & 1) * half
     copies = [

time: 65.7 us -> 65.7 us (level)
  no operation moved by 1% of the time
where the time goes in v7:
time: 65.7 us; the launch traced here: 65.6 us
  waiting for transfers between devices  24.7 us (38%)
  starting transfers between devices  22 us (33%)
  Pallas kernels  16.9 us (26%)
  local copies, waits for them, and re-layouts  1.6 us (2%)
    ppermute x19, waiting for transfers between devices, swap(): lax.ppermute(x, axis, [(a, a ^ bits) for a in range(lax.axis_size(axis))])  24.7 us
    ppermute x19, starting transfers between devices, swap(): lax.ppermute(x, axis, [(a, a ^ bits) for a in range(lax.axis_size(axis))])  22 us
    pallas_call x19, Pallas kernels, run(): pl.pallas_call(ordered, out_shape=[jax.ShapeDtypeStruct(s, d) for s, d in...  16.9 us
    unnamed x34, local copies, waits for them, and re-layouts  1.6 us
  transfers between devices with their start and end apart: 19, of which 13 were waited for; matrix products, arithmetic and copies ran while one was open for 0% of the time, Pallas kernels for 12%

profile of v7, /device:TPU:0, one launch (start us, length us, event | category | flops | bytes accessed | tf_op | source)
XLA Modules:
  0.0 65.6 jit_solution(6918132994679973382)
XLA Ops:
  0.0 0.5 collective-permute-start
  0.5 2.0 %queries.1 = (bf16[512,512]{1,0:T(8,128)(2,1)S(1)}, bf16[512,64]{1,0:T(8,128)(2,1)S(1)}, bf16[576,384]{1,0:T(8,128)(2,1)S(1)}) custom-call(bf16[64,16,128]{2,1,0:T(8,128)(2,1)} %refs_0_.1, bf16[64,16,64]{2,1,0:T(8,128)(2,1)} %refs_1_.7, bf16[16,128,512]{2,1,0:T(8,128)(2,1)} %refs_2_.6, bf16[576,384]{1,0:T(8,128)(2,1)} %bitcast.10), custom_call_target="tpu_custom_call" | custom-call | flops 2300000000 | bytes 1024 | tf_op jit(solution)/shard_map/queries/pallas_call | solution.py:42
  2.4 0.0 collective-permute-done.refs_3_
  2.4 0.0 slice-start.13
  2.5 0.0 copy-start
  2.5 0.0 copy-start.1
  2.5 0.0 slice-start.4
  2.5 0.0 slice-start.5
  2.5 0.0 slice-start.6
  2.5 3.2 %attend.1 = (f32[64,1152]{1,0:T(8,128)S(1)}, bf16[64,1152]{1,0:T(8,128)(2,1)S(1)}) custom-call(bf16[512,512]{1,0:T(8,128)(2,1)S(1)} %get-tuple-element.35.refs_0_, bf16[512,64]{1,0:T(8,128)(2,1)S(1)} %get-tuple-element.36.refs_1_, bf16[576,384]{1,0:T(8,128)(2,1)S(1)} %get-tuple-element.37.refs_2_, bf16[576,384]{1,0:T(8,128)(2,1)S(1)} %collective-permute-done.refs_3_, ...), custom_call_target="tpu_custom_call" | custom-call | flops 13799999488 | bytes 1024 | tf_op jit(solution)/shard_map/attend/pallas_call | solution.py:42
  5.7 0.0 copy-start.2
  5.7 2.5 %collective-permute-start.1 = (bf16[64,1152]{1,0:T(8,128)(2,1)S(1)}, bf16[64,1152]{1,0:T(8,128)(2,1)S(1)}, u32[]{:S(2)}, u32[]{:S(2)}) collective-permute-start(bf16[64,1152]{1,0:T(8,128)(2,1)S(1)} %get-tuple-element.39), channel_id=1, source_target_pairs={{0,2},{1,3},{2,0},{3,1},{4,6},{5,7},{6,4},{7,5},{8,10},{9,11},{10,... | collective-permute-start | bytes 442376 | tf_op jit(solution)/shard_map/ppermute | solution.py:17
  8.3 4.5 %collective-permute-done.1.refs_1_ = bf16[64,1152]{1,0:T(8,128)(2,1)S(1)} collective-permute-done((bf16[64,1152]{1,0:T(8,128)(2,1)S(1)}, bf16[64,1152]{1,0:T(8,128)(2,1)S(1)}, u32[]{:S(2)}, u32[]{:S(2)}) %collective-permute-start.1) | collective-permute-done | bytes 147488 | tf_op jit(solution)/shard_map/ppermute | solution.py:17
  12.8 0.3 merge.1.refs_0_
  13.1 0.0 slice-start.1
  13.1 0.0 slice-start.7
  13.1 0.1 collective-permute-start.2
  13.2 0.8 %project_mine.1.refs_0_ = f32[64,1792]{1,0:T(8,128)S(1)} custom-call(bf16[64,1024]{1,0:T(8,128)(2,1)S(1)} %merge.1.refs_0_, bf16[2048,1792]{1,0:T(8,128)(2,1)S(1)} %bitcast.8), custom_call_target="tpu_custom_call" | custom-call | flops 575000000 | bytes 1024 | tf_op jit(solution)/shard_map/project_mine/pallas_call | solution.py:42
  14.0 0.0 slice-start.2
  14.0 0.5 collective-permute-done.2.refs_1_
  14.5 0.8 %project.1 = (f32[16,1792]{1,0:T(8,128)S(1)}, bf16[16,1920]{1,0:T(8,128)(2,1)S(1)}, bf16[16,1920]{1,0:T(8,128)(2,1)S(1)}, bf16[16,1920]{1,0:T(8,128)(2,1)S(1)}, f32[8,128]{1,0:T(8,128)S(1)}) custom-call(f32[64,1792]{1,0:T(8,128)S(1)} %project_mine.1.refs_0_, bf16[64,1024]{1,0:T(8,128)(2,1)S(1)} %collective-permute-done.2.refs_1_, s32[8,8]{1,0:T(8,128)S(1)} %copy-done, ...), custom_call_target="tpu_custom_call" | custom-call | flops 1150000000 | bytes 1024 | tf_op jit(solution)/shard_map/project/pallas_call | solution.py:42
  15.3 3.9 %collective-permute-start.3 = (bf16[16,1920]{1,0:T(8,128)(2,1)S(1)}, bf16[16,1920]{1,0:T(8,128)(2,1)S(1)}, u32[]{:S(2)}, u32[]{:S(2)}) collective-permute-start(bf16[16,1920]{1,0:T(8,128)(2,1)S(1)} %get-tuple-element.42), channel_id=1, source_target_pairs={{0,24},{4,28},{8,16},{12,20},{16,8},{20,12},{24,0},{28,4},{1,25},{... | collective-permute-start | bytes 184328 | tf_op jit(solution)/shard_map/ppermute | solution.py:17
  19.3 0.0 collective-permute-start.4
  19.3 0.6 collective-permute-start.5
  19.9 1.8 %collective-permute-done.3.refs_3_ = bf16[16,1920]{1,0:T(8,128)(2,1)S(1)} collective-permute-done((bf16[16,1920]{1,0:T(8,128)(2,1)S(1)}, bf16[16,1920]{1,0:T(8,128)(2,1)S(1)}, u32[]{:S(2)}, u32[]{:S(2)}) %collective-permute-start.3) | collective-permute-done | bytes 61472 | tf_op jit(solution)/shard_map/ppermute | solution.py:17
  21.7 3.1 %collective-permute-done.4.refs_4_ = bf16[16,1920]{1,0:T(8,128)(2,1)S(1)} collective-permute-done((bf16[16,1920]{1,0:T(8,128)(2,1)S(1)}, bf16[16,1920]{1,0:T(8,128)(2,1)S(1)}, u32[]{:S(2)}, u32[]{:S(2)}) %collective-permute-start.4) | collective-permute-done | bytes 61472 | tf_op jit(solution)/shard_map/ppermute | solution.py:17
  24.8 0.0 collective-permute-done.5.refs_5_
  24.8 0.1 rest_sum.1
  24.9 1.6 %collective-permute-start.6 = (bf16[16,1920]{1,0:T(8,128)(2,1)S(1)}, bf16[16,1920]{1,0:T(8,128)(2,1)S(1)}, u32[]{:S(2)}, u32[]{:S(2)}) collective-permute-start(bf16[16,1920]{1,0:T(8,128)(2,1)S(1)} %get-tuple-element.46.refs_0_), channel_id=1, source_target_pairs={{0,4},{4,0},{8,12},{12,8},{16,20},{20,16},{24,28},{28,24},{1,5},{5... | collective-permute-start | bytes 184328 | tf_op jit(solution)/shard_map/ppermute | solution.py:17
  26.5 2.7 %collective-permute-done.6.refs_1_ = bf16[16,1920]{1,0:T(8,128)(2,1)S(1)} collective-permute-done((bf16[16,1920]{1,0:T(8,128)(2,1)S(1)}, bf16[16,1920]{1,0:T(8,128)(2,1)S(1)}, u32[]{:S(2)}, u32[]{:S(2)}) %collective-permute-start.6) | collective-permute-done | bytes 61472 | tf_op jit(solution)/shard_map/ppermute | solution.py:17
  29.2 2.5 %collective-permute-start.7 = (bf16[16,1792]{1,0:T(8,128)(2,1)S(1)}, bf16[16,1792]{1,0:T(8,128)(2,1)S(1)}, u32[]{:S(2)}, u32[]{:S(2)}) collective-permute-start(bf16[16,1792]{1,0:T(8,128)(2,1)S(1)} %get-tuple-element.48.refs_3_), channel_id=1, source_target_pairs={{0,24},{4,28},{8,16},{12,20},{16,8},{20,12},{24,0},{28,4},{1,25},{... | collective-permute-start | bytes 172040 | tf_op jit(solution)/shard_map/ppermute | solution.py:17
  31.7 0.1 collective-permute-start.9
  31.9 1.8 %collective-permute-start.8 = (bf16[16,1792]{1,0:T(8,128)(2,1)S(1)}, bf16[16,1792]{1,0:T(8,128)(2,1)S(1)}, u32[]{:S(2)}, u32[]{:S(2)}) collective-permute-start(bf16[16,1792]{1,0:T(8,128)(2,1)S(1)} %get-tuple-element.48.refs_3_), channel_id=1, source_target_pairs={{0,8},{4,12},{8,0},{12,4},{16,24},{20,28},{24,16},{28,20},{1,9},{5... | collective-permute-start | bytes 172040 | tf_op jit(solution)/shard_map/ppermute | solution.py:17
  33.7 1.9 %collective-permute-done.7.refs_2_.refs_6_ = bf16[16,1792]{1,0:T(8,128)(2,1)S(1)} collective-permute-done((bf16[16,1792]{1,0:T(8,128)(2,1)S(1)}, bf16[16,1792]{1,0:T(8,128)(2,1)S(1)}, u32[]{:S(2)}, u32[]{:S(2)}) %collective-permute-start.7) | collective-permute-done | bytes 57376 | tf_op jit(solution)/shard_map/ppermute | solution.py:17
  35.6 0.5 route.1
  36.1 0.7 %collective-permute-done.9.refs_5_ = bf16[16,1792]{1,0:T(8,128)(2,1)S(1)} collective-permute-done((bf16[16,1792]{1,0:T(8,128)(2,1)S(1)}, bf16[16,1792]{1,0:T(8,128)(2,1)S(1)}, u32[]{:S(2)}, u32[]{:S(2)}) %collective-permute-start.9) | collective-permute-done | bytes 57376 | tf_op jit(solution)/shard_map/ppermute | solution.py:17
  36.8 0.0 collective-permute-done.8.refs_4_
  36.9 2.8 %other_half.1 = (bf16[128,1792]{1,0:T(8,128)(2,1)S(1)}, bf16[4,32,1024]{2,1,0:T(8,128)(2,1)S(1)}) custom-call(bf16[128,64]{1,0:T(8,128)(2,1)S(1)} %get-tuple-element.49.refs_0_, bf16[4,1792,1024]{2,1,0:T(8,128)(2,1)S(1)} %bitcast.2, bf16[4,1792,1024]{2,1,0:T(8,128)(2,1)S(1)} %bitcast.4, bf16[16,1792]{1,0:T(8,128)(2,1)S(1)} %get-tuple-element.48.refs_3_, ...), custom_call_target="tpu_custom_call" | custom-call | flops 575000000 | bytes 1024 | tf_op jit(solution)/shard_map/other_half/pallas_call | solution.py:42
  39.7 0.0 collective-permute-start.10
  39.7 1.4 %own_half.1.refs_0_ = f32[2,32,1024]{2,1,0:T(8,128)S(1)} custom-call(bf16[128,1792]{1,0:T(8,128)(2,1)S(1)} %get-tuple-element.50.refs_0_, bf16[4,1792,1024]{2,1,0:T(8,128)(2,1)S(1)} %bitcast.2, bf16[4,1792,1024]{2,1,0:T(8,128)(2,1)S(1)} %bitcast.4, bf16[4,32,1024]{2,1,0:T(8,128)(2,1)S(1)} %get-tuple-element.51.refs_3_), custom_call_target="tpu_custom_call" | custom-call | flops 575000000 | bytes 1024 | tf_op jit(solution)/shard_map/own_half/pallas_call | solution.py:42
  41.1 0.2 collective-permute-done.10.refs_1_.refs_3_
  41.3 1.6 %collective-permute-start.11 = (bf16[2,32,1024]{2,1,0:T(8,128)(2,1)S(1)}, bf16[2,32,1024]{2,1,0:T(8,128)(2,1)S(1)}, u32[]{:S(2)}, u32[]{:S(2)}) collective-permute-start(bf16[2,32,1024]{2,1,0:T(8,128)(2,1)S(1)} %get-tuple-element.53), channel_id=1, source_target_pairs={{0,2},{1,3},{2,0},{3,1},{4,6},{5,7},{6,4},{7,5},{8,10},{9,11},{10,... | collective-permute-start | bytes 393224 | tf_op jit(solution)/shard_map/ppermute | solution.py:17
  42.9 1.3 %own_sum.1 = (f32[2,32,1024]{2,1,0:T(8,128)S(1)}, bf16[2,32,1024]{2,1,0:T(8,128)(2,1)S(1)}) custom-call(bf16[128,1792]{1,0:T(8,128)(2,1)S(1)} %get-tuple-element.50.refs_0_, bf16[4,1792,1024]{2,1,0:T(8,128)(2,1)S(1)} %bitcast.2, bf16[4,1792,1024]{2,1,0:T(8,128)(2,1)S(1)} %bitcast.4, bf16[4,32,1024]{2,1,0:T(8,128)(2,1)S(1)} %collective-permute-done.10.refs_1_.refs_3_, ...), custom_call_target="tpu_custom_call" | custom-call | flops 575000000 | bytes 1024 | tf_op jit(solution)/shard_map/own_sum/pallas_call | solution.py:42
  44.2 0.6 collective-permute-start.13
  44.8 2.4 %collective-permute-done.11.refs_1_ = bf16[2,32,1024]{2,1,0:T(8,128)(2,1)S(1)} collective-permute-done((bf16[2,32,1024]{2,1,0:T(8,128)(2,1)S(1)}, bf16[2,32,1024]{2,1,0:T(8,128)(2,1)S(1)}, u32[]{:S(2)}, u32[]{:S(2)}) %collective-permute-start.11) | collective-permute-done | bytes 131104 | tf_op jit(solution)/shard_map/ppermute | solution.py:17
  47.2 0.1 act.2.refs_0_
  47.2 0.1 collective-permute-start.12
  47.3 0.2 slice-done.10
  47.5 1.3 %slice-done.11 = s8[2097152]{0:T(1024)(128)(4,1)S(1)} async-done(((s8[14680064]{0:T(1024)(128)(4,1)}), s8[2097152]{0:T(1024)(128)(4,1)S(1)}, s32[]{:S(2)}) %slice-start.11) | async-done | bytes 2097176
  48.8 0.7 %down_mine.1.refs_2_.refs_0_ = f32[2,32,1792]{2,1,0:T(8,128)S(1)} custom-call(bf16[2,32,512]{2,1,0:T(8,128)(2,1)S(1)} %act.2.refs_0_, bf16[4,1024,1792]{2,1,0:T(8,128)(2,1)S(1)} %bitcast.6), custom_call_target="tpu_custom_call" | custom-call | flops 575000000 | bytes 1024 | tf_op jit(solution)/shard_map/down_mine/pallas_call | solution.py:42
  49.6 0.3 collective-permute-done.13.refs_1_
  49.9 0.1 act.3.refs_2_
  50.0 0.1 collective-permute-start.14
  50.1 1.4 %down_next.1 = (bf16[2,32,1792]{2,1,0:T(8,128)(2,1)S(1)}, f32[2,32,1792]{2,1,0:T(8,128)S(1)}) custom-call(f32[2,32,1792]{2,1,0:T(8,128)S(1)} %down_mine.1.refs_2_.refs_0_, bf16[2,32,512]{2,1,0:T(8,128)(2,1)S(1)} %collective-permute-done.12.refs_1_, bf16[2,32,512]{2,1,0:T(8,128)(2,1)S(1)} %act.3.refs_2_, bf16[4,1024,1792]{2,1,0:T(8,128)(2,1)S(1)} %bitcast.6), custom_call_target="tpu_custom_call" | custom-call | flops 1150000000 | bytes 1024 | tf_op jit(solution)/shard_map/down_next/pallas_call | solution.py:42
  51.4 0.0 collective-permute-done.14.refs_1_
  51.4 0.9 %down_last.1 = (f32[16,1792]{1,0:T(8,128)S(1)}, bf16[16,1792]{1,0:T(8,128)(2,1)S(1)}, bf16[16,1792]{1,0:T(8,128)(2,1)S(1)}, bf16[16,1792]{1,0:T(8,128)(2,1)S(1)}) custom-call(f32[2,32,1792]{2,1,0:T(8,128)S(1)} %get-tuple-element.56.refs_0_, bf16[2,32,512]{2,1,0:T(8,128)(2,1)S(1)} %collective-permute-done.14.refs_1_, bf16[4,1024,1792]{2,1,0:T(8,128)(2,1)S(1)} %bitcast.6, ...), custom_call_target="tpu_custom_call" | custom-call | flops 1150000000 | bytes 1024 | tf_op jit(solution)/shard_map/down_last/pallas_call | solution.py:42
  52.4 2.2 %collective-permute-start.15 = (bf16[16,1792]{1,0:T(8,128)(2,1)S(1)}, bf16[16,1792]{1,0:T(8,128)(2,1)S(1)}, u32[]{:S(2)}, u32[]{:S(2)}) collective-permute-start(bf16[16,1792]{1,0:T(8,128)(2,1)S(1)} %get-tuple-element.60), channel_id=1, source_target_pairs={{0,24},{4,28},{8,16},{12,20},{16,8},{20,12},{24,0},{28,4},{1,25},{... | collective-permute-start | bytes 172040 | tf_op jit(solution)/shard_map/ppermute | solution.py:17
  54.5 0.3 collective-permute-start.16
  54.9 1.9 %collective-permute-start.17 = (bf16[16,1792]{1,0:T(8,128)(2,1)S(1)}, bf16[16,1792]{1,0:T(8,128)(2,1)S(1)}, u32[]{:S(2)}, u32[]{:S(2)}) collective-permute-start(bf16[16,1792]{1,0:T(8,128)(2,1)S(1)} %get-tuple-element.62), channel_id=1, source_target_pairs={{0,8},{4,12},{8,0},{12,4},{16,24},{20,28},{24,16},{28,20},{1,9},{5... | collective-permute-start | bytes 172040 | tf_op jit(solution)/shard_map/ppermute | solution.py:17
  56.8 2.2 %collective-permute-done.15.refs_1_ = bf16[16,1792]{1,0:T(8,128)(2,1)S(1)} collective-permute-done((bf16[16,1792]{1,0:T(8,128)(2,1)S(1)}, bf16[16,1792]{1,0:T(8,128)(2,1)S(1)}, u32[]{:S(2)}, u32[]{:S(2)}) %collective-permute-start.15) | collective-permute-done | bytes 57376 | tf_op jit(solution)/shard_map/ppermute | solution.py:17
  59.0 2.0 %collective-permute-done.16.refs_2_ = bf16[16,1792]{1,0:T(8,128)(2,1)S(1)} collective-permute-done((bf16[16,1792]{1,0:T(8,128)(2,1)S(1)}, bf16[16,1792]{1,0:T(8,128)(2,1)S(1)}, u32[]{:S(2)}, u32[]{:S(2)}) %collective-permute-start.16) | collective-permute-done | bytes 57376 | tf_op jit(solution)/shard_map/ppermute | solution.py:17
  61.0 1.6 %collective-permute-start.18 = (bf16[8,1792]{1,0:T(8,128)(2,1)S(1)}, bf16[8,1792]{1,0:T(8,128)(2,1)S(1)}, u32[]{:S(2)}, u32[]{:S(2)}) collective-permute-start(bf16[8,1792]{1,0:T(8,128)(2,1)S(1)} %get-tuple-element.64), channel_id=1, source_target_pairs={{0,4},{4,0},{8,12},{12,8},{16,20},{20,16},{24,28},{28,24},{1,5},{5... | collective-permute-start | bytes 86024 | tf_op jit(solution)/shard_map/ppermute | solution.py:17
  62.6 2.4 %collective-permute-done.18.refs_2_ = bf16[8,1792]{1,0:T(8,128)(2,1)S(1)} collective-permute-done((bf16[8,1792]{1,0:T(8,128)(2,1)S(1)}, bf16[8,1792]{1,0:T(8,128)(2,1)S(1)}, u32[]{:S(2)}, u32[]{:S(2)}) %collective-permute-start.18) | collective-permute-done | bytes 28704 | tf_op jit(solution)/shard_map/ppermute | solution.py:17
  65.0 0.6 out.1
  (31 shorter events, 0.1 us)
Async XLA Ops:
  0.0 2.4 %collective-permute-start = (bf16[576,384]{1,0:T(8,128)(2,1)}, bf16[576,384]{1,0:T(8,128)(2,1)S(1)}, u32[]{:S(2)}, u32[]{:S(2)}) collective-permute-start(bf16[576,384]{1,0:T(8,128)(2,1)} %bitcast.9), channel_id=1, source_target_pairs={{0,1},{1,0},{2,3},{3,2},{4,5},{5,4},{6,7},{7,6},{8,9},{9,8},{10,11... | collective-permute-start | bytes 1327112 | tf_op jit(solution)/shard_map/ppermute | solution.py:17
  0.5 12.8 %slice-start.12 = ((s8[7340032]{0:T(1024)(128)(4,1)}), s8[4194304]{0:T(1024)(128)(4,1)S(1)}, s32[]{:S(2)}) async-start(s8[7340032]{0:T(1024)(128)(4,1)} %bitcast.7), calls=%async_computation.12 | async-start | bytes 8388608
  2.4 10.8 %slice-start.13 = ((s8[7340032]{0:T(1024)(128)(4,1)}), s8[3145728]{0:T(1024)(128)(4,1)S(1)}, s32[]{:S(2)}) async-start(s8[7340032]{0:T(1024)(128)(4,1)} %bitcast.7), calls=%async_computation.13 | async-start | bytes 6291456
  2.5 12.1 %copy-start = (s32[8,8]{1,0:T(8,128)S(1)}, s32[8,8]{1,0:T(8,128)}, u32[]{:S(2)}) copy-start(s32[8,8]{1,0:T(8,128)} %refs_2_.7) | copy-start | bytes 772
  2.5 12.1 %copy-start.1 = (f32[8,8]{1,0:T(8,128)S(1)}, f32[8,8]{1,0:T(8,128)}, u32[]{:S(2)}) copy-start(f32[8,8]{1,0:T(8,128)} %refs_3_.2) | copy-start | bytes 772
  2.5 34.4 %slice-start.4 = ((s8[14680064]{0:T(1024)(128)(4,1)}), s8[4194304]{0:T(1024)(128)(4,1)S(1)}, s32[]{:S(2)}) async-start(s8[14680064]{0:T(1024)(128)(4,1)} %bitcast.3), calls=%async_computation.4 | async-start | bytes 8388608
  2.5 34.3 %slice-start.5 = ((s8[14680064]{0:T(1024)(128)(4,1)}), s8[4194304]{0:T(1024)(128)(4,1)S(1)}, s32[]{:S(2)}) async-start(s8[14680064]{0:T(1024)(128)(4,1)} %bitcast.3), calls=%async_computation.5 | async-start | bytes 8388608
  2.5 34.3 %slice-start.6 = ((s8[14680064]{0:T(1024)(128)(4,1)}), s8[4194304]{0:T(1024)(128)(4,1)S(1)}, s32[]{:S(2)}) async-start(s8[14680064]{0:T(1024)(128)(4,1)} %bitcast.3), calls=%async_computation.6 | async-start | bytes 8388608
  5.7 19.1 %copy-start.2 = (bf16[8,1792]{1,0:T(8,128)(2,1)S(1)}, bf16[8,1792]{1,0:T(8,128)(2,1)}, u32[]{:S(2)}) copy-start(bf16[8,1792]{1,0:T(8,128)(2,1)} %refs_1_.9) | copy-start | bytes 86020
  5.7 7.1 %collective-permute-start.1 = (bf16[64,1152]{1,0:T(8,128)(2,1)S(1)}, bf16[64,1152]{1,0:T(8,128)(2,1)S(1)}, u32[]{:S(2)}, u32[]{:S(2)}) collective-permute-start(bf16[64,1152]{1,0:T(8,128)(2,1)S(1)} %get-tuple-element.39), channel_id=1, source_target_pairs={{0,2},{1,3},{2,0},{3,1},{4,6},{5,7},{6,4},{7,5},{8,10},{9,11},{10,... | collective-permute-start | bytes 442376 | tf_op jit(solution)/shard_map/ppermute | solution.py:17
  12.8 24.1 %slice-start = ((s8[14680064]{0:T(1024)(128)(4,1)}), s8[4194304]{0:T(1024)(128)(4,1)S(1)}, s32[]{:S(2)}) async-start(s8[14680064]{0:T(1024)(128)(4,1)} %bitcast.1), calls=%async_computation | async-start | bytes 8388608
  13.1 23.8 %slice-start.1 = ((s8[14680064]{0:T(1024)(128)(4,1)}), s8[4194304]{0:T(1024)(128)(4,1)S(1)}, s32[]{:S(2)}) async-start(s8[14680064]{0:T(1024)(128)(4,1)} %bitcast.1), calls=%async_computation.1 | async-start | bytes 8388608
  13.1 23.8 %slice-start.7 = ((s8[14680064]{0:T(1024)(128)(4,1)}), s8[2097152]{0:T(1024)(128)(4,1)S(1)}, s32[]{:S(2)}) async-start(s8[14680064]{0:T(1024)(128)(4,1)} %bitcast.3), calls=%async_computation.7 | async-start | bytes 4194304
  13.1 1.4 %collective-permute-start.2 = (bf16[64,1024]{1,0:T(8,128)(2,1)S(1)}, bf16[64,1024]{1,0:T(8,128)(2,1)S(1)}, u32[]{:S(2)}, u32[]{:S(2)}) collective-permute-start(bf16[64,1024]{1,0:T(8,128)(2,1)S(1)} %merge.1.refs_0_), channel_id=1, source_target_pairs={{0,1},{1,0},{2,3},{3,2},{4,5},{5,4},{6,7},{7,6},{8,9},{9,8},{10,11... | collective-permute-start | bytes 393224 | tf_op jit(solution)/shard_map/ppermute | solution.py:17
  14.0 22.9 %slice-start.2 = ((s8[14680064]{0:T(1024)(128)(4,1)}), s8[4194304]{0:T(1024)(128)(4,1)S(1)}, s32[]{:S(2)}) async-start(s8[14680064]{0:T(1024)(128)(4,1)} %bitcast.1), calls=%async_computation.2 | async-start | bytes 8388608
  15.3 6.4 %collective-permute-start.3 = (bf16[16,1920]{1,0:T(8,128)(2,1)S(1)}, bf16[16,1920]{1,0:T(8,128)(2,1)S(1)}, u32[]{:S(2)}, u32[]{:S(2)}) collective-permute-start(bf16[16,1920]{1,0:T(8,128)(2,1)S(1)} %get-tuple-element.42), channel_id=1, source_target_pairs={{0,24},{4,28},{8,16},{12,20},{16,8},{20,12},{24,0},{28,4},{1,25},{... | collective-permute-start | bytes 184328 | tf_op jit(solution)/shard_map/ppermute | solution.py:17
  19.3 5.6 %collective-permute-start.4 = (bf16[16,1920]{1,0:T(8,128)(2,1)S(1)}, bf16[16,1920]{1,0:T(8,128)(2,1)S(1)}, u32[]{:S(2)}, u32[]{:S(2)}) collective-permute-start(bf16[16,1920]{1,0:T(8,128)(2,1)S(1)} %get-tuple-element.43), channel_id=1, source_target_pairs={{0,16},{4,20},{8,24},{12,28},{16,0},{20,4},{24,8},{28,12},{1,17},{... | collective-permute-start | bytes 184328 | tf_op jit(solution)/shard_map/ppermute | solution.py:17
  19.3 5.6 %collective-permute-start.5 = (bf16[16,1920]{1,0:T(8,128)(2,1)S(1)}, bf16[16,1920]{1,0:T(8,128)(2,1)S(1)}, u32[]{:S(2)}, u32[]{:S(2)}) collective-permute-start(bf16[16,1920]{1,0:T(8,128)(2,1)S(1)} %get-tuple-element.44), channel_id=1, source_target_pairs={{0,8},{4,12},{8,0},{12,4},{16,24},{20,28},{24,16},{28,20},{1,9},{5... | collective-permute-start | bytes 184328 | tf_op jit(solution)/shard_map/ppermute | solution.py:17
  24.8 12.0 %slice-start.3 = ((s8[14680064]{0:T(1024)(128)(4,1)}), s8[2097152]{0:T(1024)(128)(4,1)S(1)}, s32[]{:S(2)}) async-start(s8[14680064]{0:T(1024)(128)(4,1)} %bitcast.1), calls=%async_computation.3 | async-start | bytes 4194304
  24.9 4.3 %collective-permute-start.6 = (bf16[16,1920]{1,0:T(8,128)(2,1)S(1)}, bf16[16,1920]{1,0:T(8,128)(2,1)S(1)}, u32[]{:S(2)}, u32[]{:S(2)}) collective-permute-start(bf16[16,1920]{1,0:T(8,128)(2,1)S(1)} %get-tuple-element.46.refs_0_), channel_id=1, source_target_pairs={{0,4},{4,0},{8,12},{12,8},{16,20},{20,16},{24,28},{28,24},{1,5},{5... | collective-permute-start | bytes 184328 | tf_op jit(solution)/shard_map/ppermute | solution.py:17
  29.2 6.4 %collective-permute-start.7 = (bf16[16,1792]{1,0:T(8,128)(2,1)S(1)}, bf16[16,1792]{1,0:T(8,128)(2,1)S(1)}, u32[]{:S(2)}, u32[]{:S(2)}) collective-permute-start(bf16[16,1792]{1,0:T(8,128)(2,1)S(1)} %get-tuple-element.48.refs_3_), channel_id=1, source_target_pairs={{0,24},{4,28},{8,16},{12,20},{16,8},{20,12},{24,0},{28,4},{1,25},{... | collective-permute-start | bytes 172040 | tf_op jit(solution)/shard_map/ppermute | solution.py:17
  31.7 5.1 %collective-permute-start.9 = (bf16[16,1792]{1,0:T(8,128)(2,1)S(1)}, bf16[16,1792]{1,0:T(8,128)(2,1)S(1)}, u32[]{:S(2)}, u32[]{:S(2)}) collective-permute-start(bf16[16,1792]{1,0:T(8,128)(2,1)S(1)} %get-tuple-element.48.refs_3_), channel_id=1, source_target_pairs={{0,16},{4,20},{8,24},{12,28},{16,0},{20,4},{24,8},{28,12},{1,17},{... | collective-permute-start | bytes 172040 | tf_op jit(solution)/shard_map/ppermute | solution.py:17
  31.9 4.9 %collective-permute-start.8 = (bf16[16,1792]{1,0:T(8,128)(2,1)S(1)}, bf16[16,1792]{1,0:T(8,128)(2,1)S(1)}, u32[]{:S(2)}, u32[]{:S(2)}) collective-permute-start(bf16[16,1792]{1,0:T(8,128)(2,1)S(1)} %get-tuple-element.48.refs_3_), channel_id=1, source_target_pairs={{0,8},{4,12},{8,0},{12,4},{16,24},{20,28},{24,16},{28,20},{1,9},{5... | collective-permute-start | bytes 172040 | tf_op jit(solution)/shard_map/ppermute | solution.py:17
  39.7 1.6 %collective-permute-start.10 = (bf16[4,32,1024]{2,1,0:T(8,128)(2,1)S(1)}, bf16[4,32,1024]{2,1,0:T(8,128)(2,1)S(1)}, u32[]{:S(2)}, u32[]{:S(2)}) collective-permute-start(bf16[4,32,1024]{2,1,0:T(8,128)(2,1)S(1)} %get-tuple-element.51.refs_3_), channel_id=1, source_target_pairs={{0,1},{1,0},{2,3},{3,2},{4,5},{5,4},{6,7},{7,6},{8,9},{9,8},{10,11... | collective-permute-start | bytes 786440 | tf_op jit(solution)/shard_map/ppermute | solution.py:17
  41.3 5.9 %collective-permute-start.11 = (bf16[2,32,1024]{2,1,0:T(8,128)(2,1)S(1)}, bf16[2,32,1024]{2,1,0:T(8,128)(2,1)S(1)}, u32[]{:S(2)}, u32[]{:S(2)}) collective-permute-start(bf16[2,32,1024]{2,1,0:T(8,128)(2,1)S(1)} %get-tuple-element.53), channel_id=1, source_target_pairs={{0,2},{1,3},{2,0},{3,1},{4,6},{5,7},{6,4},{7,5},{8,10},{9,11},{10,... | collective-permute-start | bytes 393224 | tf_op jit(solution)/shard_map/ppermute | solution.py:17
  42.8 4.5 %slice-start.8 = ((s8[14680064]{0:T(1024)(128)(4,1)}), s8[4194304]{0:T(1024)(128)(4,1)S(1)}, s32[]{:S(2)}) async-start(s8[14680064]{0:T(1024)(128)(4,1)} %bitcast.5), calls=%async_computation.8 | async-start | bytes 8388608
  42.8 4.5 %slice-start.9 = ((s8[14680064]{0:T(1024)(128)(4,1)}), s8[4194304]{0:T(1024)(128)(4,1)S(1)}, s32[]{:S(2)}) async-start(s8[14680064]{0:T(1024)(128)(4,1)} %bitcast.5), calls=%async_computation.9 | async-start | bytes 8388608
  42.9 4.7 %slice-start.10 = ((s8[14680064]{0:T(1024)(128)(4,1)}), s8[4194304]{0:T(1024)(128)(4,1)S(1)}, s32[]{:S(2)}) async-start(s8[14680064]{0:T(1024)(128)(4,1)} %bitcast.5), calls=%async_computation.10 | async-start | bytes 8388608
  44.2 5.7 %collective-permute-start.13 = (bf16[2,32,1024]{2,1,0:T(8,128)(2,1)S(1)}, bf16[2,32,1024]{2,1,0:T(8,128)(2,1)S(1)}, u32[]{:S(2)}, u32[]{:S(2)}) collective-permute-start(bf16[2,32,1024]{2,1,0:T(8,128)(2,1)S(1)} %get-tuple-element.55), channel_id=1, source_target_pairs={{0,2},{1,3},{2,0},{3,1},{4,6},{5,7},{6,4},{7,5},{8,10},{9,11},{10,... | collective-permute-start | bytes 393224 | tf_op jit(solution)/shard_map/ppermute | solution.py:17
  47.2 1.7 %slice-start.11 = ((s8[14680064]{0:T(1024)(128)(4,1)}), s8[2097152]{0:T(1024)(128)(4,1)S(1)}, s32[]{:S(2)}) async-start(s8[14680064]{0:T(1024)(128)(4,1)} %bitcast.5), calls=%async_computation.11 | async-start | bytes 4194304
  47.2 2.8 %collective-permute-start.12 = (bf16[2,32,512]{2,1,0:T(8,128)(2,1)S(1)}, bf16[2,32,512]{2,1,0:T(8,128)(2,1)S(1)}, u32[]{:S(2)}, u32[]{:S(2)}) collective-permute-start(bf16[2,32,512]{2,1,0:T(8,128)(2,1)S(1)} %act.2.refs_0_), channel_id=1, source_target_pairs={{0,1},{1,0},{2,3},{3,2},{4,5},{5,4},{6,7},{7,6},{8,9},{9,8},{10,11... | collective-permute-start | bytes 196616 | tf_op jit(solution)/shard_map/ppermute | solution.py:17
  50.0 1.5 %collective-permute-start.14 = (bf16[2,32,512]{2,1,0:T(8,128)(2,1)S(1)}, bf16[2,32,512]{2,1,0:T(8,128)(2,1)S(1)}, u32[]{:S(2)}, u32[]{:S(2)}) collective-permute-start(bf16[2,32,512]{2,1,0:T(8,128)(2,1)S(1)} %act.3.refs_2_), channel_id=1, source_target_pairs={{0,1},{1,0},{2,3},{3,2},{4,5},{5,4},{6,7},{7,6},{8,9},{9,8},{10,11... | collective-permute-start | bytes 196616 | tf_op jit(solution)/shard_map/ppermute | solution.py:17
  52.4 6.6 %collective-permute-start.15 = (bf16[16,1792]{1,0:T(8,128)(2,1)S(1)}, bf16[16,1792]{1,0:T(8,128)(2,1)S(1)}, u32[]{:S(2)}, u32[]{:S(2)}) collective-permute-start(bf16[16,1792]{1,0:T(8,128)(2,1)S(1)} %get-tuple-element.60), channel_id=1, source_target_pairs={{0,24},{4,28},{8,16},{12,20},{16,8},{20,12},{24,0},{28,4},{1,25},{... | collective-permute-start | bytes 172040 | tf_op jit(solution)/shard_map/ppermute | solution.py:17
  54.5 6.4 %collective-permute-start.16 = (bf16[16,1792]{1,0:T(8,128)(2,1)S(1)}, bf16[16,1792]{1,0:T(8,128)(2,1)S(1)}, u32[]{:S(2)}, u32[]{:S(2)}) collective-permute-start(bf16[16,1792]{1,0:T(8,128)(2,1)S(1)} %get-tuple-element.61), channel_id=1, source_target_pairs={{0,16},{4,20},{8,24},{12,28},{16,0},{20,4},{24,8},{28,12},{1,17},{... | collective-permute-start | bytes 172040 | tf_op jit(solution)/shard_map/ppermute | solution.py:17
  54.9 6.1 %collective-permute-start.17 = (bf16[16,1792]{1,0:T(8,128)(2,1)S(1)}, bf16[16,1792]{1,0:T(8,128)(2,1)S(1)}, u32[]{:S(2)}, u32[]{:S(2)}) collective-permute-start(bf16[16,1792]{1,0:T(8,128)(2,1)S(1)} %get-tuple-element.62), channel_id=1, source_target_pairs={{0,8},{4,12},{8,0},{12,4},{16,24},{20,28},{24,16},{28,20},{1,9},{5... | collective-permute-start | bytes 172040 | tf_op jit(solution)/shard_map/ppermute | solution.py:17
  61.0 3.9 %collective-permute-start.18 = (bf16[8,1792]{1,0:T(8,128)(2,1)S(1)}, bf16[8,1792]{1,0:T(8,128)(2,1)S(1)}, u32[]{:S(2)}, u32[]{:S(2)}) collective-permute-start(bf16[8,1792]{1,0:T(8,128)(2,1)S(1)} %get-tuple-element.64), channel_id=1, source_target_pairs={{0,4},{4,0},{8,12},{12,8},{16,20},{20,16},{24,28},{28,24},{1,5},{5... | collective-permute-start | bytes 86024 | tf_op jit(solution)/shard_map/ppermute | solution.py:17
